TPU v7x, 128 devices: a whole 4x4x4 slice. The times are simulated.
128 devices in a mesh: dp: 8 (over x_lo, z), sky: 16 (over x_hi, y, core).
Axes of the slice: x: 4 (x_hi: 2, x_lo: 2; x = x_hi * 2 + x_lo), y: 4, z: 4, core: 2. Of those that a mesh axis runs over, the one named last changes fastest.
Arguments:
- queries: bfloat16 [8, 4096, 3072], P('dp', 'sky'), may hold values from -5 to 5
- key_states: bfloat16 [8, 4096, 3072], P('dp', 'sky'), may hold values from -5 to 5
- value_states: bfloat16 [8, 4096, 3072], P('dp', 'sky'), may hold values from -6 to 6
- key_blocks: int32 [16, 2], replicated, may hold values from -1 to 15, as said below
- global_block: int32 [1], replicated, may hold values from 0 to 15
- w_out: bfloat16 [3072, 3072], P('dp'), may hold values from -0.109375 to 0.109375
- grad_out: bfloat16 [8, 4096, 3072], P('dp', 'sky'), may hold values from -6 to 6
Outputs:
- attended: bfloat16 [8, 4096, 3072], P('dp', 'sky')
- grad_queries: bfloat16 [8, 4096, 3072], P('dp', 'sky')
- grad_keys: bfloat16 [8, 4096, 3072], P('dp', 'sky')
- grad_values: bfloat16 [8, 4096, 3072], P('dp', 'sky')
Inputs may be any that keep to these rules, and one draw needn't show every extreme that they name: key_blocks[b, 0] is b - 1 or -1 and key_blocks[b, 1] is b + 1 or -1; -1 marks a missing neighbour. key_blocks[0, 0] and key_blocks[15, 1] are -1, key_blocks[14, 1] is 15.
All inputs are finite; a program needn't handle non-finite values.
Results may differ from a plain program's by a relative error of at most 0.03.
Values may be sent and summed in bfloat16 or wider, within the bound.
No kernel may reach another device: no remote copies, remote signals or barrier semaphores. Data moves between devices by JAX's collectives and lax.ppermute only.
A program may use at most 256 MiB of HBM per device.

v0:
```python
import math

import jax
import jax.numpy as jnp
from jax import lax
from jax.sharding import PartitionSpec as P

HEADS = 24
HD = 128
BLK = 256


def shifted(block, axis, distance):
    devices = range(lax.axis_size(axis))
    route = [(i - distance, i) for i in devices if i - distance in devices]
    return lax.ppermute(block, axis, route)


def from_root(value, axis, source):
    kept = jnp.where(lax.axis_index(axis) == source, value, 0).astype(value.dtype)
    return lax.psum(kept, axis)


def project_back(grad_out, w_out):
    combined = jnp.einsum(
        "td,hd->th",
        grad_out[0],
        lax.all_gather(w_out, "dp", axis=0, tiled=True),
        preferred_element_type=jnp.float32,
    )
    return combined.astype(jnp.bfloat16)


def local(queries, key_states, value_states, key_blocks, global_block, w_out, grad_out):
    row_count = queries.shape[1]
    feature_width = queries.shape[2]
    blocks = row_count // BLK
    score_scale = 1.0 / math.sqrt(HD)
    position = lax.axis_index("sky")
    first_block = position * blocks
    local_ids = first_block + jnp.arange(blocks, dtype=jnp.int32)
    global_id = global_block[0]
    owner_rank = global_id // blocks
    kv_stack = jnp.stack([key_states[0], value_states[0]])
    above_rows = shifted(kv_stack, "sky", 1)
    below_rows = shifted(kv_stack, "sky", -1)
    extended = jnp.concatenate([above_rows, kv_stack, below_rows], axis=1)
    global_rows = from_root(kv_stack, "sky", owner_rank)
    extended = extended.reshape(2, blocks + 2, BLK, feature_width)
    spread = global_rows[:, None]
    slots = jnp.stack(
        [extended[:, 1 : blocks + 1], extended[:, :blocks], extended[:, 2:], spread], axis=2
    )
    slots = slots.reshape(2, blocks, 4 * BLK, HEADS, HD)
    key_slots = slots[0]
    value_slots = slots[1]
    neighbours = lax.dynamic_slice_in_dim(key_blocks, first_block, blocks, 0)
    above_id = neighbours[:, 0]
    below_id = neighbours[:, 1]
    valid = jnp.stack(
        [
            local_ids >= 0,
            above_id >= 0,
            below_id >= 0,
            (global_id != local_ids) & (global_id != above_id) & (global_id != below_id),
        ],
        axis=1,
    )
    keep = jnp.repeat(valid, BLK, axis=1)[:, None, None, :]
    query_rows = queries[0].reshape(blocks, BLK, HEADS, HD)
    scores = (
        jnp.einsum("jqhd,jkhd->jhqk", query_rows, key_slots, preferred_element_type=jnp.float32)
        * score_scale
    )
    scores = jnp.where(keep, scores, -jnp.inf)
    row_max = jnp.max(scores, axis=-1, keepdims=True)
    exponent = jnp.exp(scores - row_max)
    attention = exponent / jnp.sum(exponent, axis=-1, keepdims=True)
    attention_b = attention.astype(jnp.bfloat16)
    attended = jnp.einsum(
        "jhqk,jkhd->jqhd", attention_b, value_slots, preferred_element_type=jnp.float32
    ).astype(jnp.bfloat16)
    grad_rows = project_back(grad_out, w_out).reshape(blocks, BLK, HEADS, HD)
    delta = jnp.einsum("jqhd,jqhd->jhq", grad_rows, attended, preferred_element_type=jnp.float32)
    grad_weights = jnp.einsum(
        "jqhd,jkhd->jhqk", grad_rows, value_slots, preferred_element_type=jnp.float32
    )
    grad_scores = (attention * (grad_weights - delta[..., None])).astype(jnp.bfloat16)
    grad_query = (
        jnp.einsum("jhqk,jkhd->jqhd", grad_scores, key_slots, preferred_element_type=jnp.float32)
        * score_scale
    ).astype(jnp.bfloat16)
    key_terms = (
        jnp.einsum("jhqk,jqhd->jkhd", grad_scores, query_rows, preferred_element_type=jnp.float32)
        * score_scale
    )
    value_terms = jnp.einsum(
        "jhqk,jqhd->jkhd", attention_b, grad_rows, preferred_element_type=jnp.float32
    )
    terms = jnp.stack([key_terms, value_terms]).reshape(2, blocks, 4, BLK, feature_width)
    own_terms = terms[:, :, 0]
    up_terms = lax.optimization_barrier(terms[:, :, 1].astype(jnp.bfloat16))
    down_terms = lax.optimization_barrier(terms[:, :, 2].astype(jnp.bfloat16))
    global_part = jnp.sum(terms[:, :, 3], axis=1)
    from_upper = shifted(up_terms[:, 0], "sky", -1)
    from_lower = shifted(down_terms[:, blocks - 1], "sky", 1)
    global_total = lax.psum(global_part.astype(jnp.bfloat16), "sky").astype(jnp.float32)
    from_above = jnp.concatenate([up_terms[:, 1:], from_upper[:, None]], axis=1)
    from_below = jnp.concatenate([from_lower[:, None], down_terms[:, : blocks - 1]], axis=1)
    hit = (local_ids == global_id)[None, :, None, None]
    total = (
        own_terms
        + from_above.astype(jnp.float32)
        + from_below.astype(jnp.float32)
        + jnp.where(hit, global_total[:, None], jnp.float32(0.0))
    )
    total = total.astype(jnp.bfloat16)
    return (
        attended.reshape(1, row_count, feature_width),
        grad_query.reshape(1, row_count, feature_width),
        total[0],
        total[1],
    )


def solution(mesh):
    in_specs = (
        P("dp", "sky", None),
        P("dp", "sky", None),
        P("dp", "sky", None),
        P(),
        P(),
        P("dp", None),
        P("dp", "sky", None),
    )
    out_specs = (
        P("dp", "sky", None),
        P("dp", "sky", None),
        P("dp", "sky", None),
        P("dp", "sky", None),
    )
    return jax.shard_map(local, mesh=mesh, in_specs=in_specs, out_specs=out_specs, check_vma=False)
```

profile of v0, /device:TPU:1, one launch (start us, length us, event | category | flops | bytes accessed | tf_op | source)
XLA Modules:
  0.0 735.2 jit_solution(4961470145596186313)
XLA Ops:
  28.1 33.0 %collective-permute-done.1 = bf16[2,256,3072]{2,1,0:T(8,128)(2,1)} collective-permute-done((bf16[2,256,3072]{2,1,0:T(8,128)(2,1)}, bf16[2,256,3072]{2,1,0:T(8,128)(2,1)}, u32[]{:S(2)}, u32[]{:S(2)}) %collective-permute-start.1) | collective-permute-done | bytes 3145760 | tf_op jit(solution)/shard_map/ppermute | solution.py:16
  61.1 5.7 pad_maximum_fusion.2
  66.9 3.8 slice_bitcast_fusion.5
  70.6 286.5 %all-reduce.3.cloned.1.call-done = bf16[2,1,1,256,3072]{4,3,0,2,1:T(8,128)(2,1)} async-done(((bf16[2,1,1,256,3072]{4,3,0,2,1:T(8,128)(2,1)}), bf16[2,1,1,256,3072]{4,3,0,2,1:T(8,128)(2,1)}) %all-reduce.3.cloned.1.call-update) | async-done | bytes 3145744 | tf_op jit(solution)/shard_map/psum | solution.py:21
  357.1 6.3 pad_maximum_fusion.1
  367.1 4.6 copy.63
  371.7 9.0 %copy.34 = bf16[1024,24,128]{0,2,1:T(8,128)(2,1)} copy(bf16[1024,24,128]{2,1,0:T(8,128)(2,1)} %bitcast.120) | data formatting | bytes 12582912 | tf_op jit(solution)/shard_map/reshape.13
  380.7 7.4 %copy.62 = bf16[128,8,24,128]{3,2,1,0:T(8,128)(2,1)} copy(bf16[128,8,24,128]{3,1,2,0:T(8,128)(2,1)} %bitcast.122) | data formatting | bytes 12582912
  388.1 9.1 %copy.56 = bf16[1024,24,128]{0,2,1:T(8,128)(2,1)} copy(bf16[1024,24,128]{2,1,0:T(8,128)(2,1)} %bitcast.121) | data formatting | bytes 12582912 | tf_op jit(solution)/shard_map/reshape.21
  397.2 15.3 %fusion.33 = (f32[24,256]{1,0:T(8,128)S(1)}, f32[24,256,1024]{1,2,0:T(8,128)}) fusion(pred[1024]{0:T(1024)(128)(4,1)S(1)} %broadcast_in_dim.44, bf16[1024,24,128]{0,2,1:T(8,128)(2,1)} %copy.34, bf16[256,24,128]{2,1,0:T(8,128)(2,1)S(1)} %bitcast.130), kind=kOutput, calls=%fused_computation.53 | convolution fusion | flops 1635779584 | bytes 33055744 | tf_op jit(solution)/shard_map/sub | solution.py:77
  412.5 13.5 %fusion.9 = bf16[24,256,1024]{1,2,0:T(8,128)(2,1)} fusion(f32[24,256,1024]{1,2,0:T(8,128)} %get-tuple-element.25, f32[24,256]{1,0:T(8,128)S(1)} %get-tuple-element.24), kind=kLoop, calls=%fused_computation.17 | loop fusion | flops 12582912 | bytes 37773312 | tf_op jit(solution)/shard_map/convert_element_type | solution.py:79
  426.0 9.7 %fusion.17 = bf16[32,8,24,128]{3,1,2,0:T(8,128)(2,1)S(1)} fusion(bf16[3072,3072]{1,0:T(8,128)(2,1)} %all-gather.2.cloned.1.call-done, bf16[1,256,3072]{2,1,0:T(8,128)(2,1)S(1)} %copy-done), kind=kOutput, calls=%fused_computation.39 | convolution fusion | flops 4832624640 | bytes 22020096 | tf_op jit(solution)/shard_map/td,hd->th/dot_general | solution.py:25
  442.7 13.2 %convolution_bitcast_fusion = f32[1,1024,24,128]{1,3,2,0:T(8,128)} fusion(bf16[256,24,128]{0,2,1:T(8,128)(2,1)S(1)} %copy.38, bf16[24,256,1024]{1,2,0:T(8,128)(2,1)} %fusion.9), kind=kOutput, calls=%fused_computation.24 | convolution fusion | flops 1610612736 | bytes 26738688 | tf_op jit(solution)/shard_map/jhqk,jqhd->jkhd/dot_general | solution.py:97
  455.9 12.7 %copy.59 = f32[1,1024,24,128]{3,2,1,0:T(8,128)} copy(f32[1,1024,24,128]{1,3,2,0:T(8,128)} %convolution_bitcast_fusion) | data formatting | bytes 25165824 | tf_op jit(solution)/shard_map/stack | solution.py:100
  468.6 9.1 %multiply_reduce_fusion = (f32[24,256]{1,0:T(8,128)S(1)}, bf16[24,128,256]{2,1,0:T(8,128)(2,1)S(1)}) fusion(f32[24,256,128]{1,2,0:T(8,128)} %copy.53, bf16[1024,24,128]{0,2,1:T(8,128)(2,1)} %copy.56, bf16[24,256,1024]{1,2,0:T(8,128)(2,1)} %fusion.9), kind=kOutput, calls=%fused_computation.32 | convolution fusion | flops 1613752320 | bytes 23617536 | tf_op jit(solution)/shard_map/jhqk,jkhd->jqhd/dot_general | solution.py:80
  477.7 16.5 %multiply_convert_fusion = bf16[24,256,1024]{1,2,0:T(8,128)(2,1)} fusion(f32[24,256]{1,0:T(8,128)S(1)} %get-tuple-element.26, f32[24,256,1024]{1,2,0:T(8,128)} %get-tuple-element.25, f32[24,256]{1,0:T(8,128)S(1)} %get-tuple-element.24, bf16[256,24,128]{0,2,1:T(8,128)(2,1)S(1)} %copy.38, bf16[1024,24,128]{0,2,1:T(8,128)(2,1)} %copy.56), kind=kOutput, calls=%fused_computation.9 | convolution fusion | flops 1635778560 | bytes 45662208 | tf_op jit(solution)/shard_map/jqhd,jkhd->jhqk/dot_general | solution.py:85
  494.3 12.5 %multiply_bitcast_fusion = f32[1,1024,24,128]{3,1,2,0:T(8,128)} fusion(bf16[24,256,1024]{1,2,0:T(8,128)(2,1)} %multiply_convert_fusion, bf16[256,24,128]{2,1,0:T(8,128)(2,1)S(1)} %bitcast.131), kind=kOutput, calls=%fused_computation.12 | convolution fusion | flops 1613758464 | bytes 26738688 | tf_op jit(solution)/shard_map/jhqk,jqhd->jkhd/dot_general | solution.py:94
  506.8 16.4 %copy.37 = f32[1,1024,24,128]{3,2,0,1:T(8,128)} copy(f32[1,1024,24,128]{3,1,2,0:T(8,128)} %multiply_bitcast_fusion) | data formatting | bytes 25165824 | tf_op jit(solution)/shard_map/mul | solution.py:94
  523.2 24.8 %fusion.1 = bf16[2,1,4,256,3072]{4,0,3,2,1:T(2,128)(2,1)S(1)} fusion(f32[1,1,4,256,3072]{4,0,3,2,1:T(1,128)} %bitcast.115, f32[1,1,4,256,3072]{4,0,3,2,1:T(1,128)} %bitcast.117), kind=kLoop, calls=%fused_computation.4 | loop fusion | flops 25165824 | bytes 37748736 | tf_op jit(solution)/shard_map/convert.2
  547.9 7.9 %slice_bitcast_fusion.2 = (bf16[2,1,256,3072]{3,0,2,1:T(2,128)(2,1)}, bf16[2,256,3072]{2,0,1:T(2,128)(2,1)}, bf16[2,1,256,3072]{3,0,2,1:T(2,128)(2,1)}) fusion(bf16[2,1,4,256,3072]{4,0,3,2,1:T(2,128)(2,1)S(1)} %fusion.1), kind=kLoop, calls=%fused_computation.28 | loop fusion | bytes 18874368 | tf_op jit(solution)/shard_map/convert_element_type | solution.py:102
  561.4 8.4 %multiply_convert_fusion.1 = bf16[24,128,256]{2,1,0:T(8,128)(2,1)S(1)} fusion(bf16[1024,24,128]{0,2,1:T(8,128)(2,1)} %copy.34, bf16[24,256,1024]{1,2,0:T(8,128)(2,1)} %multiply_convert_fusion), kind=kOutput, calls=%fused_computation.33 | convolution fusion | flops 1612185600 | bytes 20447232 | tf_op jit(solution)/shard_map/jhqk,jkhd->jqhd/dot_general | solution.py:90
  573.3 134.1 %all-reduce.5.cloned.1.call-done = bf16[2,256,3072]{2,0,1:T(2,128)(2,1)} async-done(((bf16[2,256,3072]{2,0,1:T(2,128)(2,1)}), bf16[2,256,3072]{2,0,1:T(2,128)(2,1)}) %all-reduce.5.cloned.1.call-update) | async-done | bytes 3145744 | tf_op jit(solution)/shard_map/psum | solution.py:107
  707.4 12.4 %fusion.13 = bf16[2,256,3072]{2,0,1:T(2,128)(2,1)S(1)} fusion(bf16[2,256,3072]{2,0,1:T(2,128)(2,1)} %all-reduce.5.cloned.1.call-done, bf16[2,256,3072]{2,0,1:T(2,128)(2,1)} %collective-permute-done.3, bf16[2,256,3072]{2,0,1:T(2,128)(2,1)} %collective-permute-done.2, f32[1,1,4,256,3072]{4,0,3,2,1:T(1,128)} %bitcast.116, f32[1,1,4,256,3072]{4,0,3,2,1:T(1,128)} %bitcast.118, ...), kind=kLoop, calls=%fused_computation.23 | loop fusion | flops 14155776 | bytes 37748736 | tf_op jit(solution)/shard_map/convert_element_type | solution.py:117
  719.8 4.5 fusion.31
  (44 shorter events, 39.7 us)
Async XLA Ops:
  8.0 418.0 %copy-start = (bf16[1,256,3072]{2,1,0:T(8,128)(2,1)S(1)}, bf16[1,256,3072]{2,1,0:T(8,128)(2,1)}, u32[]{:S(2)}) copy-start(bf16[1,256,3072]{2,1,0:T(8,128)(2,1)} %param.13) | copy-start | bytes 4718596
  8.0 349.1 %all-reduce.3.cloned.1.call-start = ((), (), s32[]{:S(2)}) async-start(), calls=%async_computation | async-start | bytes 6291456 | tf_op jit(solution)/shard_map/psum | solution.py:21
  14.1 9.1 %copy-start.5 = (s32[16,2]{0,1:T(2,128)S(1)}, s32[16,2]{0,1:T(2,128)}, u32[]{:S(2)}) copy-start(s32[16,2]{0,1:T(2,128)} %param.10) | copy-start | bytes 388
  14.1 12.5 %copy-start.2 = (bf16[1,256,3072]{2,1,0:T(8,128)(2,1)S(1)}, bf16[1,256,3072]{2,1,0:T(8,128)(2,1)}, u32[]{:S(2)}) copy-start(bf16[1,256,3072]{2,1,0:T(8,128)(2,1)} %param.7) | copy-start | bytes 4718596
  16.0 409.9 %all-gather.2.cloned.1.call-start = ((), (), s32[]{:S(2)}) async-start(), calls=%async_computation.1 | async-start | bytes 21233664 | tf_op jit(solution)/shard_map/all_gather | solution.py:28
  16.6 690.8 %all-reduce.5.cloned.1.call-start = ((), (), s32[]{:S(2)}) async-start(), calls=%async_computation.2 | async-start | bytes 6291456 | tf_op jit(solution)/shard_map/psum | solution.py:107
  16.7 44.4 %collective-permute-start.1 = (bf16[2,256,3072]{2,1,0:T(8,128)(2,1)}, bf16[2,256,3072]{2,1,0:T(8,128)(2,1)}, u32[]{:S(2)}, u32[]{:S(2)}) collective-permute-start(bf16[2,256,3072]{2,1,0:T(8,128)(2,1)} %constant_dynamic-update-slice_fusion), channel_id=1, source_target_pairs={{1,0},{2,1},{3,2},{4,3},{5,4},{6,5},{7,6},{8,7},{9,8},{10,9},{11,1... | collective-permute-start | bytes 9437192 | tf_op jit(solution)/shard_map/ppermute | solution.py:16
  20.0 41.1 %collective-permute-start = (bf16[2,256,3072]{2,1,0:T(8,128)(2,1)}, bf16[2,256,3072]{2,1,0:T(8,128)(2,1)}, u32[]{:S(2)}, u32[]{:S(2)}) collective-permute-start(bf16[2,256,3072]{2,1,0:T(8,128)(2,1)} %constant_dynamic-update-slice_fusion), channel_id=1, source_target_pairs={{0,1},{1,2},{2,3},{3,4},{4,5},{5,6},{6,7},{7,8},{8,9},{9,10},{10,1... | collective-permute-start | bytes 9437192 | tf_op jit(solution)/shard_map/ppermute | solution.py:16
  388.1 9.1 %copy-start.3 = (bf16[32,8,24,128]{3,2,1,0:T(8,128)(2,1)S(1)}, bf16[32,8,24,128]{3,2,1,0:T(8,128)(2,1)}, u32[]{:S(2)}) copy-start(bf16[32,8,24,128]{3,2,1,0:T(8,128)(2,1)} %copy.64) | copy-start | bytes 4718596
  477.7 16.6 %copy-start.4 = (bf16[32,8,24,128]{3,2,1,0:T(8,128)(2,1)S(1)}, bf16[32,8,24,128]{3,2,1,0:T(8,128)(2,1)}, u32[]{:S(2)}) copy-start(bf16[32,8,24,128]{3,2,1,0:T(8,128)(2,1)} %copy.64) | copy-start | bytes 4718596
  555.8 151.6 %collective-permute-start.2 = (bf16[2,256,3072]{2,0,1:T(2,128)(2,1)}, bf16[2,256,3072]{2,0,1:T(2,128)(2,1)}, u32[]{:S(2)}, u32[]{:S(2)}) collective-permute-start(bf16[2,256,3072]{2,0,1:T(2,128)(2,1)} %bitcast.128), channel_id=1, source_target_pairs={{1,0},{2,1},{3,2},{4,3},{5,4},{6,5},{7,6},{8,7},{9,8},{10,9},{11,1... | collective-permute-start | bytes 9437192 | tf_op jit(solution)/shard_map/ppermute | solution.py:16
  559.0 148.4 %collective-permute-start.3 = (bf16[2,256,3072]{2,0,1:T(2,128)(2,1)}, bf16[2,256,3072]{2,0,1:T(2,128)(2,1)}, u32[]{:S(2)}, u32[]{:S(2)}) collective-permute-start(bf16[2,256,3072]{2,0,1:T(2,128)(2,1)} %bitcast.127), channel_id=1, source_target_pairs={{0,1},{1,2},{2,3},{3,4},{4,5},{5,6},{6,7},{7,8},{8,9},{9,10},{10,1... | collective-permute-start | bytes 9437192 | tf_op jit(solution)/shard_map/ppermute | solution.py:16
  719.8 7.7 %copy-start.1 = (bf16[1,256,3072]{2,1,0:T(8,128)(2,1)S(1)}, bf16[1,256,3072]{2,1,0:T(8,128)(2,1)}, u32[]{:S(2)}) copy-start(bf16[1,256,3072]{2,1,0:T(8,128)(2,1)} %param.13) | copy-start | bytes 4718596
Sparse Core Ops, SparseCore 0:
  16.2 340.9 all-reduce.2
  556.0 151.3 all-reduce.4
Sparse Core Ops, SparseCore 1:
  18.2 195.4 all-gather.1
where the time goes:
time: 746 us; the launch traced here: 735 us
  waiting for transfers between devices  454 us (61%)
  local copies, waits for them, and re-layouts  98.2 us (13%)
  matrix products  84.8 us (11%)
  other arithmetic  66.6 us (9%)
  between operations  19.3 us (3%)
  starting transfers between devices  12.2 us (2%)
    psum x1, waiting for transfers between devices, from_root(): return lax.psum(kept, axis)  286 us
    psum x1, waiting for transfers between devices, local(): lax.psum(global_part.astype(jnp.bfloat16), 'sky').astype(jnp.float32)  134 us
    ppermute x4, waiting for transfers between devices, shifted(): return lax.ppermute(block, axis, route)  33.1 us
    unnamed x22, local copies, waits for them, and re-layouts  26.7 us
    another operation x1, other arithmetic  24.8 us
    another operation x3, local copies, waits for them, and re-layouts  19.2 us
    dot_general x1, matrix products, local(): jnp.einsum('jqhd,jkhd->jhqk', grad_rows, value_slots, preferred_element_t...  16.5 us
    mul x1, local copies, waits for them, and re-layouts, local(): jnp.einsum('jhqk,jqhd->jkhd', grad_scores, query_rows, preferred_element_...  16.4 us
  transfers between devices with their start and end apart: 7, of which 4 were waited for; matrix products, arithmetic and copies ran while one was open for 13% of the time, Pallas kernels for 0%

commit v1 on v0

v1 whole, which is shorter than its diff:
```python
import functools
import math

import jax
import jax.numpy as jnp
from jax import lax
from jax.experimental import pallas as pl
from jax.experimental.pallas import tpu as pltpu
from jax.sharding import Mesh, PartitionSpec as P

HEADS = 24
HD = 128
BLK = 256
D = 3072
HALF = D // 2
PART = BLK // 4
PER = 3
SHARDS = 8
SCALE = 1.0 / math.sqrt(HD)
LOG2E = 1.4426950408889634
DP = ("x_lo", "z")
SKY = ("x_hi", "y", "core")
CHUNKS = ((0, 1), (1, 1), (2, 1))
F32 = jnp.float32
BF16 = jnp.bfloat16


def attention_kernel(info, q_ref, ko_ref, vo_ref, inner_ref, outer_ref, kg_ref, vg_ref, go_ref, wm_ref, wo_ref, *rest):
    att_ref, gq_ref, own_ref, tin_ref, tout_ref, keep_ref, send_ref = rest[-7:]
    core = info[3]
    across = (((1,), (1,)), ((), ()))
    q = q_ref[...]
    first = pl.multiple_of(core * HALF, HALF)
    second = pl.multiple_of((1 - core) * HALF, HALF)
    ga_t = lax.dot_general(wm_ref[...], go_ref[:, pl.ds(first, HALF)], across, preferred_element_type=F32)
    ga_t += lax.dot_general(wo_ref[...], go_ref[:, pl.ds(second, HALF)], across, preferred_element_type=F32)
    ga_tb = ga_t.astype(BF16)
    ga_r = ga_tb.astype(F32)
    ga = ga_r.T.astype(BF16)
    keys = [ko_ref[...], inner_ref[0], outer_ref[0], kg_ref[...]]
    values = [vo_ref[...], inner_ref[1], outer_ref[1], vg_ref[...]]
    scores = []
    for j in range(4):
        s = lax.dot_general(keys[j], q, across, preferred_element_type=F32) * (SCALE * LOG2E)
        if j > 0:
            s = s + jnp.where(info[j - 1] > 0, 0.0, -jnp.inf).astype(F32)
        scores.append(s)
    top = functools.reduce(jnp.maximum, [jnp.max(s, axis=0, keepdims=True) for s in scores])
    exps = [jnp.exp2(s - top) for s in scores]
    total = functools.reduce(jnp.add, [jnp.sum(e, axis=0, keepdims=True) for e in exps])
    inverse = 1.0 / total
    weights = [e * inverse for e in exps]
    weights_b = [p.astype(BF16) for p in weights]
    att_t = jnp.zeros((HD, BLK), F32)
    for j in range(4):
        att_t += jnp.dot(values[j].T, weights_b[j], preferred_element_type=F32)
    att_r = att_t.astype(BF16).astype(F32)
    att_ref[...] = att_r.T.astype(BF16)
    delta = jnp.sum(ga_r * att_r, axis=0, keepdims=True)
    gq_t = jnp.zeros((HD, BLK), F32)
    key_terms, value_terms = [], []
    for j in range(4):
        gw = jnp.dot(values[j], ga_tb, preferred_element_type=F32)
        gs = (weights[j] * (gw - delta)).astype(BF16)
        gq_t += jnp.dot(keys[j].T, gs, preferred_element_type=F32)
        key_terms.append((jnp.dot(gs, q, preferred_element_type=F32) * SCALE).astype(BF16))
        value_terms.append(jnp.dot(weights_b[j], ga, preferred_element_type=F32).astype(BF16))
    gq_ref[...] = (gq_t * SCALE).T.astype(BF16)
    for ref, j in ((own_ref, 0), (tin_ref, 1), (tout_ref, 2)):
        ref[0] = key_terms[j]
        ref[1] = value_terms[j]
    keep_ref[...] = jnp.where(core == 0, key_terms[3], value_terms[3])
    send_ref[...] = jnp.where(core == 0, value_terms[3], key_terms[3])


def attention(chunk, info, q, k, v, inner, outer, kg, vg, go, wm, wo, prior):
    start, n = chunk
    width = SHARDS * n * HD
    steps = SHARDS * n

    def head(t, *_):
        return (0, PER * (t // n) + start + t % n)

    def col(t, *_):
        return (0, t)

    def row(t, *_):
        return (t, 0)

    def pair(t, *_):
        return (0, 0, t)

    def whole(t, *_):
        return (0, 0)

    one = (BLK, HD)
    two = (2, BLK, HD)
    in_specs = [
        pl.BlockSpec(one, head),
        pl.BlockSpec(one, head),
        pl.BlockSpec(one, head),
        pl.BlockSpec(two, pair),
        pl.BlockSpec(two, pair),
        pl.BlockSpec(one, col),
        pl.BlockSpec(one, col),
        pl.BlockSpec((BLK, D), whole),
        pl.BlockSpec((HD, HALF), row),
        pl.BlockSpec((HD, HALF), row),
    ] + [pl.BlockSpec(memory_space=pl.ANY)] * len(prior)
    out_specs = [
        pl.BlockSpec(one, head),
        pl.BlockSpec(one, head),
        pl.BlockSpec(two, pair),
        pl.BlockSpec(two, pair),
        pl.BlockSpec(two, pair),
        pl.BlockSpec(one, col),
        pl.BlockSpec(one, col),
    ]
    full = jax.ShapeDtypeStruct((BLK, D), BF16)
    stacked = jax.ShapeDtypeStruct((2, BLK, width), BF16)
    single = jax.ShapeDtypeStruct((BLK, width), BF16)
    return pl.pallas_call(
        attention_kernel,
        grid_spec=pltpu.PrefetchScalarGridSpec(
            num_scalar_prefetch=1, grid=(steps,), in_specs=in_specs, out_specs=out_specs
        ),
        out_shape=[full, full, stacked, stacked, stacked, single, single],
        input_output_aliases={11: 0, 12: 1} if prior else {},
        compiler_params=pltpu.CompilerParams(vmem_limit_bytes=32 * 2**20),
        cost_estimate=pl.CostEstimate(
            flops=steps * (12 * BLK * 4 * BLK * HD + 2 * BLK * HD * D),
            bytes_accessed=steps * (BLK * HD * 2 * 20 + HD * D * 2),
            transcendentals=steps * BLK * 4 * BLK,
        ),
        name="attention",
    )(info, q, k, v, inner, outer, kg, vg, go, wm, wo, *prior)


def combine_kernel(info, own_ref, rin_ref, rout_ref, mine_ref, theirs_ref, *rest):
    gk_ref, gv_ref, total = rest[-3:]
    hit, y, core = info[4], info[5], info[3]
    total[...] = own_ref[...].astype(F32) + rin_ref[...].astype(F32) + rout_ref[...].astype(F32)

    @pl.when(hit > 0)
    def _():
        for r in range(4):
            place = pl.multiple_of(lax.rem(y + r, 4) * PART, PART)
            mine = mine_ref[r].astype(F32)
            theirs = theirs_ref[r].astype(F32)
            total[0, pl.ds(place, PART)] += jnp.where(core == 0, mine, theirs)
            total[1, pl.ds(place, PART)] += jnp.where(core == 0, theirs, mine)

    gk_ref[...] = total[0].astype(BF16)
    gv_ref[...] = total[1].astype(BF16)


def combine(chunk, info, own, rin, rout, mine, theirs, prior):
    start, n = chunk
    steps = SHARDS * n

    def head(t, *_):
        return (0, PER * (t // n) + start + t % n)

    def pair(t, *_):
        return (0, 0, t)

    two = pl.BlockSpec((2, BLK, HD), pair)
    quarters = pl.BlockSpec((4, PART, HD), pair)
    full = jax.ShapeDtypeStruct((BLK, D), BF16)
    return pl.pallas_call(
        combine_kernel,
        grid_spec=pltpu.PrefetchScalarGridSpec(
            num_scalar_prefetch=1,
            grid=(steps,),
            in_specs=[two, two, two, quarters, quarters] + [pl.BlockSpec(memory_space=pl.ANY)] * len(prior),
            out_specs=[pl.BlockSpec((BLK, HD), head)] * 2,
            scratch_shapes=[pltpu.VMEM((2, BLK, HD), F32)],
        ),
        out_shape=[full, full],
        input_output_aliases={6: 0, 7: 1} if prior else {},
        compiler_params=pltpu.CompilerParams(vmem_limit_bytes=32 * 2**20),
        cost_estimate=pl.CostEstimate(
            flops=steps * BLK * HD * 8, bytes_accessed=steps * BLK * HD * 2 * 12, transcendentals=0
        ),
        name="combine",
    )(info, own, rin, rout, mine, theirs, *prior)


def move(x, axis, step, size):
    return lax.ppermute(x, axis, [(i, (i + step) % size) for i in range(size)])


def swap_core(x):
    return move(x, "core", 1, 2)


def swap_outer(x):
    route = [(i, i + 1) for i in range(1, 15, 2)] + [(i + 1, i) for i in range(1, 15, 2)]
    return lax.ppermute(x, SKY, route)


def columns(x, chunk):
    start, n = chunk
    return x.reshape(BLK, SHARDS, PER, HD)[:, :, start : start + n].reshape(BLK, SHARDS * n * HD)


def spread_global(kv, inner, root, x, y, core):
    root_core, root_y, root_x = root % 2, (root // 2) % 4, root // 8
    source = jnp.where(root_core == core, kv, inner)
    cand = jnp.where(core == 0, source[0], source[1])
    pieces = [lax.dynamic_slice_in_dim(cand, ((y + r) % 4) * PART, PART, 0) for r in range(4)]
    arrived = [pieces[0]] + [move(pieces[r], "y", r, 4) for r in range(1, 4)]
    came = (y - root_y) % 4
    mine = arrived[0]
    for r in range(1, 4):
        mine = jnp.where(came == r, arrived[r], mine)
    other = move(mine, "x_hi", 1, 2)
    quarter = jnp.where(root_x == x, mine, other)
    parts = [quarter] + [move(quarter, "y", -r, 4) for r in range(1, 4)]
    held = jnp.concatenate(parts, axis=0)
    theirs = swap_core(held)
    return jnp.where(core == 0, held, theirs), jnp.where(core == 0, theirs, held)


def gather_terms(keep, send):
    both = (keep.astype(F32) + swap_core(send).astype(F32)).astype(BF16)
    arrived = [both[:PART]] + [move(both[r * PART : (r + 1) * PART], "y", r, 4) for r in range(1, 4)]
    quarter = functools.reduce(jnp.add, [a.astype(F32) for a in arrived]).astype(BF16)
    quarter = (quarter.astype(F32) + move(quarter, "x_hi", 1, 2).astype(F32)).astype(BF16)
    parts = [quarter] + [move(quarter, "y", -r, 4) for r in range(1, 4)]
    mine = jnp.stack(parts)
    return mine, swap_core(mine)


def local(queries, key_states, value_states, key_blocks, global_block, w_out, grad_out):
    x, y, core = lax.axis_index("x_hi"), lax.axis_index("y"), lax.axis_index("core")
    row = (x * 4 + y) * 2 + core
    root = global_block[0]
    ids = lax.dynamic_slice_in_dim(key_blocks, row, 1, 0)[0]
    above, below = ids[0], ids[1]
    inner_id = jnp.where(core == 0, below, above)
    outer_id = jnp.where(core == 0, above, below)
    live = (root != row) & (root != above) & (root != below)
    info = jnp.stack([inner_id >= 0, outer_id >= 0, live, core, root == row, y]).astype(jnp.int32)
    q, k, v, go = queries[0], key_states[0], value_states[0], grad_out[0]
    w_half = lax.dynamic_slice_in_dim(w_out, core * HALF, HALF, 1)
    grads, totals = (), ()
    for chunk in CHUNKS:
        start, n = chunk
        rows = w_half[start * HD : (start + n) * HD]
        wm = lax.all_gather(rows, DP, axis=0, tiled=True)
        wo = swap_core(wm)
        kv = jnp.stack([columns(k, chunk), columns(v, chunk)])
        inner = swap_core(kv)
        outer = swap_outer(kv)
        kg, vg = spread_global(kv, inner, root, x, y, core)
        out = attention(chunk, info, q, k, v, inner, outer, kg, vg, go, wm, wo, grads)
        grads = tuple(out[:2])
        own, tin, tout, keep, send = out[2:]
        rin, rout = swap_core(tin), swap_outer(tout)
        mine, theirs = gather_terms(keep, send)
        totals = tuple(combine(chunk, info, own, rin, rout, mine, theirs, totals))
    return tuple(a[None] for a in grads + totals)


def solution(mesh):
    inside = Mesh(mesh.devices.reshape(2, 4, 2, 4, 2), DP + SKY)
    rows = P(DP, SKY, None)
    return jax.shard_map(
        local,
        mesh=inside,
        in_specs=(rows, rows, rows, P(), P(), P(DP, None), rows),
        out_specs=(rows, rows, rows, rows),
        check_vma=False,
    )
```

time: 746 us -> 391 us (0.52)
  waiting for transfers between devices: 454 us -> 117 us
  starting transfers between devices: 12.2 us -> 110 us
  matrix products: 84.8 us -> 0 us
  Pallas kernels: 0 us -> 81.2 us
  local copies, waits for them, and re-layouts: 98.2 us -> 30.5 us
  other arithmetic: 66.6 us -> 26.9 us
    psum x2 -> x0, waiting for transfers between devices: 421 us -> none  [the longest x1 286 us: from_root(): return lax.psum(kept, axis)]
    ppermute x4 -> x66, starting transfers between devices: 12.1 us -> 110 us  [the longest x60 89.8 us: move(): return lax.ppermute(x, axis, [(i, (i + step) % size) for i in range(size)])]
    pallas_call x0 -> x6, Pallas kernels: none -> 81.2 us  [the longest x3 68.6 us: attention(): pl.pallas_call(attention_kernel, grid_spec=pltpu.PrefetchScalarGridSpec(n...]
    dot_general x6 -> x0, matrix products: 69.5 us -> none  [the longest x1 16.5 us: local(): jnp.einsum('jqhd,jkhd->jhqk', grad_rows, value_slots, preferred_element_t...]
    all_gather x1 -> x3, waiting for transfers between devices: 0.01 us -> 62 us  [local(): wm = lax.all_gather(rows, DP, axis=0, tiled=True)]
    another operation x4 -> x6, other arithmetic: 33 us -> 7.04 us  [the longest x3 6.83 us: local(): kv = jnp.stack([columns(k, chunk), columns(v, chunk)])]
    another operation x6 -> x7, local copies, waits for them, and re-layouts: 38.3 us -> 12.5 us  [the longest x6 12.4 us: local(): kv = jnp.stack([columns(k, chunk), columns(v, chunk)])]
    convert_element_type x2 -> x9, other arithmetic: 25.9 us -> 1.94 us  [the longest x3 1.61 us: gather_terms(): both = (keep.astype(F32) + swap_core(send).astype(F32)).astype(BF16)]
  transfers between devices with their start and end apart: 7 -> 69, of which waited for: 4 -> 27; matrix products, arithmetic and copies ran while one was open for 13% -> 13% of each run, Pallas kernels for 0% -> 20%
where the time goes in v1:
time: 391 us; the launch traced here: 385 us
  waiting for transfers between devices  117 us (30%)
  starting transfers between devices  110 us (28%)
  Pallas kernels  81.2 us (21%)
  local copies, waits for them, and re-layouts  30.5 us (8%)
  other arithmetic  26.9 us (7%)
  between operations  18.8 us (5%)
    ppermute x60, starting transfers between devices, move(): return lax.ppermute(x, axis, [(i, (i + step) % size) for i in range(size)])  89.8 us
    pallas_call x3, Pallas kernels, attention(): pl.pallas_call(attention_kernel, grid_spec=pltpu.PrefetchScalarGridSpec(n...  68.6 us
    all_gather x3, waiting for transfers between devices, local(): wm = lax.all_gather(rows, DP, axis=0, tiled=True)  62 us
    ppermute x60, waiting for transfers between devices, move(): return lax.ppermute(x, axis, [(i, (i + step) % size) for i in range(size)])  44.6 us
    ppermute x6, starting transfers between devices, swap_outer(): return lax.ppermute(x, SKY, route)  20.4 us
    pallas_call x3, Pallas kernels, combine(): pl.pallas_call(combine_kernel, grid_spec=pltpu.PrefetchScalarGridSpec(num...  12.6 us
    another operation x6, local copies, waits for them, and re-layouts, local(): kv = jnp.stack([columns(k, chunk), columns(v, chunk)])  12.4 us
    ppermute x6, waiting for transfers between devices, swap_outer(): return lax.ppermute(x, SKY, route)  9.35 us
  transfers between devices with their start and end apart: 69, of which 27 were waited for; matrix products, arithmetic and copies ran while one was open for 13% of the time, Pallas kernels for 20%

profile of v1, /device:TPU:1, one launch (start us, length us, event | category | flops | bytes accessed | tf_op | source)
XLA Modules:
  0.0 384.9 jit_solution(15465379250713105500)
XLA Ops:
  33.8 3.7 collective-permute-start.23
  46.5 3.9 %collective-permute-start.24 = (bf16[64,1024]{1,0:T(8,128)(2,1)S(1)}, bf16[64,1024]{1,0:T(8,128)(2,1)S(1)}, u32[]{:S(2)}, u32[]{:S(2)}) collective-permute-start(bf16[64,1024]{1,0:T(8,128)(2,1)S(1)} %get-tuple-element.84), channel_id=1, source_target_pairs={{0,6},{2,0},{4,2},{6,4},{1,7},{3,1},{5,3},{7,5},{8,14},{10,8},{12,... | collective-permute-start | bytes 393224 | tf_op jit(solution)/shard_map/ppermute | solution.py:190
  65.8 7.7 %collective-permute-start.2 = (bf16[64,1024]{1,0:T(8,128)(2,1)}, bf16[64,1024]{1,0:T(8,128)(2,1)S(1)}, u32[]{:S(2)}, u32[]{:S(2)}) collective-permute-start(bf16[64,1024]{1,0:T(8,128)(2,1)} %get-tuple-element.90), channel_id=1, source_target_pairs={{0,6},{2,0},{4,2},{6,4},{1,7},{3,1},{5,3},{7,5},{8,14},{10,8},{12,... | collective-permute-start | bytes 393224 | tf_op jit(solution)/shard_map/ppermute | solution.py:190
  75.0 4.2 %collective-permute-done.2 = bf16[64,1024]{1,0:T(8,128)(2,1)S(1)} collective-permute-done((bf16[64,1024]{1,0:T(8,128)(2,1)}, bf16[64,1024]{1,0:T(8,128)(2,1)S(1)}, u32[]{:S(2)}, u32[]{:S(2)}) %collective-permute-start.2) | collective-permute-done | bytes 131104 | tf_op jit(solution)/shard_map/ppermute | solution.py:190
  83.1 27.8 %all-gather.6.cloned.1.call-done.wm_ref = bf16[1024,1536]{1,0:T(8,128)(2,1)} async-done(((bf16[128,1536]{1,0:T(8,128)(2,1)}), bf16[1024,1536]{1,0:T(8,128)(2,1)}) %all-gather.6.cloned.1.call-update) | async-done | bytes 3145744 | tf_op jit(solution)/shard_map/all_gather | solution.py:251
  121.9 34.1 %all-gather.4.cloned.1.call-done.wm_ref = bf16[1024,1536]{1,0:T(8,128)(2,1)} async-done(((bf16[128,1536]{1,0:T(8,128)(2,1)}), bf16[1024,1536]{1,0:T(8,128)(2,1)}) %all-gather.4.cloned.1.call-update) | async-done | bytes 3145744 | tf_op jit(solution)/shard_map/all_gather | solution.py:251
  183.9 4.5 %collective-permute-start.31 = (bf16[256,1024]{1,0:T(8,128)(2,1)}, bf16[256,1024]{1,0:T(8,128)(2,1)}, u32[]{:S(2)}, u32[]{:S(2)}) collective-permute-start(bf16[256,1024]{1,0:T(8,128)(2,1)} %pad_maximum_fusion.5), channel_id=1, source_target_pairs={{0,1},{1,0},{2,3},{3,2},{4,5},{5,4},{6,7},{7,6},{8,9},{9,8},{10,11... | collective-permute-start | bytes 1572872 | tf_op jit(solution)/shard_map/ppermute | solution.py:190
  201.5 3.5 collective-permute-start.1
  205.4 22.9 %attention.3 = (bf16[256,3072]{1,0:T(8,128)(2,1)}, bf16[256,3072]{1,0:T(8,128)(2,1)}, bf16[2,256,1024]{2,1,0:T(8,128)(2,1)S(1)}, bf16[2,256,1024]{2,1,0:T(8,128)...) custom-call(s32[6]{0:T(128)S(1)} %stack.97.info, ...), custom_call_target="tpu_custom_call" | custom-call | flops 4831838208 | bytes 16777216 | tf_op jit(solution)/shard_map/attention/pallas_call | solution.py:122
  231.2 23.0 %attention.4 = (bf16[256,3072]{1,0:T(8,128)(2,1)}, bf16[256,3072]{1,0:T(8,128)(2,1)}, bf16[2,256,1024]{2,1,0:T(8,128)(2,1)S(1)}, bf16[2,256,1024]{2,1,0:T(8,128)...) custom-call(s32[6]{0:T(128)S(1)} %stack.97.info, ...), custom_call_target="tpu_custom_call", output_to_operand_aliasing={{0}: (11, {}), {1}: (12, {})} | custom-call | flops 4831838208 | bytes 16777216 | tf_op jit(solution)/shard_map/attention/pallas_call | solution.py:122
  254.3 22.7 %attention.5 = (bf16[256,3072]{1,0:T(8,128)(2,1)}, bf16[256,3072]{1,0:T(8,128)(2,1)}, bf16[2,256,1024]{2,1,0:T(8,128)(2,1)S(1)}, bf16[2,256,1024]{2,1,0:T(8,128)...) custom-call(s32[6]{0:T(128)S(1)} %stack.97.info, ...), custom_call_target="tpu_custom_call", output_to_operand_aliasing={{0}: (11, {}), {1}: (12, {})} | custom-call | flops 4831838208 | bytes 16777216 | tf_op jit(solution)/shard_map/attention/pallas_call | solution.py:122
  278.7 3.7 collective-permute-start.58
  282.5 5.3 %collective-permute-start.59 = (bf16[64,1024]{1,0:T(8,128)(2,1)S(1)}, bf16[64,1024]{1,0:T(8,128)(2,1)S(1)}, u32[]{:S(2)}, u32[]{:S(2)}) collective-permute-start(bf16[64,1024]{1,0:T(8,128)(2,1)S(1)} %get-tuple-element.75), channel_id=1, source_target_pairs={{0,4},{2,6},{4,0},{6,2},{1,5},{3,7},{5,1},{7,3},{8,12},{10,14},{12... | collective-permute-start | bytes 393224 | tf_op jit(solution)/shard_map/ppermute | solution.py:190
  290.4 3.8 collective-permute-done.59
  299.9 3.4 collective-permute-start.38
  306.4 7.0 %collective-permute-start.61 = (bf16[64,1024]{1,0:T(8,128)(2,1)S(1)}, bf16[64,1024]{1,0:T(8,128)(2,1)S(1)}, u32[]{:S(2)}, u32[]{:S(2)}) collective-permute-start(bf16[64,1024]{1,0:T(8,128)(2,1)S(1)} %add_convert_fusion.4), channel_id=1, source_target_pairs={{0,8},{8,0},{1,9},{9,1},{2,10},{10,2},{3,11},{11,3},{4,12},{12,4},... | collective-permute-start | bytes 393224 | tf_op jit(solution)/shard_map/ppermute | solution.py:190
  313.7 3.7 collective-permute-done.61
  324.4 4.2 %collective-permute-done.63 = bf16[64,1024]{1,0:T(8,128)(2,1)S(1)} collective-permute-done((bf16[64,1024]{1,0:T(8,128)(2,1)S(1)}, bf16[64,1024]{1,0:T(8,128)(2,1)S(1)}, u32[]{:S(2)}, u32[]{:S(2)}) %collective-permute-start.63) | collective-permute-done | bytes 131104 | tf_op jit(solution)/shard_map/ppermute | solution.py:190
  332.8 3.5 collective-permute-done.52
  344.1 6.3 %collective-permute-start.45 = (bf16[2,256,1024]{2,1,0:T(8,128)(2,1)S(1)}, bf16[2,256,1024]{2,1,0:T(8,128)(2,1)S(1)}, u32[]{:S(2)}, u32[]{:S(2)}) collective-permute-start(bf16[2,256,1024]{2,1,0:T(8,128)(2,1)S(1)} %get-tuple-element.44), channel_id=1, source_target_pairs={{1,2},{3,4},{5,6},{7,8},{9,10},{11,12},{13,14},{2,1},{4,3},{6,5},{... | collective-permute-start | bytes 3145736 | tf_op jit(solution)/shard_map/ppermute | solution.py:199
  356.4 4.2 %combine.3 = (bf16[256,3072]{1,0:T(8,128)(2,1)}, bf16[256,3072]{1,0:T(8,128)(2,1)}) custom-call(s32[6]{0:T(128)S(1)} %stack.97.info, bf16[2,256,1024]{2,1,0:T(8,128)(2,1)S(1)} %get-tuple-element.47.own_ref, bf16[2,256,1024]{2,1,0:T(8,128)(2,1)S(1)} %collective-permute-done.55.rin_ref, bf16[2,256,1024]{2,1,0:T(8,128)(2,1)S(1)} %collective-permute-done.56.rout_ref, ...), custom_call_target="tpu_custom_call" | custom-call | flops 2097152 | bytes 6291456 | tf_op jit(solution)/shard_map/combine/pallas_call | solution.py:170
  362.9 4.2 %combine.4 = (bf16[256,3072]{1,0:T(8,128)(2,1)}, bf16[256,3072]{1,0:T(8,128)(2,1)}) custom-call(s32[6]{0:T(128)S(1)} %stack.97.info, bf16[2,256,1024]{2,1,0:T(8,128)(2,1)S(1)} %get-tuple-element.42.own_ref, bf16[2,256,1024]{2,1,0:T(8,128)(2,1)S(1)} %collective-permute-done.44.rin_ref, ...), custom_call_target="tpu_custom_call", output_to_operand_aliasing={{0}: (6, {}), {1}: (7, {})} | custom-call | flops 2097152 | bytes 6291456 | tf_op jit(solution)/shard_map/combine/pallas_call | solution.py:170
  367.1 7.0 %collective-permute-done.34.rout_ref = bf16[2,256,1024]{2,1,0:T(8,128)(2,1)S(1)} collective-permute-done((bf16[2,256,1024]{2,1,0:T(8,128)(2,1)S(1)}, bf16[2,256,1024]{2,1,0:T(8,128)(2,1)S(1)}, u32[]{:S(2)}, u32[]{:S(2)}) %collective-permute-start.34) | collective-permute-done | bytes 1048608 | tf_op jit(solution)/shard_map/ppermute | solution.py:199
  374.1 4.2 %combine.5 = (bf16[256,3072]{1,0:T(8,128)(2,1)}, bf16[256,3072]{1,0:T(8,128)(2,1)}) custom-call(s32[6]{0:T(128)S(1)} %stack.97.info, bf16[2,256,1024]{2,1,0:T(8,128)(2,1)S(1)} %get-tuple-element.37.own_ref, bf16[2,256,1024]{2,1,0:T(8,128)(2,1)S(1)} %collective-permute-done.33.rin_ref, ...), custom_call_target="tpu_custom_call", output_to_operand_aliasing={{0}: (6, {}), {1}: (7, {})} | custom-call | flops 2097152 | bytes 6291456 | tf_op jit(solution)/shard_map/combine/pallas_call | solution.py:170
  (246 shorter events, 147.5 us)
Async XLA Ops:
  7.2 55.6 %all-gather.8.cloned.1.call-start = ((), (), s32[]{:S(2)}) async-start(), calls=%async_computation.2 | async-start | bytes 3538944 | tf_op jit(solution)/shard_map/all_gather | solution.py:251
  9.7 101.2 %all-gather.6.cloned.1.call-start = ((), (), s32[]{:S(2)}) async-start(), calls=%async_computation.1 | async-start | bytes 3538944 | tf_op jit(solution)/shard_map/all_gather | solution.py:251
  10.4 145.6 %all-gather.4.cloned.1.call-start = ((), (), s32[]{:S(2)}) async-start(), calls=%async_computation | async-start | bytes 3538944 | tf_op jit(solution)/shard_map/all_gather | solution.py:251
  25.9 18.7 %collective-permute-start.22 = (bf16[2,256,1024]{2,1,0:T(8,128)(2,1)}, bf16[2,256,1024]{2,1,0:T(8,128)(2,1)}, u32[]{:S(2)}, u32[]{:S(2)}) collective-permute-start(bf16[2,256,1024]{2,1,0:T(8,128)(2,1)} %pad_maximum_fusion.2), channel_id=1, source_target_pairs={{0,1},{1,0},{2,3},{3,2},{4,5},{5,4},{6,7},{7,6},{8,9},{9,8},{10,11... | collective-permute-start | bytes 3145736 | tf_op jit(solution)/shard_map/ppermute | solution.py:190
  33.8 16.6 %collective-permute-start.11 = (bf16[2,256,1024]{2,1,0:T(8,128)(2,1)}, bf16[2,256,1024]{2,1,0:T(8,128)(2,1)}, u32[]{:S(2)}, u32[]{:S(2)}) collective-permute-start(bf16[2,256,1024]{2,1,0:T(8,128)(2,1)} %pad_maximum_fusion.1), channel_id=1, source_target_pairs={{0,1},{1,0},{2,3},{3,2},{4,5},{5,4},{6,7},{7,6},{8,9},{9,8},{10,11... | collective-permute-start | bytes 3145736 | tf_op jit(solution)/shard_map/ppermute | solution.py:190
  33.8 85.5 %collective-permute-start.23 = (bf16[2,256,1024]{2,1,0:T(8,128)(2,1)}, bf16[2,256,1024]{2,1,0:T(8,128)(2,1)}, u32[]{:S(2)}, u32[]{:S(2)}) collective-permute-start(bf16[2,256,1024]{2,1,0:T(8,128)(2,1)} %pad_maximum_fusion.2), channel_id=1, source_target_pairs={{1,2},{3,4},{5,6},{7,8},{9,10},{11,12},{13,14},{2,1},{4,3},{6,5},{... | collective-permute-start | bytes 3145736 | tf_op jit(solution)/shard_map/ppermute | solution.py:199
  62.8 142.6 %collective-permute-start.32 = (bf16[1024,1536]{1,0:T(8,128)(2,1)}, bf16[1024,1536]{1,0:T(8,128)(2,1)}, u32[]{:S(2)}, u32[]{:S(2)}) collective-permute-start(bf16[1024,1536]{1,0:T(8,128)(2,1)} %all-gather.8.cloned.1.call-done.wm_ref), channel_id=1, source_target_pairs={{0,1},{1,0},{2,3},{3,2},{4,5},{5,4},{6,7},{7,6},{8,9},{9,8},{10,11... | collective-permute-start | bytes 9437192 | tf_op jit(solution)/shard_map/ppermute | solution.py:190
  79.2 36.0 %collective-permute-start.27 = (bf16[64,1024]{1,0:T(8,128)(2,1)S(1)}, bf16[64,1024]{1,0:T(8,128)(2,1)S(1)}, u32[]{:S(2)}, u32[]{:S(2)}) collective-permute-start(bf16[64,1024]{1,0:T(8,128)(2,1)S(1)} %fusion.1), channel_id=1, source_target_pairs={{0,8},{8,0},{1,9},{9,1},{2,10},{10,2},{3,11},{11,3},{4,12},{12,4},... | collective-permute-start | bytes 393224 | tf_op jit(solution)/shard_map/ppermute | solution.py:190
  80.6 41.3 %collective-permute-start.16 = (bf16[64,1024]{1,0:T(8,128)(2,1)S(1)}, bf16[64,1024]{1,0:T(8,128)(2,1)}, u32[]{:S(2)}, u32[]{:S(2)}) collective-permute-start(bf16[64,1024]{1,0:T(8,128)(2,1)S(1)} %fusion.3), channel_id=1, source_target_pairs={{0,8},{8,0},{1,9},{9,1},{2,10},{10,2},{3,11},{11,3},{4,12},{12,4},... | collective-permute-start | bytes 393224 | tf_op jit(solution)/shard_map/ppermute | solution.py:190
  110.9 117.9 %collective-permute-start.21 = (bf16[1024,1536]{1,0:T(8,128)(2,1)}, bf16[1024,1536]{1,0:T(8,128)(2,1)}, u32[]{:S(2)}, u32[]{:S(2)}) collective-permute-start(bf16[1024,1536]{1,0:T(8,128)(2,1)} %all-gather.6.cloned.1.call-done.wm_ref), channel_id=1, source_target_pairs={{0,1},{1,0},{2,3},{3,2},{4,5},{5,4},{6,7},{7,6},{8,9},{9,8},{10,11... | collective-permute-start | bytes 9437192 | tf_op jit(solution)/shard_map/ppermute | solution.py:190
  115.9 43.4 %collective-permute-start.5 = (bf16[64,1024]{1,0:T(8,128)(2,1)}, bf16[64,1024]{1,0:T(8,128)(2,1)}, u32[]{:S(2)}, u32[]{:S(2)}) collective-permute-start(bf16[64,1024]{1,0:T(8,128)(2,1)} %fusion.5), channel_id=1, source_target_pairs={{0,8},{8,0},{1,9},{9,1},{2,10},{10,2},{3,11},{11,3},{4,12},{12,4},... | collective-permute-start | bytes 393224 | tf_op jit(solution)/shard_map/ppermute | solution.py:190
  119.2 42.8 %collective-permute-start.28 = (bf16[64,1024]{1,0:T(8,128)(2,1)S(1)}, bf16[64,1024]{1,0:T(8,128)(2,1)S(1)}, u32[]{:S(2)}, u32[]{:S(2)}) collective-permute-start(bf16[64,1024]{1,0:T(8,128)(2,1)S(1)} %broadcast_select_fusion.9), channel_id=1, source_target_pairs={{0,6},{2,0},{4,2},{6,4},{1,7},{3,1},{5,3},{7,5},{8,14},{10,8},{12,... | collective-permute-start | bytes 393224 | tf_op jit(solution)/shard_map/ppermute | solution.py:190
  156.0 98.3 %collective-permute-start.10 = (bf16[1024,1536]{1,0:T(8,128)(2,1)}, bf16[1024,1536]{1,0:T(8,128)(2,1)}, u32[]{:S(2)}, u32[]{:S(2)}) collective-permute-start(bf16[1024,1536]{1,0:T(8,128)(2,1)} %all-gather.4.cloned.1.call-done.wm_ref), channel_id=1, source_target_pairs={{0,1},{1,0},{2,3},{3,2},{4,5},{5,4},{6,7},{7,6},{8,9},{9,8},{10,11... | collective-permute-start | bytes 9437192 | tf_op jit(solution)/shard_map/ppermute | solution.py:190
  196.2 32.1 %collective-permute-start.12 = (bf16[2,256,1024]{2,1,0:T(8,128)(2,1)}, bf16[2,256,1024]{2,1,0:T(8,128)(2,1)S(1)}, u32[]{:S(2)}, u32[]{:S(2)}) collective-permute-start(bf16[2,256,1024]{2,1,0:T(8,128)(2,1)} %pad_maximum_fusion.1), channel_id=1, source_target_pairs={{1,2},{3,4},{5,6},{7,8},{9,10},{11,12},{13,14},{2,1},{4,3},{6,5},{... | collective-permute-start | bytes 3145736 | tf_op jit(solution)/shard_map/ppermute | solution.py:199
  201.5 52.7 %collective-permute-start.1 = (bf16[2,256,1024]{2,1,0:T(8,128)(2,1)}, bf16[2,256,1024]{2,1,0:T(8,128)(2,1)S(1)}, u32[]{:S(2)}, u32[]{:S(2)}) collective-permute-start(bf16[2,256,1024]{2,1,0:T(8,128)(2,1)} %pad_maximum_fusion), channel_id=1, source_target_pairs={{1,2},{3,4},{5,6},{7,8},{9,10},{11,12},{13,14},{2,1},{4,3},{6,5},{... | collective-permute-start | bytes 3145736 | tf_op jit(solution)/shard_map/ppermute | solution.py:199
  228.3 49.2 %collective-permute-start.57 = (bf16[256,1024]{1,0:T(8,128)(2,1)S(1)}, bf16[256,1024]{1,0:T(8,128)(2,1)}, u32[]{:S(2)}, u32[]{:S(2)}) collective-permute-start(bf16[256,1024]{1,0:T(8,128)(2,1)S(1)} %get-tuple-element.51), channel_id=1, source_target_pairs={{0,1},{1,0},{2,3},{3,2},{4,5},{5,4},{6,7},{7,6},{8,9},{9,8},{10,11... | collective-permute-start | bytes 1572872 | tf_op jit(solution)/shard_map/ppermute | solution.py:190
  228.3 123.7 %collective-permute-start.55 = (bf16[2,256,1024]{2,1,0:T(8,128)(2,1)S(1)}, bf16[2,256,1024]{2,1,0:T(8,128)(2,1)S(1)}, u32[]{:S(2)}, u32[]{:S(2)}) collective-permute-start(bf16[2,256,1024]{2,1,0:T(8,128)(2,1)S(1)} %get-tuple-element.48), channel_id=1, source_target_pairs={{0,1},{1,0},{2,3},{3,2},{4,5},{5,4},{6,7},{7,6},{8,9},{9,8},{10,11... | collective-permute-start | bytes 3145736 | tf_op jit(solution)/shard_map/ppermute | solution.py:190
  228.8 125.4 %collective-permute-start.56 = (bf16[2,256,1024]{2,1,0:T(8,128)(2,1)S(1)}, bf16[2,256,1024]{2,1,0:T(8,128)(2,1)S(1)}, u32[]{:S(2)}, u32[]{:S(2)}) collective-permute-start(bf16[2,256,1024]{2,1,0:T(8,128)(2,1)S(1)} %get-tuple-element.49), channel_id=1, source_target_pairs={{1,2},{3,4},{5,6},{7,8},{9,10},{11,12},{13,14},{2,1},{4,3},{6,5},{... | collective-permute-start | bytes 3145736 | tf_op jit(solution)/shard_map/ppermute | solution.py:199
  254.2 28.3 %collective-permute-start.46 = (bf16[256,1024]{1,0:T(8,128)(2,1)S(1)}, bf16[256,1024]{1,0:T(8,128)(2,1)S(1)}, u32[]{:S(2)}, u32[]{:S(2)}) collective-permute-start(bf16[256,1024]{1,0:T(8,128)(2,1)S(1)} %get-tuple-element.46), channel_id=1, source_target_pairs={{0,1},{1,0},{2,3},{3,2},{4,5},{5,4},{6,7},{7,6},{8,9},{9,8},{10,11... | collective-permute-start | bytes 1572872 | tf_op jit(solution)/shard_map/ppermute | solution.py:190
  303.8 50.6 %collective-permute-start.44 = (bf16[2,256,1024]{2,1,0:T(8,128)(2,1)S(1)}, bf16[2,256,1024]{2,1,0:T(8,128)(2,1)S(1)}, u32[]{:S(2)}, u32[]{:S(2)}) collective-permute-start(bf16[2,256,1024]{2,1,0:T(8,128)(2,1)S(1)} %get-tuple-element.43), channel_id=1, source_target_pairs={{0,1},{1,0},{2,3},{3,2},{4,5},{5,4},{6,7},{7,6},{8,9},{9,8},{10,11... | collective-permute-start | bytes 3145736 | tf_op jit(solution)/shard_map/ppermute | solution.py:190
  344.1 18.8 %collective-permute-start.45 = (bf16[2,256,1024]{2,1,0:T(8,128)(2,1)S(1)}, bf16[2,256,1024]{2,1,0:T(8,128)(2,1)S(1)}, u32[]{:S(2)}, u32[]{:S(2)}) collective-permute-start(bf16[2,256,1024]{2,1,0:T(8,128)(2,1)S(1)} %get-tuple-element.44), channel_id=1, source_target_pairs={{1,2},{3,4},{5,6},{7,8},{9,10},{11,12},{13,14},{2,1},{4,3},{6,5},{... | collective-permute-start | bytes 3145736 | tf_op jit(solution)/shard_map/ppermute | solution.py:199
  350.5 16.6 %collective-permute-start.33 = (bf16[2,256,1024]{2,1,0:T(8,128)(2,1)S(1)}, bf16[2,256,1024]{2,1,0:T(8,128)(2,1)S(1)}, u32[]{:S(2)}, u32[]{:S(2)}) collective-permute-start(bf16[2,256,1024]{2,1,0:T(8,128)(2,1)S(1)} %get-tuple-element.38), channel_id=1, source_target_pairs={{0,1},{1,0},{2,3},{3,2},{4,5},{5,4},{6,7},{7,6},{8,9},{9,8},{10,11... | collective-permute-start | bytes 3145736 | tf_op jit(solution)/shard_map/ppermute | solution.py:190
  352.0 22.1 %collective-permute-start.34 = (bf16[2,256,1024]{2,1,0:T(8,128)(2,1)S(1)}, bf16[2,256,1024]{2,1,0:T(8,128)(2,1)S(1)}, u32[]{:S(2)}, u32[]{:S(2)}) collective-permute-start(bf16[2,256,1024]{2,1,0:T(8,128)(2,1)S(1)} %get-tuple-element.39), channel_id=1, source_target_pairs={{1,2},{3,4},{5,6},{7,8},{9,10},{11,12},{13,14},{2,1},{4,3},{6,5},{... | collective-permute-start | bytes 3145736 | tf_op jit(solution)/shard_map/ppermute | solution.py:199
  356.2 17.9 %collective-permute-start.43 = (bf16[4,64,1024]{2,1,0:T(8,128)(2,1)S(1)}, bf16[4,64,1024]{2,1,0:T(8,128)(2,1)S(1)}, u32[]{:S(2)}, u32[]{:S(2)}) collective-permute-start(bf16[4,64,1024]{2,1,0:T(8,128)(2,1)S(1)} %pad_maximum_fusion.6.mine_ref), channel_id=1, source_target_pairs={{0,1},{1,0},{2,3},{3,2},{4,5},{5,4},{6,7},{7,6},{8,9},{9,8},{10,11... | collective-permute-start | bytes 1572872 | tf_op jit(solution)/shard_map/ppermute | solution.py:190
  (80 other events, 781.6 us)
Sparse Core Ops, SparseCore 0:
  9.8 44.9 all-gather.7
  56.4 54.4 all-gather.5
  112.5 43.4 all-gather.3

commit v2 on v1

v2 whole, which is shorter than its diff:
```python
import functools
import math

import jax
import jax.numpy as jnp
from jax import lax
from jax.experimental import pallas as pl
from jax.experimental.pallas import tpu as pltpu
from jax.sharding import Mesh, PartitionSpec as P

HEADS = 24
HD = 128
BLK = 256
D = 3072
HALF = D // 2
PART = BLK // 4
ROWS = D // 8
PAIR = 2
SCALE = 1.0 / math.sqrt(HD)
LOG2E = 1.4426950408889634
DP = ("x_lo", "z")
SKY = ("x_hi", "y", "core")
CHUNK = 12
ACROSS = (((1,), (1,)), ((), ()))
F32 = jnp.float32
BF16 = jnp.bfloat16
VMEM = 60 * 2**20


ANY = pl.BlockSpec(memory_space=pl.ANY)


def project_kernel(mine_ref, theirs_ref, piece_ref, *rest):
    own_ref, send_ref = rest[-2:]
    piece = piece_ref[...]
    own_ref[...] = lax.dot_general(mine_ref[...], piece, ACROSS, preferred_element_type=F32)
    send_ref[...] = lax.dot_general(theirs_ref[...], piece, ACROSS, preferred_element_type=F32).astype(BF16)


def project(mine, theirs, places, w, after):
    width = w.shape[0]
    first = pl.BlockSpec((None, BLK, HALF), lambda p: (places[0], 0, 0))
    second = pl.BlockSpec((None, BLK, HALF), lambda p: (places[1], 0, 0))
    out = pl.BlockSpec((BLK, ROWS), lambda p: (0, p))
    return pl.pallas_call(
        project_kernel,
        grid=(width // ROWS,),
        in_specs=[first, second, pl.BlockSpec((ROWS, HALF), lambda p: (p, 0))] + [ANY] * len(after),
        out_specs=[out, out],
        out_shape=[jax.ShapeDtypeStruct((BLK, width), F32), jax.ShapeDtypeStruct((BLK, width), BF16)],
        compiler_params=pltpu.CompilerParams(vmem_limit_bytes=VMEM),
        cost_estimate=pl.CostEstimate(
            flops=4 * BLK * width * HALF, bytes_accessed=width * HALF * 2 + BLK * width * 6, transcendentals=0
        ),
        name="project",
    )(mine, theirs, w, *after)


def one_head(info, q, keys, values, ga):
    ga_r = ga.astype(F32).T
    ga_t = ga_r.astype(BF16)
    raw = [lax.dot_general(k, q, ACROSS, preferred_element_type=F32) for k in keys]
    yield
    grad_weights = [jnp.dot(v, ga_t, preferred_element_type=F32) for v in values]
    scores = []
    for j in range(4):
        s = raw[j] * (SCALE * LOG2E)
        if j > 0:
            s = s + jnp.where(info[j - 1] > 0, 0.0, -jnp.inf).astype(F32)
        scores.append(s)
    top = functools.reduce(jnp.maximum, [jnp.max(s, axis=0, keepdims=True) for s in scores])
    exps = [jnp.exp2(s - top) for s in scores]
    total = functools.reduce(jnp.add, [jnp.sum(e, axis=0, keepdims=True) for e in exps])
    inverse = 1.0 / total
    weights = [e * inverse for e in exps]
    weights_b = [p.astype(BF16) for p in weights]
    yield
    att_t = jnp.zeros((HD, BLK), F32)
    for j in range(4):
        att_t += jnp.dot(values[j].T, weights_b[j], preferred_element_type=F32)
    att_r = att_t.astype(BF16).astype(F32)
    attended = att_r.T.astype(BF16)
    delta = jnp.sum(ga_r * att_r, axis=0, keepdims=True)
    value_terms = [jnp.dot(p, ga, preferred_element_type=F32).astype(BF16) for p in weights_b]
    yield
    gq_t = jnp.zeros((HD, BLK), F32)
    key_terms = []
    for j in range(4):
        gs = (weights[j] * (grad_weights[j] - delta)).astype(BF16)
        gq_t += jnp.dot(keys[j].T, gs, preferred_element_type=F32)
        key_terms.append((jnp.dot(gs, q, preferred_element_type=F32) * SCALE).astype(BF16))
    yield attended, (gq_t * SCALE).T.astype(BF16), key_terms, value_terms


def attention_kernel(
    terms, rolled, info, q_ref, ko_ref, vo_ref, inner_ref, outer_ref, held_ref, theirs_ref, *rest
):
    ga_refs = rest[:terms]
    att_ref, gq_ref, own_ref, tin_ref, tout_ref, keep_ref, send_ref = rest[-7:]
    core, y = info[3], info[5]
    heads = []
    for a in range(PAIR):
        c = slice(a * HD, (a + 1) * HD)
        ga = functools.reduce(jnp.add, [ref[:, c].astype(F32) for ref in ga_refs]).astype(BF16)
        held, theirs = held_ref[:, c], theirs_ref[:, c]
        keys = [ko_ref[:, c], inner_ref[0, :, c], outer_ref[0, :, c], jnp.where(core == 0, held, theirs)]
        values = [vo_ref[:, c], inner_ref[1, :, c], outer_ref[1, :, c], jnp.where(core == 0, theirs, held)]
        heads.append(one_head(info, q_ref[:, c], keys, values, ga))
    for _ in range(3):
        for h in heads:
            next(h)
    for a in range(PAIR):
        c = slice(a * HD, (a + 1) * HD)
        attended, grad_query, key_terms, value_terms = next(heads[a])
        att_ref[:, c] = attended
        gq_ref[:, c] = grad_query
        for ref, j in ((own_ref, 0), (tin_ref, 1), (tout_ref, 2)):
            ref[0, :, c] = key_terms[j]
            ref[1, :, c] = value_terms[j]
        keep = jnp.where(core == 0, key_terms[3], value_terms[3])
        send = jnp.where(core == 0, value_terms[3], key_terms[3])
        for r in range(4):
            place = pl.multiple_of(lax.rem(y + r, 4) * PART, PART) if rolled else r * PART
            keep_ref[pl.ds(place, PART), c] = keep[r * PART : (r + 1) * PART]
            send_ref[pl.ds(place, PART), c] = send[r * PART : (r + 1) * PART]


def attention(part, begin, count, info, rows, ga, prior, after):
    wide = PAIR * HD
    whole = CHUNK // PAIR
    steps = count // PAIR
    first = begin // PAIR

    def head(t, info):
        return (0, info[6 + part] * whole + first + t)

    def heads(t, info):
        return (0, 0, info[6 + part] * whole + first + t)

    def col(t, *_):
        return (0, first + t)

    def pair(t, *_):
        return (0, 0, first + t)

    one = (BLK, wide)
    two = (2, BLK, wide)
    in_specs = (
        [pl.BlockSpec(one, head)] * 3
        + [pl.BlockSpec(two, heads)] * 2
        + [pl.BlockSpec(one, head)] * 2
        + [pl.BlockSpec(one, col)] * len(ga)
        + [ANY] * (len(prior) + len(after))
    )
    out_specs = (
        [pl.BlockSpec(one, head)] * 2 + [pl.BlockSpec(two, pair)] * 3 + [pl.BlockSpec(one, col)] * 2
    )
    full = jax.ShapeDtypeStruct((BLK, D), BF16)
    stacked = jax.ShapeDtypeStruct((2, BLK, CHUNK * HD), BF16)
    single = jax.ShapeDtypeStruct((BLK, CHUNK * HD), BF16)
    return pl.pallas_call(
        functools.partial(attention_kernel, len(ga), part == 0),
        grid_spec=pltpu.PrefetchScalarGridSpec(
            num_scalar_prefetch=1, grid=(steps,), in_specs=in_specs, out_specs=out_specs
        ),
        out_shape=[full, full, stacked, stacked, stacked, single, single],
        input_output_aliases={8 + len(ga) + i: i for i in range(len(prior))},
        compiler_params=pltpu.CompilerParams(vmem_limit_bytes=VMEM),
        cost_estimate=pl.CostEstimate(
            flops=count * 12 * BLK * 4 * BLK * HD,
            bytes_accessed=count * BLK * HD * 2 * 21,
            transcendentals=count * BLK * 4 * BLK,
        ),
        name="attention",
    )(info, *rows, *ga, *prior, *after)


def combine_kernel(info, own_ref, rin_ref, rout_ref, mine_ref, theirs_ref, *rest):
    gk_ref, gv_ref, total = rest[-3:]
    core, hit, y = info[3], info[4], info[5]
    total[...] = own_ref[...].astype(F32) + rin_ref[...].astype(F32) + rout_ref[...].astype(F32)

    @pl.when(hit > 0)
    def _():
        for r in range(4):
            place = pl.multiple_of(lax.rem(y + r, 4) * PART, PART)
            mine = mine_ref[r * PART : (r + 1) * PART].astype(F32)
            theirs = theirs_ref[r * PART : (r + 1) * PART].astype(F32)
            total[0, pl.ds(place, PART)] += jnp.where(core == 0, mine, theirs)
            total[1, pl.ds(place, PART)] += jnp.where(core == 0, theirs, mine)

    gk_ref[...] = total[0].astype(BF16)
    gv_ref[...] = total[1].astype(BF16)


def combine(part, info, own, rin, rout, sums, prior):
    wide = 4 * HD
    steps = CHUNK * HD // wide

    def head(t, info):
        return (0, info[6 + part] * steps + t)

    def col(t, *_):
        return (0, part * steps + t)

    def pair(t, *_):
        return (0, 0, t)

    two = pl.BlockSpec((2, BLK, wide), pair)
    one = pl.BlockSpec((BLK, wide), col)
    full = jax.ShapeDtypeStruct((BLK, D), BF16)
    return pl.pallas_call(
        combine_kernel,
        grid_spec=pltpu.PrefetchScalarGridSpec(
            num_scalar_prefetch=1,
            grid=(steps,),
            in_specs=[two, two, two, one, one] + [ANY] * len(prior),
            out_specs=[pl.BlockSpec((BLK, wide), head)] * 2,
            scratch_shapes=[pltpu.VMEM((2, BLK, wide), F32)],
        ),
        out_shape=[full, full],
        input_output_aliases={6: 0, 7: 1} if prior else {},
        compiler_params=pltpu.CompilerParams(vmem_limit_bytes=VMEM),
        cost_estimate=pl.CostEstimate(
            flops=CHUNK * BLK * HD * 8, bytes_accessed=CHUNK * BLK * HD * 2 * 10, transcendentals=0
        ),
        name="combine",
    )(info, own, rin, rout, *sums, *prior)


def add_kernel(a_ref, b_ref, *rest):
    rest[-1][...] = (a_ref[...].astype(F32) + b_ref[...].astype(F32)).astype(BF16)


def add(a, b, after=()):
    width = a.shape[1] // 2
    spec = pl.BlockSpec((a.shape[0], width), lambda t: (0, t))
    return pl.pallas_call(
        add_kernel,
        grid=(2,),
        in_specs=[spec, spec] + [ANY] * len(after),
        out_specs=spec,
        out_shape=jax.ShapeDtypeStruct(a.shape, BF16),
        compiler_params=pltpu.CompilerParams(vmem_limit_bytes=VMEM),
        cost_estimate=pl.CostEstimate(flops=a.size, bytes_accessed=a.size * 6, transcendentals=0),
        name="add",
    )(a, b, *after)


def gather_kernel(first_ref, *refs):
    total = functools.reduce(jnp.add, [ref[...].astype(F32) for ref in refs[:4]])
    width = first_ref.shape[1]
    refs[-1][:, :width] = first_ref[...]
    refs[-1][:, width:] = total.astype(BF16)


def gather(first, both, after):
    pieces = [both[:PART]] + [move(both[r * PART : (r + 1) * PART], "y", r, 4) for r in range(1, 4)]
    whole = pl.BlockSpec(memory_space=pltpu.VMEM)
    return pl.pallas_call(
        gather_kernel,
        in_specs=[whole] * 5 + [ANY] * len(after),
        out_specs=whole,
        out_shape=jax.ShapeDtypeStruct((PART, D), BF16),
        compiler_params=pltpu.CompilerParams(vmem_limit_bytes=VMEM),
        cost_estimate=pl.CostEstimate(
            flops=pieces[0].size * 4, bytes_accessed=pieces[0].size * 14, transcendentals=0
        ),
        name="gather",
    )(first, *pieces, *after)


def hold_kernel(*refs):
    del refs


def hold(x, after):
    return pl.pallas_call(
        hold_kernel,
        in_specs=[ANY] * (1 + len(after)),
        out_specs=ANY,
        out_shape=jax.ShapeDtypeStruct(x.shape, x.dtype),
        input_output_aliases={0: 0},
        cost_estimate=pl.CostEstimate(flops=0, bytes_accessed=0, transcendentals=0),
        name="hold",
    )(x, *after)


def pack_kernel(info, k_ref, v_ref, inner_ref, *outs):
    outs = outs[-4:]
    y, which = info[5], info[8]
    for r in range(4):
        rows = pl.ds(pl.multiple_of(lax.rem(y + r, 4) * PART, PART), PART)
        for i in range(4):

            @pl.when(which == i)
            def _():
                outs[r][...] = (k_ref, v_ref, inner_ref.at[0], inner_ref.at[1])[i][rows]


def pack(info, k, v, inner, after):
    def col(t, *_):
        return (0, t)

    wide = D // 2
    return pl.pallas_call(
        pack_kernel,
        grid_spec=pltpu.PrefetchScalarGridSpec(
            num_scalar_prefetch=1,
            grid=(2,),
            in_specs=[pl.BlockSpec((BLK, wide), col)] * 2
            + [pl.BlockSpec((2, BLK, wide), lambda t, *_: (0, 0, t))]
            + [ANY] * len(after),
            out_specs=[pl.BlockSpec((PART, wide), col)] * 4,
        ),
        out_shape=[jax.ShapeDtypeStruct((PART, D), BF16)] * 4,
        compiler_params=pltpu.CompilerParams(vmem_limit_bytes=VMEM),
        cost_estimate=pl.CostEstimate(flops=0, bytes_accessed=BLK * D * 10, transcendentals=0),
        name="pack",
    )(info, k, v, inner, *after)


def pick(which, pieces, after=()):
    count = len(pieces)

    def kernel(which, *refs):
        for i in range(count):

            @pl.when(which[0] == i)
            def _():
                refs[-1][...] = refs[i][...]

    spec = pl.BlockSpec(pieces[0].shape, lambda t, *_: (0, 0))
    return pl.pallas_call(
        kernel,
        grid_spec=pltpu.PrefetchScalarGridSpec(
            num_scalar_prefetch=1, grid=(1,), in_specs=[spec] * count + [ANY] * len(after), out_specs=spec
        ),
        out_shape=jax.ShapeDtypeStruct(pieces[0].shape, BF16),
        compiler_params=pltpu.CompilerParams(vmem_limit_bytes=VMEM),
        cost_estimate=pl.CostEstimate(flops=0, bytes_accessed=pieces[0].size * 10, transcendentals=0),
        name="pick",
    )(which[None].astype(jnp.int32), *pieces, *after)


def move(x, axis, step, size):
    return lax.ppermute(x, axis, [(i, (i + step) % size) for i in range(size)])


def swap_core(x):
    return move(x, "core", 1, 2)


def swap_outer(x):
    route = [(i, i + 1) for i in range(1, 15, 2)] + [(i + 1, i) for i in range(1, 15, 2)]
    return lax.ppermute(x, SKY, route)


def join_kernel(*refs):
    for r in range(4):
        refs[-1][r * PART : (r + 1) * PART] = refs[r][...]


def join(parts, after):
    wide = D // 2
    return pl.pallas_call(
        join_kernel,
        grid=(2,),
        in_specs=[pl.BlockSpec((PART, wide), lambda t: (0, t))] * 4 + [ANY] * len(after),
        out_specs=pl.BlockSpec((BLK, wide), lambda t: (0, t)),
        out_shape=jax.ShapeDtypeStruct((BLK, D), BF16),
        compiler_params=pltpu.CompilerParams(vmem_limit_bytes=VMEM),
        cost_estimate=pl.CostEstimate(flops=0, bytes_accessed=BLK * D * 4, transcendentals=0),
        name="join",
    )(*parts, *after)


def local(queries, key_states, value_states, key_blocks, global_block, w_out, grad_out):
    x, y, core = lax.axis_index("x_hi"), lax.axis_index("y"), lax.axis_index("core")
    side = lax.axis_index("x_lo")
    row = (x * 4 + y) * 2 + core
    root = global_block[0]
    ids = lax.dynamic_slice_in_dim(key_blocks, row, 1, 0)[0]
    above, below = ids[0], ids[1]
    inner_id = jnp.where(core == 0, below, above)
    outer_id = jnp.where(core == 0, above, below)
    live = (root != row) & (root != above) & (root != below)
    which = jnp.where(root % 2 == core, core, core + 2)
    info = jnp.stack(
        [inner_id >= 0, outer_id >= 0, live, core, root == row, y, side, 1 - side, which]
    ).astype(jnp.int32)
    q, k, v, go = queries[0], key_states[0], value_states[0], grad_out[0]
    w = lax.dynamic_slice_in_dim(w_out, core * HALF, HALF, 1)
    near = lax.all_gather(w, "z", axis=0, tiled=True)
    far = move(w, "x_lo", 1, 2)
    go_mine = lax.dynamic_slice_in_dim(go, core * HALF, HALF, 1)
    go_core = swap_core(lax.dynamic_slice_in_dim(go, (1 - core) * HALF, HALF, 1))
    kv = jnp.stack([k, v])
    inner = swap_core(kv)
    outer = swap_outer(kv)

    root_y, root_x = (root // 2) % 4, root // 8
    pieces = pack(info, k, v, inner, (go_core,))
    arrived = [pieces[0]] + [move(pieces[r], "y", r, 4) for r in range(1, 4)]
    mine = pick((y - root_y) % 4, arrived, (outer,))
    far = lax.all_gather(hold(far, (mine,)), "z", axis=0, tiled=True)
    ga_own, ga_core = project(go_mine[None], go_core[None], (0, 0), near, (arrived[1],))
    other = move(mine, "x_hi", 1, 2)
    quarter = pick((root_x - x) % 2, (mine, other), (ga_own,))
    held = join([quarter] + [move(quarter, "y", -r, 4) for r in range(1, 4)], ())
    rows = (q, k, v, inner, outer, held, swap_core(held))
    ga_near = (ga_own, swap_core(ga_core))

    out = attention(0, 0, CHUNK, info, rows, ga_near, (), ())
    att, gq, own0, tin0, tout0, keep, send = out
    ga_own, ga_core = project(go_mine[None], go_core[None], (0, 0), far, (held,))
    ga_far = (ga_own, swap_core(ga_core))
    rin0, rout0 = swap_core(tin0), swap_outer(tout0)
    both0 = add(keep, swap_core(send))
    quarter0 = lax.psum_scatter(both0, "y", scatter_dimension=0, tiled=True)

    out = attention(1, 0, CHUNK, info, rows, ga_far, (att, gq), (both0,))
    att, gq, own1, tin1, tout1, keep, send = out
    rin1, rout1 = swap_core(tin1), swap_outer(tout1)
    both1 = add(keep, swap_core(send), (rin0, rout0))
    quarters = gather(quarter0, both1, (rin1, rout1))
    halves = add(quarters, move(quarters, "x_hi", 1, 2))
    sums = join([halves] + [move(halves, "y", -r, 4) for r in range(1, 4)], ())
    sums = (sums, swap_core(sums))
    grads = combine(0, info, own0, rin0, rout0, sums, ())
    gk, gv = combine(1, info, own1, rin1, rout1, sums, grads)
    return tuple(a[None] for a in (att, gq, gk, gv))


def solution(mesh):
    inside = Mesh(mesh.devices.reshape(2, 4, 2, 4, 2), DP + SKY)
    rows = P(DP, SKY, None)
    return jax.shard_map(
        local,
        mesh=inside,
        in_specs=(rows, rows, rows, P(), P(), P(DP, None), rows),
        out_specs=(rows, rows, rows, rows),
        check_vma=False,
    )
```

time: 391 us -> 282 us (0.72); the launches traced: 385 us -> 281 us
  starting transfers between devices: 110 us -> 43.9 us
  other arithmetic: 26.9 us -> 0 us
  waiting for transfers between devices: 117 us -> 112 us
  local copies, waits for them, and re-layouts: 30.5 us -> 26 us
    all_gather x3 -> x2, waiting for transfers between devices: 62 us -> 0.01 us  [the longest x1 0.01 us: local(): near = lax.all_gather(w, 'z', axis=0, tiled=True)]
    ppermute x60 -> x25, starting transfers between devices: 89.8 us -> 34.9 us  [move(): return lax.ppermute(x, axis, [(i, (i + step) % size) for i in range(size)])]
    ppermute x60 -> x25, waiting for transfers between devices: 44.6 us -> 73.2 us  [move(): return lax.ppermute(x, axis, [(i, (i + step) % size) for i in range(size)])]
    ppermute x6 -> x3, waiting for transfers between devices: 9.35 us -> 26.3 us  [swap_outer(): return lax.ppermute(x, SKY, route)]
    select_n x15 -> x0, other arithmetic: 14.2 us -> none  [the longest x3 4.42 us: spread_global(): source = jnp.where(root_core == core, kv, inner)]
    reduce_scatter x0 -> x1, waiting for transfers between devices: none -> 12.5 us  [local(): quarter0 = lax.psum_scatter(both0, 'y', scatter_dimension=0, tiled=True)]
    ppermute x6 -> x3, starting transfers between devices: 20.4 us -> 8.88 us  [swap_outer(): return lax.ppermute(x, SKY, route)]
    another operation x7 -> x2, local copies, waits for them, and re-layouts: 12.5 us -> 2.04 us  [the longest x1 1.36 us: local(): kv = jnp.stack([k, v])]
  transfers between devices with their start and end apart: 69 -> 31, of which waited for: 27 -> 18; matrix products, arithmetic and copies ran while one was open for 13% -> 4% of each run, Pallas kernels for 20% -> 22%
where the time goes in v2:
time: 282 us; the launch traced here: 281 us
  waiting for transfers between devices  112 us (40%)
  Pallas kernels  80.3 us (28%)
  starting transfers between devices  43.9 us (16%)
  local copies, waits for them, and re-layouts  26 us (9%)
  between operations  18.3 us (6%)
    ppermute x25, waiting for transfers between devices, move(): return lax.ppermute(x, axis, [(i, (i + step) % size) for i in range(size)])  73.2 us
    ppermute x25, starting transfers between devices, move(): return lax.ppermute(x, axis, [(i, (i + step) % size) for i in range(size)])  34.9 us
    pallas_call x2, Pallas kernels, attention(): pl.pallas_call(functools.partial(attention_kernel, len(ga), part == 0), g...  33.8 us
    ppermute x3, waiting for transfers between devices, swap_outer(): return lax.ppermute(x, SKY, route)  26.3 us
    unnamed x61, local copies, waits for them, and re-layouts  17.6 us
    pallas_call x2, Pallas kernels, project(): pl.pallas_call(project_kernel, grid=(width // ROWS,), in_specs=[first, se...  13.6 us
    reduce_scatter x1, waiting for transfers between devices, local(): quarter0 = lax.psum_scatter(both0, 'y', scatter_dimension=0, tiled=True)  12.5 us
    pallas_call x2, Pallas kernels, combine(): pl.pallas_call(combine_kernel, grid_spec=pltpu.PrefetchScalarGridSpec(num...  10.9 us
  transfers between devices with their start and end apart: 31, of which 18 were waited for; matrix products, arithmetic and copies ran while one was open for 4% of the time, Pallas kernels for 22%

profile of v2, /device:TPU:1, one launch (start us, length us, event | category | flops | bytes accessed | tf_op | source)
XLA Modules:
  0.0 280.5 jit_solution(17910514201092598748)
XLA Ops:
  29.2 4.5 %pack.1 = (bf16[64,3072]{1,0:T(8,128)(2,1)}, bf16[64,3072]{1,0:T(8,128)(2,1)}, bf16[64,3072]{1,0:T(8,128)(2,1)}, bf16[64,3072]{1,0:T(8,128)(2,1)}) custom-call(s32[9]{0:T(128)} %stack.58.info, bf16[256,3072]{1,0:T(8,128)(2,1)} %bitcast.32, bf16[256,3072]{1,0:T(8,128)(2,1)} %bitcast.35, bf16[2,256,3072]{2,1,0:T(8,128)(2,1)} %collective-permute-done.inner_ref, ...), custom_call_target="tpu_custom_call" | custom-call | bytes 7864320 | tf_op jit(solution)/shard_map/pack/pallas_call | solution.py:306
  38.4 24.8 %collective-permute-done.1.refs_4_.outer_ref = bf16[2,256,3072]{2,1,0:T(8,128)(2,1)} collective-permute-done((bf16[2,256,3072]{2,1,0:T(8,128)(2,1)}, bf16[2,256,3072]{2,1,0:T(8,128)(2,1)}, u32[]{:S(2)}, u32[]{:S(2)}) %collective-permute-start.1) | collective-permute-done | bytes 3145760 | tf_op jit(solution)/shard_map/ppermute | solution.py:356
  65.9 7.2 %collective-permute-done.4.refs_2_ = bf16[64,3072]{1,0:T(8,128)(2,1)S(1)} collective-permute-done((bf16[64,3072]{1,0:T(8,128)(2,1)}, bf16[64,3072]{1,0:T(8,128)(2,1)S(1)}, u32[]{:S(2)}, u32[]{:S(2)}) %collective-permute-start.4) | collective-permute-done | bytes 393248 | tf_op jit(solution)/shard_map/ppermute | solution.py:347
  73.1 6.2 %collective-permute-done.5.refs_3_ = bf16[64,3072]{1,0:T(8,128)(2,1)S(1)} collective-permute-done((bf16[64,3072]{1,0:T(8,128)(2,1)}, bf16[64,3072]{1,0:T(8,128)(2,1)S(1)}, u32[]{:S(2)}, u32[]{:S(2)}) %collective-permute-start.5) | collective-permute-done | bytes 393248 | tf_op jit(solution)/shard_map/ppermute | solution.py:347
  83.4 4.2 %collective-permute-start.6 = (bf16[64,3072]{1,0:T(8,128)(2,1)S(1)}, bf16[64,3072]{1,0:T(8,128)(2,1)S(1)}, u32[]{:S(2)}, u32[]{:S(2)}) collective-permute-start(bf16[64,3072]{1,0:T(8,128)(2,1)S(1)} %copy-done.7), channel_id=1, source_target_pairs={{0,8},{8,0},{1,9},{9,1},{2,10},{10,2},{3,11},{11,3},{4,12},{12,4},... | collective-permute-start | bytes 1179656 | tf_op jit(solution)/shard_map/ppermute | solution.py:347
  87.6 6.8 %project.2 = (f32[256,1536]{1,0:T(8,128)}, bf16[256,1536]{1,0:T(8,128)(2,1)}) custom-call(bf16[1,256,1536]{2,1,0:T(8,128)(2,1)} %get-tuple-element.56.mine_ref, bf16[1,256,1536]{2,1,0:T(8,128)(2,1)} %bitcast.44, bf16[1536,1536]{1,0:T(8,128)(2,1)} %all-gather.3.cloned.1.call-done.piece_ref, bf16[64,3072]{1,0:T(8,128)(2,1)} %copy-done.21), custom_call_target="tpu_custom_call" | custom-call | flops 2415919104 | bytes 7077888 | tf_op jit(solution)/shard_map/project/pallas_call | solution.py:45
  97.0 5.3 %collective-permute-start.8 = (bf16[64,3072]{1,0:T(8,128)(2,1)}, bf16[64,3072]{1,0:T(8,128)(2,1)S(1)}, u32[]{:S(2)}, u32[]{:S(2)}) collective-permute-start(bf16[64,3072]{1,0:T(8,128)(2,1)} %pick.3.refs_0_), channel_id=1, source_target_pairs={{0,4},{2,6},{4,0},{6,2},{1,5},{3,7},{5,1},{7,3},{8,12},{10,14},{12... | collective-permute-start | bytes 1179656 | tf_op jit(solution)/shard_map/ppermute | solution.py:347
  102.3 5.4 %collective-permute-done.9.refs_3_ = bf16[64,3072]{1,0:T(8,128)(2,1)S(1)} collective-permute-done((bf16[64,3072]{1,0:T(8,128)(2,1)}, bf16[64,3072]{1,0:T(8,128)(2,1)S(1)}, u32[]{:S(2)}, u32[]{:S(2)}) %collective-permute-start.9) | collective-permute-done | bytes 393248 | tf_op jit(solution)/shard_map/ppermute | solution.py:347
  107.7 11.0 %collective-permute-done.8.refs_2_ = bf16[64,3072]{1,0:T(8,128)(2,1)S(1)} collective-permute-done((bf16[64,3072]{1,0:T(8,128)(2,1)}, bf16[64,3072]{1,0:T(8,128)(2,1)S(1)}, u32[]{:S(2)}, u32[]{:S(2)}) %collective-permute-start.8) | collective-permute-done | bytes 393248 | tf_op jit(solution)/shard_map/ppermute | solution.py:347
  125.0 3.9 %collective-permute-done.13.rest_1_ = bf16[256,1536]{1,0:T(8,128)(2,1)S(1)} collective-permute-done((bf16[256,1536]{1,0:T(8,128)(2,1)S(1)}, bf16[256,1536]{1,0:T(8,128)(2,1)S(1)}, u32[]{:S(2)}, u32[]{:S(2)}) %collective-permute-start.13) | collective-permute-done | bytes 786464 | tf_op jit(solution)/shard_map/ppermute | solution.py:347
  130.5 16.9 %attention.2 = (bf16[256,3072]{1,0:T(8,128)(2,1)}, bf16[256,3072]{1,0:T(8,128)(2,1)}, bf16[2,256,1536]{2,1,0:T(8,128)(2,1)}, bf16[2,256,1536]{2,1,0:T(8,128)(2,1...) custom-call(s32[9]{0:T(128)} %stack.58.info, bf16[256,3072]{1,0:T(8,128)(2,1)} %bitcast.38, ...), custom_call_target="tpu_custom_call" | custom-call | flops 4831838208 | bytes 16515072 | tf_op jit(solution)/shard_map/attention/pallas_call | solution.py:161
  147.9 6.8 %project.3 = (f32[256,1536]{1,0:T(8,128)}, bf16[256,1536]{1,0:T(8,128)(2,1)}) custom-call(bf16[1,256,1536]{2,1,0:T(8,128)(2,1)} %get-tuple-element.56.mine_ref, bf16[1,256,1536]{2,1,0:T(8,128)(2,1)} %bitcast.45, bf16[1536,1536]{1,0:T(8,128)(2,1)} %all-gather.5.cloned.1.call-done.piece_ref, bf16[256,3072]{1,0:T(8,128)(2,1)} %join.2.rest_0_.held_ref), custom_call_target="tpu_custom_call" | custom-call | flops 2415919104 | bytes 7077888 | tf_op jit(solution)/shard_map/project/pallas_call | solution.py:45
  161.3 16.9 %attention.3 = (bf16[256,3072]{1,0:T(8,128)(2,1)}, bf16[256,3072]{1,0:T(8,128)(2,1)}, bf16[2,256,1536]{2,1,0:T(8,128)(2,1)}, bf16[2,256,1536]{2,1,0:T(8,128)(2,1...) custom-call(s32[9]{0:T(128)} %stack.58.info, ...), custom_call_target="tpu_custom_call", output_to_operand_aliasing={{0}: (10, {}), {1}: (11, {})} | custom-call | flops 4831838208 | bytes 16515072 | tf_op jit(solution)/shard_map/attention/pallas_call | solution.py:161
  178.3 3.6 %collective-permute-start.16 = (bf16[2,256,1536]{2,1,0:T(8,128)(2,1)}, bf16[2,256,1536]{2,1,0:T(8,128)(2,1)}, u32[]{:S(2)}, u32[]{:S(2)}) collective-permute-start(bf16[2,256,1536]{2,1,0:T(8,128)(2,1)} %get-tuple-element.46), channel_id=1, source_target_pairs={{1,2},{3,4},{5,6},{7,8},{9,10},{11,12},{13,14},{2,1},{4,3},{6,5},{... | collective-permute-start | bytes 4718600 | tf_op jit(solution)/shard_map/ppermute | solution.py:356
  189.6 4.7 %collective-permute-start.22 = (bf16[64,1536]{1,0:T(8,128)(2,1)S(1)}, bf16[64,1536]{1,0:T(8,128)(2,1)S(1)}, u32[]{:S(2)}, u32[]{:S(2)}) collective-permute-start(bf16[64,1536]{1,0:T(8,128)(2,1)S(1)} %get-tuple-element.58), channel_id=1, source_target_pairs={{0,6},{2,0},{4,2},{6,4},{1,7},{3,1},{5,3},{7,5},{8,14},{10,8},{12,... | collective-permute-start | bytes 589832 | tf_op jit(solution)/shard_map/ppermute | solution.py:347
  194.9 12.5 %reduce-scatter.2.cloned.1.call-done.first_ref = bf16[64,1536]{1,0:T(8,128)(2,1)} async-done(((bf16[256,1536]{1,0:T(8,128)(2,1)}), bf16[64,1536]{1,0:T(8,128)(2,1)}) %reduce-scatter.2.cloned.1.call-update) | async-done | bytes 196624 | tf_op jit(solution)/shard_map/reduce_scatter | solution.py:420
  207.3 5.9 %collective-permute-done.22.refs_3_ = bf16[64,1536]{1,0:T(8,128)(2,1)S(1)} collective-permute-done((bf16[64,1536]{1,0:T(8,128)(2,1)S(1)}, bf16[64,1536]{1,0:T(8,128)(2,1)S(1)}, u32[]{:S(2)}, u32[]{:S(2)}) %collective-permute-start.22) | collective-permute-done | bytes 196640 | tf_op jit(solution)/shard_map/ppermute | solution.py:347
  219.3 9.4 %collective-permute-done.23.b_ref = bf16[64,3072]{1,0:T(8,128)(2,1)S(1)} collective-permute-done((bf16[64,3072]{1,0:T(8,128)(2,1)}, bf16[64,3072]{1,0:T(8,128)(2,1)S(1)}, u32[]{:S(2)}, u32[]{:S(2)}) %collective-permute-start.23) | collective-permute-done | bytes 393248 | tf_op jit(solution)/shard_map/ppermute | solution.py:347
  231.4 4.6 %collective-permute-start.25 = (bf16[64,3072]{1,0:T(8,128)(2,1)}, bf16[64,3072]{1,0:T(8,128)(2,1)S(1)}, u32[]{:S(2)}, u32[]{:S(2)}) collective-permute-start(bf16[64,3072]{1,0:T(8,128)(2,1)} %add.52.refs_0_), channel_id=1, source_target_pairs={{0,4},{2,6},{4,0},{6,2},{1,5},{3,7},{5,1},{7,3},{8,12},{10,14},{12... | collective-permute-start | bytes 1179656 | tf_op jit(solution)/shard_map/ppermute | solution.py:347
  236.0 7.2 %collective-permute-done.26.refs_3_ = bf16[64,3072]{1,0:T(8,128)(2,1)S(1)} collective-permute-done((bf16[64,3072]{1,0:T(8,128)(2,1)}, bf16[64,3072]{1,0:T(8,128)(2,1)S(1)}, u32[]{:S(2)}, u32[]{:S(2)}) %collective-permute-start.26) | collective-permute-done | bytes 393248 | tf_op jit(solution)/shard_map/ppermute | solution.py:347
  243.2 9.3 %collective-permute-done.25.refs_2_ = bf16[64,3072]{1,0:T(8,128)(2,1)S(1)} collective-permute-done((bf16[64,3072]{1,0:T(8,128)(2,1)}, bf16[64,3072]{1,0:T(8,128)(2,1)S(1)}, u32[]{:S(2)}, u32[]{:S(2)}) %collective-permute-start.25) | collective-permute-done | bytes 393248 | tf_op jit(solution)/shard_map/ppermute | solution.py:347
  258.6 3.2 %collective-permute-done.27.theirs_ref = bf16[256,3072]{1,0:T(8,128)(2,1)S(1)} collective-permute-done((bf16[256,3072]{1,0:T(8,128)(2,1)}, bf16[256,3072]{1,0:T(8,128)(2,1)S(1)}, u32[]{:S(2)}, u32[]{:S(2)}) %collective-permute-start.27) | collective-permute-done | bytes 1572896 | tf_op jit(solution)/shard_map/ppermute | solution.py:347
  263.1 5.4 %combine.2 = (bf16[256,3072]{1,0:T(8,128)(2,1)}, bf16[256,3072]{1,0:T(8,128)(2,1)}) custom-call(s32[9]{0:T(128)} %stack.58.info, bf16[2,256,1536]{2,1,0:T(8,128)(2,1)} %get-tuple-element.51.own_ref, bf16[2,256,1536]{2,1,0:T(8,128)(2,1)} %collective-permute-done.18.rest_0_.rin_ref, bf16[2,256,1536]{2,1,0:T(8,128)(2,1)} %collective-permute-done.19.rest_1_.rout_ref, ...), custom_call_target="tpu_custom_call" | custom-call | flops 3145728 | bytes 7864320 | tf_op jit(solution)/shard_map/combine/pallas_call | solution.py:212
  268.5 5.5 %combine.3 = (bf16[256,3072]{1,0:T(8,128)(2,1)}, bf16[256,3072]{1,0:T(8,128)(2,1)}) custom-call(s32[9]{0:T(128)} %stack.58.info, bf16[2,256,1536]{2,1,0:T(8,128)(2,1)} %get-tuple-element.44.own_ref, bf16[2,256,1536]{2,1,0:T(8,128)(2,1)} %copy-done.3, ...), custom_call_target="tpu_custom_call", output_to_operand_aliasing={{0}: (6, {}), {1}: (7, {})} | custom-call | flops 3145728 | bytes 7864320 | tf_op jit(solution)/shard_map/combine/pallas_call | solution.py:212
  (125 shorter events, 71.0 us)
Async XLA Ops:
  7.2 80.4 %all-gather.3.cloned.1.call-start = ((), (), s32[]{:S(2)}) async-start(), calls=%async_computation.1 | async-start | bytes 5898240 | tf_op jit(solution)/shard_map/all_gather | solution.py:394
  10.0 137.9 %all-gather.5.cloned.1.call-start = ((), (), s32[]{:S(2)}) async-start(), calls=%async_computation.2 | async-start | bytes 5898240 | tf_op jit(solution)/shard_map/all_gather | solution.py:406
  14.2 14.2 %collective-permute-start = (bf16[2,256,3072]{2,1,0:T(8,128)(2,1)}, bf16[2,256,3072]{2,1,0:T(8,128)(2,1)}, u32[]{:S(2)}, u32[]{:S(2)}) collective-permute-start(bf16[2,256,3072]{2,1,0:T(8,128)(2,1)} %constant_dynamic-update-slice_fusion), channel_id=1, source_target_pairs={{0,1},{1,0},{2,3},{3,2},{4,5},{5,4},{6,7},{7,6},{8,9},{9,8},{10,11... | collective-permute-start | bytes 9437192 | tf_op jit(solution)/shard_map/ppermute | solution.py:347
  15.6 47.6 %collective-permute-start.1 = (bf16[2,256,3072]{2,1,0:T(8,128)(2,1)}, bf16[2,256,3072]{2,1,0:T(8,128)(2,1)}, u32[]{:S(2)}, u32[]{:S(2)}) collective-permute-start(bf16[2,256,3072]{2,1,0:T(8,128)(2,1)} %constant_dynamic-update-slice_fusion), channel_id=1, source_target_pairs={{1,2},{3,4},{5,6},{7,8},{9,10},{11,12},{13,14},{2,1},{4,3},{6,5},{... | collective-permute-start | bytes 9437192 | tf_op jit(solution)/shard_map/ppermute | solution.py:356
  21.5 60.7 %collective-permute-start.11 = (bf16[384,1536]{1,0:T(8,128)(2,1)S(1)}, bf16[384,1536]{1,0:T(8,128)(2,1)S(1)}, u32[]{:S(2)}, u32[]{:S(2)}) collective-permute-start(bf16[384,1536]{1,0:T(8,128)(2,1)S(1)} %copy-done.5), channel_id=1, source_target_pairs={{0,64},{64,0},{1,65},{65,1},{2,66},{66,2},{3,67},{67,3},{4,68},{68... | collective-permute-start | bytes 3538952 | tf_op jit(solution)/shard_map/ppermute | solution.py:347
  33.7 32.2 %collective-permute-start.3 = (bf16[64,3072]{1,0:T(8,128)(2,1)}, bf16[64,3072]{1,0:T(8,128)(2,1)S(1)}, u32[]{:S(2)}, u32[]{:S(2)}) collective-permute-start(bf16[64,3072]{1,0:T(8,128)(2,1)} %get-tuple-element.31), channel_id=1, source_target_pairs={{0,2},{2,4},{4,6},{6,0},{1,3},{3,5},{5,7},{7,1},{8,10},{10,12},{12... | collective-permute-start | bytes 1179656 | tf_op jit(solution)/shard_map/ppermute | solution.py:347
  35.0 38.0 %collective-permute-start.4 = (bf16[64,3072]{1,0:T(8,128)(2,1)}, bf16[64,3072]{1,0:T(8,128)(2,1)S(1)}, u32[]{:S(2)}, u32[]{:S(2)}) collective-permute-start(bf16[64,3072]{1,0:T(8,128)(2,1)} %get-tuple-element.32), channel_id=1, source_target_pairs={{0,4},{2,6},{4,0},{6,2},{1,5},{3,7},{5,1},{7,3},{8,12},{10,14},{12... | collective-permute-start | bytes 1179656 | tf_op jit(solution)/shard_map/ppermute | solution.py:347
  37.9 41.4 %collective-permute-start.5 = (bf16[64,3072]{1,0:T(8,128)(2,1)}, bf16[64,3072]{1,0:T(8,128)(2,1)S(1)}, u32[]{:S(2)}, u32[]{:S(2)}) collective-permute-start(bf16[64,3072]{1,0:T(8,128)(2,1)} %get-tuple-element.33), channel_id=1, source_target_pairs={{0,6},{2,0},{4,2},{6,4},{1,7},{3,1},{5,3},{7,5},{8,14},{10,8},{12,... | collective-permute-start | bytes 1179656 | tf_op jit(solution)/shard_map/ppermute | solution.py:347
  83.3 124.1 %reduce-scatter.2.cloned.1.call-start = ((), (), s32[]{:S(2)}) async-start(), calls=%async_computation.3 | async-start | bytes 983040 | tf_op jit(solution)/shard_map/reduce_scatter | solution.py:420
  83.4 11.0 %collective-permute-start.6 = (bf16[64,3072]{1,0:T(8,128)(2,1)S(1)}, bf16[64,3072]{1,0:T(8,128)(2,1)S(1)}, u32[]{:S(2)}, u32[]{:S(2)}) collective-permute-start(bf16[64,3072]{1,0:T(8,128)(2,1)S(1)} %copy-done.7), channel_id=1, source_target_pairs={{0,8},{8,0},{1,9},{9,1},{2,10},{10,2},{3,11},{11,3},{4,12},{12,4},... | collective-permute-start | bytes 1179656 | tf_op jit(solution)/shard_map/ppermute | solution.py:347
  97.0 10.7 %collective-permute-start.9 = (bf16[64,3072]{1,0:T(8,128)(2,1)}, bf16[64,3072]{1,0:T(8,128)(2,1)S(1)}, u32[]{:S(2)}, u32[]{:S(2)}) collective-permute-start(bf16[64,3072]{1,0:T(8,128)(2,1)} %pick.3.refs_0_), channel_id=1, source_target_pairs={{0,2},{2,4},{4,6},{6,0},{1,3},{3,5},{5,7},{7,1},{8,10},{10,12},{12... | collective-permute-start | bytes 1179656 | tf_op jit(solution)/shard_map/ppermute | solution.py:347
  97.0 21.7 %collective-permute-start.8 = (bf16[64,3072]{1,0:T(8,128)(2,1)}, bf16[64,3072]{1,0:T(8,128)(2,1)S(1)}, u32[]{:S(2)}, u32[]{:S(2)}) collective-permute-start(bf16[64,3072]{1,0:T(8,128)(2,1)} %pick.3.refs_0_), channel_id=1, source_target_pairs={{0,4},{2,6},{4,0},{6,2},{1,5},{3,7},{5,1},{7,3},{8,12},{10,14},{12... | collective-permute-start | bytes 1179656 | tf_op jit(solution)/shard_map/ppermute | solution.py:347
  102.3 16.7 %collective-permute-start.7 = (bf16[64,3072]{1,0:T(8,128)(2,1)}, bf16[64,3072]{1,0:T(8,128)(2,1)S(1)}, u32[]{:S(2)}, u32[]{:S(2)}) collective-permute-start(bf16[64,3072]{1,0:T(8,128)(2,1)} %pick.3.refs_0_), channel_id=1, source_target_pairs={{0,6},{2,0},{4,2},{6,4},{1,7},{3,1},{5,3},{7,5},{8,14},{10,8},{12,... | collective-permute-start | bytes 1179656 | tf_op jit(solution)/shard_map/ppermute | solution.py:347
  154.8 27.2 %collective-permute-start.18 = (bf16[2,256,1536]{2,1,0:T(8,128)(2,1)}, bf16[2,256,1536]{2,1,0:T(8,128)(2,1)}, u32[]{:S(2)}, u32[]{:S(2)}) collective-permute-start(bf16[2,256,1536]{2,1,0:T(8,128)(2,1)} %get-tuple-element.49), channel_id=1, source_target_pairs={{0,1},{1,0},{2,3},{3,2},{4,5},{5,4},{6,7},{7,6},{8,9},{9,8},{10,11... | collective-permute-start | bytes 4718600 | tf_op jit(solution)/shard_map/ppermute | solution.py:347
  155.2 28.4 %collective-permute-start.19 = (bf16[2,256,1536]{2,1,0:T(8,128)(2,1)}, bf16[2,256,1536]{2,1,0:T(8,128)(2,1)}, u32[]{:S(2)}, u32[]{:S(2)}) collective-permute-start(bf16[2,256,1536]{2,1,0:T(8,128)(2,1)} %get-tuple-element.50), channel_id=1, source_target_pairs={{1,2},{3,4},{5,6},{7,8},{9,10},{11,12},{13,14},{2,1},{4,3},{6,5},{... | collective-permute-start | bytes 4718600 | tf_op jit(solution)/shard_map/ppermute | solution.py:356
  178.2 35.0 %collective-permute-start.15 = (bf16[2,256,1536]{2,1,0:T(8,128)(2,1)}, bf16[2,256,1536]{2,1,0:T(8,128)(2,1)S(1)}, u32[]{:S(2)}, u32[]{:S(2)}) collective-permute-start(bf16[2,256,1536]{2,1,0:T(8,128)(2,1)} %get-tuple-element.45), channel_id=1, source_target_pairs={{0,1},{1,0},{2,3},{3,2},{4,5},{5,4},{6,7},{7,6},{8,9},{9,8},{10,11... | collective-permute-start | bytes 4718600 | tf_op jit(solution)/shard_map/ppermute | solution.py:347
  178.3 34.9 %collective-permute-start.16 = (bf16[2,256,1536]{2,1,0:T(8,128)(2,1)}, bf16[2,256,1536]{2,1,0:T(8,128)(2,1)}, u32[]{:S(2)}, u32[]{:S(2)}) collective-permute-start(bf16[2,256,1536]{2,1,0:T(8,128)(2,1)} %get-tuple-element.46), channel_id=1, source_target_pairs={{1,2},{3,4},{5,6},{7,8},{9,10},{11,12},{13,14},{2,1},{4,3},{6,5},{... | collective-permute-start | bytes 4718600 | tf_op jit(solution)/shard_map/ppermute | solution.py:356
  189.6 23.6 %collective-permute-start.22 = (bf16[64,1536]{1,0:T(8,128)(2,1)S(1)}, bf16[64,1536]{1,0:T(8,128)(2,1)S(1)}, u32[]{:S(2)}, u32[]{:S(2)}) collective-permute-start(bf16[64,1536]{1,0:T(8,128)(2,1)S(1)} %get-tuple-element.58), channel_id=1, source_target_pairs={{0,6},{2,0},{4,2},{6,4},{1,7},{3,1},{5,3},{7,5},{8,14},{10,8},{12,... | collective-permute-start | bytes 589832 | tf_op jit(solution)/shard_map/ppermute | solution.py:347
  194.3 18.9 %collective-permute-start.21 = (bf16[64,1536]{1,0:T(8,128)(2,1)S(1)}, bf16[64,1536]{1,0:T(8,128)(2,1)S(1)}, u32[]{:S(2)}, u32[]{:S(2)}) collective-permute-start(bf16[64,1536]{1,0:T(8,128)(2,1)S(1)} %get-tuple-element.59), channel_id=1, source_target_pairs={{0,4},{2,6},{4,0},{6,2},{1,5},{3,7},{5,1},{7,3},{8,12},{10,14},{12... | collective-permute-start | bytes 589832 | tf_op jit(solution)/shard_map/ppermute | solution.py:347
  194.3 18.9 %collective-permute-start.20 = (bf16[64,1536]{1,0:T(8,128)(2,1)S(1)}, bf16[64,1536]{1,0:T(8,128)(2,1)S(1)}, u32[]{:S(2)}, u32[]{:S(2)}) collective-permute-start(bf16[64,1536]{1,0:T(8,128)(2,1)S(1)} %get-tuple-element.60), channel_id=1, source_target_pairs={{0,2},{2,4},{4,6},{6,0},{1,3},{3,5},{5,7},{7,1},{8,10},{10,12},{12... | collective-permute-start | bytes 589832 | tf_op jit(solution)/shard_map/ppermute | solution.py:347
  216.7 12.0 %collective-permute-start.23 = (bf16[64,3072]{1,0:T(8,128)(2,1)}, bf16[64,3072]{1,0:T(8,128)(2,1)S(1)}, u32[]{:S(2)}, u32[]{:S(2)}) collective-permute-start(bf16[64,3072]{1,0:T(8,128)(2,1)} %gather.1.a_ref), channel_id=1, source_target_pairs={{0,8},{8,0},{1,9},{9,1},{2,10},{10,2},{3,11},{11,3},{4,12},{12,4},... | collective-permute-start | bytes 1179656 | tf_op jit(solution)/shard_map/ppermute | solution.py:347
  231.4 11.8 %collective-permute-start.26 = (bf16[64,3072]{1,0:T(8,128)(2,1)}, bf16[64,3072]{1,0:T(8,128)(2,1)S(1)}, u32[]{:S(2)}, u32[]{:S(2)}) collective-permute-start(bf16[64,3072]{1,0:T(8,128)(2,1)} %add.52.refs_0_), channel_id=1, source_target_pairs={{0,2},{2,4},{4,6},{6,0},{1,3},{3,5},{5,7},{7,1},{8,10},{10,12},{12... | collective-permute-start | bytes 1179656 | tf_op jit(solution)/shard_map/ppermute | solution.py:347
  231.4 21.1 %collective-permute-start.25 = (bf16[64,3072]{1,0:T(8,128)(2,1)}, bf16[64,3072]{1,0:T(8,128)(2,1)S(1)}, u32[]{:S(2)}, u32[]{:S(2)}) collective-permute-start(bf16[64,3072]{1,0:T(8,128)(2,1)} %add.52.refs_0_), channel_id=1, source_target_pairs={{0,4},{2,6},{4,0},{6,2},{1,5},{3,7},{5,1},{7,3},{8,12},{10,14},{12... | collective-permute-start | bytes 1179656 | tf_op jit(solution)/shard_map/ppermute | solution.py:347
  236.0 16.7 %collective-permute-start.24 = (bf16[64,3072]{1,0:T(8,128)(2,1)}, bf16[64,3072]{1,0:T(8,128)(2,1)S(1)}, u32[]{:S(2)}, u32[]{:S(2)}) collective-permute-start(bf16[64,3072]{1,0:T(8,128)(2,1)} %add.52.refs_0_), channel_id=1, source_target_pairs={{0,6},{2,0},{4,2},{6,4},{1,7},{3,1},{5,3},{7,5},{8,14},{10,8},{12,... | collective-permute-start | bytes 1179656 | tf_op jit(solution)/shard_map/ppermute | solution.py:347
  (37 other events, 144.8 us)
Sparse Core Ops, SparseCore 0:
  10.3 56.0 all-gather.2
  83.4 57.3 all-gather.4
  160.6 46.7 reduce-scatter.1

commit v3 on v2

--- a/solution.py
+++ b/solution.py
@@ -175,57 +175,73 @@
     )(info, *rows, *ga, *prior, *after)
 
 
-def combine_kernel(info, own_ref, rin_ref, rout_ref, mine_ref, theirs_ref, *rest):
-    gk_ref, gv_ref, total = rest[-3:]
-    core, hit, y = info[3], info[4], info[5]
-    total[...] = own_ref[...].astype(F32) + rin_ref[...].astype(F32) + rout_ref[...].astype(F32)
-
-    @pl.when(hit > 0)
-    def _():
-        for r in range(4):
-            place = pl.multiple_of(lax.rem(y + r, 4) * PART, PART)
-            mine = mine_ref[r * PART : (r + 1) * PART].astype(F32)
-            theirs = theirs_ref[r * PART : (r + 1) * PART].astype(F32)
-            total[0, pl.ds(place, PART)] += jnp.where(core == 0, mine, theirs)
-            total[1, pl.ds(place, PART)] += jnp.where(core == 0, theirs, mine)
-
+def combine_kernel(info, own_ref, rin_ref, rout_ref, *rest):
+    gk_ref, gv_ref = rest[-2:]
+    total = own_ref[...].astype(F32) + rin_ref[...].astype(F32) + rout_ref[...].astype(F32)
     gk_ref[...] = total[0].astype(BF16)
     gv_ref[...] = total[1].astype(BF16)
 
 
-def combine(part, info, own, rin, rout, sums, prior):
+def combine(part, info, own, rin, rout, prior, after):
     wide = 4 * HD
     steps = CHUNK * HD // wide
-
-    def head(t, info):
-        return (0, info[6 + part] * steps + t)
-
-    def col(t, *_):
-        return (0, part * steps + t)
-
-    def pair(t, *_):
-        return (0, 0, t)
-
-    two = pl.BlockSpec((2, BLK, wide), pair)
-    one = pl.BlockSpec((BLK, wide), col)
+    two = pl.BlockSpec((2, BLK, wide), lambda t, *_: (0, 0, t))
     full = jax.ShapeDtypeStruct((BLK, D), BF16)
     return pl.pallas_call(
         combine_kernel,
         grid_spec=pltpu.PrefetchScalarGridSpec(
             num_scalar_prefetch=1,
             grid=(steps,),
-            in_specs=[two, two, two, one, one] + [ANY] * len(prior),
-            out_specs=[pl.BlockSpec((BLK, wide), head)] * 2,
-            scratch_shapes=[pltpu.VMEM((2, BLK, wide), F32)],
+            in_specs=[two, two, two] + [ANY] * (len(prior) + len(after)),
+            out_specs=[pl.BlockSpec((BLK, wide), lambda t, info: (0, info[6 + part] * steps + t))] * 2,
         ),
         out_shape=[full, full],
-        input_output_aliases={6: 0, 7: 1} if prior else {},
+        input_output_aliases={4: 0, 5: 1} if prior else {},
         compiler_params=pltpu.CompilerParams(vmem_limit_bytes=VMEM),
         cost_estimate=pl.CostEstimate(
-            flops=CHUNK * BLK * HD * 8, bytes_accessed=CHUNK * BLK * HD * 2 * 10, transcendentals=0
+            flops=CHUNK * BLK * HD * 4, bytes_accessed=CHUNK * BLK * HD * 2 * 8, transcendentals=0
         ),
         name="combine",
-    )(info, own, rin, rout, *sums, *prior)
+    )(info, own, rin, rout, *prior, *after)
+
+
+def finish_kernel(info, mine_ref, theirs_ref, gk_ref, gv_ref, ok_ref, ov_ref):
+    core, hit, y = info[3], info[4], info[5]
+    ok_ref[...] = gk_ref[...]
+    ov_ref[...] = gv_ref[...]
+
+    @pl.when(hit > 0)
+    def _():
+        for r in range(4):
+            rows = pl.ds(pl.multiple_of(lax.rem(y + r, 4) * PART, PART), PART)
+            mine = mine_ref[r * PART : (r + 1) * PART].astype(F32)
+            theirs = theirs_ref[r * PART : (r + 1) * PART].astype(F32)
+            k_sum, v_sum = jnp.where(core == 0, mine, theirs), jnp.where(core == 0, theirs, mine)
+            ok_ref[rows] = (gk_ref[rows].astype(F32) + k_sum).astype(BF16)
+            ov_ref[rows] = (gv_ref[rows].astype(F32) + v_sum).astype(BF16)
+
+
+def finish(info, mine, theirs, gk, gv):
+    wide = 4 * HD
+    steps = CHUNK * HD // wide
+
+    def head(t, info):
+        return (0, lax.rem(info[6] * steps + t, 2 * steps))
+
+    here = pl.BlockSpec((BLK, wide), head)
+    sums = pl.BlockSpec((BLK, wide), lambda t, *_: (0, t))
+    full = jax.ShapeDtypeStruct((BLK, D), BF16)
+    return pl.pallas_call(
+        finish_kernel,
+        grid_spec=pltpu.PrefetchScalarGridSpec(
+            num_scalar_prefetch=1, grid=(2 * steps,), in_specs=[sums, sums, here, here], out_specs=[here, here]
+        ),
+        out_shape=[full, full],
+        input_output_aliases={3: 0, 4: 1},
+        compiler_params=pltpu.CompilerParams(vmem_limit_bytes=VMEM),
+        cost_estimate=pl.CostEstimate(flops=BLK * D * 2, bytes_accessed=BLK * D * 12, transcendentals=0),
+        name="finish",
+    )(info, mine, theirs, gk, gv)
 
 
 def add_kernel(a_ref, b_ref, *rest):
@@ -247,6 +263,27 @@
     )(a, b, *after)
 
 
+def split_kernel(a_ref, b_ref, *rest):
+    for r in range(4):
+        rows = slice(r * PART, (r + 1) * PART)
+        rest[-4 + r][...] = (a_ref[rows].astype(F32) + b_ref[rows].astype(F32)).astype(BF16)
+
+
+def split(a, b, after):
+    width = a.shape[1] // 2
+    spec = pl.BlockSpec((BLK, width), lambda t: (0, t))
+    return pl.pallas_call(
+        split_kernel,
+        grid=(2,),
+        in_specs=[spec, spec] + [ANY] * len(after),
+        out_specs=[pl.BlockSpec((PART, width), lambda t: (0, t))] * 4,
+        out_shape=[jax.ShapeDtypeStruct((PART, a.shape[1]), BF16)] * 4,
+        compiler_params=pltpu.CompilerParams(vmem_limit_bytes=VMEM),
+        cost_estimate=pl.CostEstimate(flops=a.size, bytes_accessed=a.size * 6, transcendentals=0),
+        name="split",
+    )(a, b, *after)
+
+
 def gather_kernel(first_ref, *refs):
     total = functools.reduce(jnp.add, [ref[...].astype(F32) for ref in refs[:4]])
     width = first_ref.shape[1]
@@ -254,8 +291,8 @@
     refs[-1][:, width:] = total.astype(BF16)
 
 
-def gather(first, both, after):
-    pieces = [both[:PART]] + [move(both[r * PART : (r + 1) * PART], "y", r, 4) for r in range(1, 4)]
+def gather(first, pieces, after):
+    pieces = [pieces[0]] + [move(pieces[r], "y", r, 4) for r in range(1, 4)]
     whole = pl.BlockSpec(memory_space=pltpu.VMEM)
     return pl.pallas_call(
         gather_kernel,
@@ -392,12 +429,12 @@
     q, k, v, go = queries[0], key_states[0], value_states[0], grad_out[0]
     w = lax.dynamic_slice_in_dim(w_out, core * HALF, HALF, 1)
     near = lax.all_gather(w, "z", axis=0, tiled=True)
-    far = move(w, "x_lo", 1, 2)
     go_mine = lax.dynamic_slice_in_dim(go, core * HALF, HALF, 1)
     go_core = swap_core(lax.dynamic_slice_in_dim(go, (1 - core) * HALF, HALF, 1))
     kv = jnp.stack([k, v])
     inner = swap_core(kv)
     outer = swap_outer(kv)
+    far = move(w, "x_lo", 1, 2)
 
     root_y, root_x = (root // 2) % 4, root // 8
     pieces = pack(info, k, v, inner, (go_core,))
@@ -422,13 +459,13 @@
     out = attention(1, 0, CHUNK, info, rows, ga_far, (att, gq), (both0,))
     att, gq, own1, tin1, tout1, keep, send = out
     rin1, rout1 = swap_core(tin1), swap_outer(tout1)
-    both1 = add(keep, swap_core(send), (rin0, rout0))
+    both1 = split(keep, swap_core(send), (rin0, rout0))
     quarters = gather(quarter0, both1, (rin1, rout1))
     halves = add(quarters, move(quarters, "x_hi", 1, 2))
-    sums = join([halves] + [move(halves, "y", -r, 4) for r in range(1, 4)], ())
-    sums = (sums, swap_core(sums))
-    grads = combine(0, info, own0, rin0, rout0, sums, ())
-    gk, gv = combine(1, info, own1, rin1, rout1, sums, grads)
+    grads = combine(0, info, own0, rin0, rout0, (), (quarters,))
+    grads = combine(1, info, own1, rin1, rout1, grads, (halves,))
+    sums = join([halves] + [move(halves, "y", -r, 4) for r in range(1, 4)], grads)
+    gk, gv = finish(info, sums, swap_core(sums), *grads)
     return tuple(a[None] for a in (att, gq, gk, gv))
 
 

time: 282 us -> 277 us (0.982)
  waiting for transfers between devices: 112 us -> 104 us
  Pallas kernels: 80.3 us -> 85.9 us
    ppermute x25, waiting for transfers between devices: 73.2 us -> 61.1 us  [move(): return lax.ppermute(x, axis, [(i, (i + step) % size) for i in range(size)])]
    pallas_call x0 -> x2, Pallas kernels: none -> 8.78 us  [the longest x1 6.65 us: finish(): pl.pallas_call(finish_kernel, grid_spec=pltpu.PrefetchScalarGridSpec(num_...]
    reduce_scatter x1, waiting for transfers between devices: 12.5 us -> 16.2 us  [local(): quarter0 = lax.psum_scatter(both0, 'y', scatter_dimension=0, tiled=True)]
    pallas_call x3 -> x2, Pallas kernels: 6.38 us -> 4.2 us  [add(): pl.pallas_call(add_kernel, grid=(2,), in_specs=[spec, spec] + [ANY] * len...]
  transfers between devices with their start and end apart: 31 -> 31, of which waited for: 18 -> 18; matrix products, arithmetic and copies ran while one was open for 4% -> 3% of each run, Pallas kernels for 22% -> 26%
where the time goes in v3:
time: 277 us; the launch traced here: 276 us
  waiting for transfers between devices  104 us (38%)
  Pallas kernels  85.9 us (31%)
  starting transfers between devices  44.6 us (16%)
  local copies, waits for them, and re-layouts  23.3 us (8%)
  between operations  18.5 us (7%)
    ppermute x25, waiting for transfers between devices, move(): return lax.ppermute(x, axis, [(i, (i + step) % size) for i in range(size)])  61.1 us
    ppermute x25, starting transfers between devices, move(): return lax.ppermute(x, axis, [(i, (i + step) % size) for i in range(size)])  35.6 us
    pallas_call x2, Pallas kernels, attention(): pl.pallas_call(functools.partial(attention_kernel, len(ga), part == 0), g...  33.9 us
    ppermute x3, waiting for transfers between devices, swap_outer(): return lax.ppermute(x, SKY, route)  26.2 us
    unnamed x61, local copies, waits for them, and re-layouts  16.9 us
    reduce_scatter x1, waiting for transfers between devices, local(): quarter0 = lax.psum_scatter(both0, 'y', scatter_dimension=0, tiled=True)  16.2 us
    pallas_call x2, Pallas kernels, project(): pl.pallas_call(project_kernel, grid=(width // ROWS,), in_specs=[first, se...  13.7 us
    pallas_call x2, Pallas kernels, combine(): pl.pallas_call(combine_kernel, grid_spec=pltpu.PrefetchScalarGridSpec(num...  9.79 us
  transfers between devices with their start and end apart: 31, of which 18 were waited for; matrix products, arithmetic and copies ran while one was open for 3% of the time, Pallas kernels for 26%

profile of v3, /device:TPU:1, one launch (start us, length us, event | category | flops | bytes accessed | tf_op | source)
XLA Modules:
  0.0 275.8 jit_solution(6712229475153228915)
XLA Ops:
  29.4 4.6 %pack.1 = (bf16[64,3072]{1,0:T(8,128)(2,1)}, bf16[64,3072]{1,0:T(8,128)(2,1)}, bf16[64,3072]{1,0:T(8,128)(2,1)}, bf16[64,3072]{1,0:T(8,128)(2,1)}) custom-call(s32[9]{0:T(128)} %stack.58.info, bf16[256,3072]{1,0:T(8,128)(2,1)} %bitcast.32, bf16[256,3072]{1,0:T(8,128)(2,1)} %bitcast.35, bf16[2,256,3072]{2,1,0:T(8,128)(2,1)} %collective-permute-done.inner_ref, ...), custom_call_target="tpu_custom_call" | custom-call | bytes 7864320 | tf_op jit(solution)/shard_map/pack/pallas_call | solution.py:343
  38.6 24.6 %collective-permute-done.1.refs_4_.outer_ref = bf16[2,256,3072]{2,1,0:T(8,128)(2,1)} collective-permute-done((bf16[2,256,3072]{2,1,0:T(8,128)(2,1)}, bf16[2,256,3072]{2,1,0:T(8,128)(2,1)}, u32[]{:S(2)}, u32[]{:S(2)}) %collective-permute-start.1) | collective-permute-done | bytes 3145760 | tf_op jit(solution)/shard_map/ppermute | solution.py:393
  65.9 7.2 %collective-permute-done.4.refs_2_ = bf16[64,3072]{1,0:T(8,128)(2,1)S(1)} collective-permute-done((bf16[64,3072]{1,0:T(8,128)(2,1)}, bf16[64,3072]{1,0:T(8,128)(2,1)S(1)}, u32[]{:S(2)}, u32[]{:S(2)}) %collective-permute-start.4) | collective-permute-done | bytes 393248 | tf_op jit(solution)/shard_map/ppermute | solution.py:384
  73.1 6.3 %collective-permute-done.5.refs_3_ = bf16[64,3072]{1,0:T(8,128)(2,1)S(1)} collective-permute-done((bf16[64,3072]{1,0:T(8,128)(2,1)}, bf16[64,3072]{1,0:T(8,128)(2,1)S(1)}, u32[]{:S(2)}, u32[]{:S(2)}) %collective-permute-start.5) | collective-permute-done | bytes 393248 | tf_op jit(solution)/shard_map/ppermute | solution.py:384
  83.5 4.1 %collective-permute-start.6 = (bf16[64,3072]{1,0:T(8,128)(2,1)S(1)}, bf16[64,3072]{1,0:T(8,128)(2,1)S(1)}, u32[]{:S(2)}, u32[]{:S(2)}) collective-permute-start(bf16[64,3072]{1,0:T(8,128)(2,1)S(1)} %copy-done.6), channel_id=1, source_target_pairs={{0,8},{8,0},{1,9},{9,1},{2,10},{10,2},{3,11},{11,3},{4,12},{12,4},... | collective-permute-start | bytes 1179656 | tf_op jit(solution)/shard_map/ppermute | solution.py:384
  87.6 6.8 %project.2 = (f32[256,1536]{1,0:T(8,128)}, bf16[256,1536]{1,0:T(8,128)(2,1)}) custom-call(bf16[1,256,1536]{2,1,0:T(8,128)(2,1)} %get-tuple-element.68.mine_ref, bf16[1,256,1536]{2,1,0:T(8,128)(2,1)} %bitcast.44, bf16[1536,1536]{1,0:T(8,128)(2,1)} %all-gather.3.cloned.1.call-done.piece_ref, bf16[64,3072]{1,0:T(8,128)(2,1)} %copy-done.21), custom_call_target="tpu_custom_call" | custom-call | flops 2415919104 | bytes 7077888 | tf_op jit(solution)/shard_map/project/pallas_call | solution.py:45
  97.1 5.3 %collective-permute-start.8 = (bf16[64,3072]{1,0:T(8,128)(2,1)}, bf16[64,3072]{1,0:T(8,128)(2,1)S(1)}, u32[]{:S(2)}, u32[]{:S(2)}) collective-permute-start(bf16[64,3072]{1,0:T(8,128)(2,1)} %pick.3.refs_0_), channel_id=1, source_target_pairs={{0,4},{2,6},{4,0},{6,2},{1,5},{3,7},{5,1},{7,3},{8,12},{10,14},{12... | collective-permute-start | bytes 1179656 | tf_op jit(solution)/shard_map/ppermute | solution.py:384
  102.4 5.5 %collective-permute-done.9.refs_3_ = bf16[64,3072]{1,0:T(8,128)(2,1)S(1)} collective-permute-done((bf16[64,3072]{1,0:T(8,128)(2,1)}, bf16[64,3072]{1,0:T(8,128)(2,1)S(1)}, u32[]{:S(2)}, u32[]{:S(2)}) %collective-permute-start.9) | collective-permute-done | bytes 393248 | tf_op jit(solution)/shard_map/ppermute | solution.py:384
  107.9 10.9 %collective-permute-done.8.refs_2_ = bf16[64,3072]{1,0:T(8,128)(2,1)S(1)} collective-permute-done((bf16[64,3072]{1,0:T(8,128)(2,1)}, bf16[64,3072]{1,0:T(8,128)(2,1)S(1)}, u32[]{:S(2)}, u32[]{:S(2)}) %collective-permute-start.8) | collective-permute-done | bytes 393248 | tf_op jit(solution)/shard_map/ppermute | solution.py:384
  125.2 3.9 %collective-permute-done.13.rest_1_ = bf16[256,1536]{1,0:T(8,128)(2,1)S(1)} collective-permute-done((bf16[256,1536]{1,0:T(8,128)(2,1)S(1)}, bf16[256,1536]{1,0:T(8,128)(2,1)S(1)}, u32[]{:S(2)}, u32[]{:S(2)}) %collective-permute-start.13) | collective-permute-done | bytes 786464 | tf_op jit(solution)/shard_map/ppermute | solution.py:384
  130.6 17.0 %attention.2 = (bf16[256,3072]{1,0:T(8,128)(2,1)}, bf16[256,3072]{1,0:T(8,128)(2,1)}, bf16[2,256,1536]{2,1,0:T(8,128)(2,1)}, bf16[2,256,1536]{2,1,0:T(8,128)(2,1...) custom-call(s32[9]{0:T(128)} %stack.58.info, bf16[256,3072]{1,0:T(8,128)(2,1)} %bitcast.40, ...), custom_call_target="tpu_custom_call" | custom-call | flops 4831838208 | bytes 16515072 | tf_op jit(solution)/shard_map/attention/pallas_call | solution.py:161
  148.1 6.9 %project.3 = (f32[256,1536]{1,0:T(8,128)}, bf16[256,1536]{1,0:T(8,128)(2,1)}) custom-call(bf16[1,256,1536]{2,1,0:T(8,128)(2,1)} %get-tuple-element.68.mine_ref, bf16[1,256,1536]{2,1,0:T(8,128)(2,1)} %bitcast.45, bf16[1536,1536]{1,0:T(8,128)(2,1)} %all-gather.5.cloned.1.call-done.piece_ref, bf16[256,3072]{1,0:T(8,128)(2,1)} %join.2.rest_0_.held_ref), custom_call_target="tpu_custom_call" | custom-call | flops 2415919104 | bytes 7077888 | tf_op jit(solution)/shard_map/project/pallas_call | solution.py:45
  161.6 16.9 %attention.3 = (bf16[256,3072]{1,0:T(8,128)(2,1)}, bf16[256,3072]{1,0:T(8,128)(2,1)}, bf16[2,256,1536]{2,1,0:T(8,128)(2,1)}, bf16[2,256,1536]{2,1,0:T(8,128)(2,1...) custom-call(s32[9]{0:T(128)} %stack.58.info, ...), custom_call_target="tpu_custom_call", output_to_operand_aliasing={{0}: (10, {}), {1}: (11, {})} | custom-call | flops 4831838208 | bytes 16515072 | tf_op jit(solution)/shard_map/attention/pallas_call | solution.py:161
  178.5 3.6 %collective-permute-start.22 = (bf16[2,256,1536]{2,1,0:T(8,128)(2,1)}, bf16[2,256,1536]{2,1,0:T(8,128)(2,1)}, u32[]{:S(2)}, u32[]{:S(2)}) collective-permute-start(bf16[2,256,1536]{2,1,0:T(8,128)(2,1)} %get-tuple-element.59), channel_id=1, source_target_pairs={{1,2},{3,4},{5,6},{7,8},{9,10},{11,12},{13,14},{2,1},{4,3},{6,5},{... | collective-permute-start | bytes 4718600 | tf_op jit(solution)/shard_map/ppermute | solution.py:393
  188.4 5.3 %collective-permute-start.19 = (bf16[64,1536]{1,0:T(8,128)(2,1)}, bf16[64,1536]{1,0:T(8,128)(2,1)S(1)}, u32[]{:S(2)}, u32[]{:S(2)}) collective-permute-start(bf16[64,1536]{1,0:T(8,128)(2,1)} %get-tuple-element.56), channel_id=1, source_target_pairs={{0,4},{2,6},{4,0},{6,2},{1,5},{3,7},{5,1},{7,3},{8,12},{10,14},{12... | collective-permute-start | bytes 589832 | tf_op jit(solution)/shard_map/ppermute | solution.py:384
  193.7 16.2 %reduce-scatter.2.cloned.1.call-done.first_ref = bf16[64,1536]{1,0:T(8,128)(2,1)} async-done(((bf16[256,1536]{1,0:T(8,128)(2,1)}), bf16[64,1536]{1,0:T(8,128)(2,1)}) %reduce-scatter.2.cloned.1.call-update) | async-done | bytes 196624 | tf_op jit(solution)/shard_map/reduce_scatter | solution.py:457
  209.8 3.3 %collective-permute-done.19.refs_2_ = bf16[64,1536]{1,0:T(8,128)(2,1)S(1)} collective-permute-done((bf16[64,1536]{1,0:T(8,128)(2,1)}, bf16[64,1536]{1,0:T(8,128)(2,1)S(1)}, u32[]{:S(2)}, u32[]{:S(2)}) %collective-permute-start.19) | collective-permute-done | bytes 196640 | tf_op jit(solution)/shard_map/ppermute | solution.py:384
  219.7 9.2 %collective-permute-done.23.b_ref = bf16[64,3072]{1,0:T(8,128)(2,1)S(1)} collective-permute-done((bf16[64,3072]{1,0:T(8,128)(2,1)}, bf16[64,3072]{1,0:T(8,128)(2,1)S(1)}, u32[]{:S(2)}, u32[]{:S(2)}) %collective-permute-start.23) | collective-permute-done | bytes 393248 | tf_op jit(solution)/shard_map/ppermute | solution.py:384
  231.7 4.5 %collective-permute-start.25 = (bf16[64,3072]{1,0:T(8,128)(2,1)}, bf16[64,3072]{1,0:T(8,128)(2,1)S(1)}, u32[]{:S(2)}, u32[]{:S(2)}) collective-permute-start(bf16[64,3072]{1,0:T(8,128)(2,1)} %add.50.rest_2_.refs_0_), channel_id=1, source_target_pairs={{0,4},{2,6},{4,0},{6,2},{1,5},{3,7},{5,1},{7,3},{8,12},{10,14},{12... | collective-permute-start | bytes 1179656 | tf_op jit(solution)/shard_map/ppermute | solution.py:384
  236.1 4.9 %combine.2 = (bf16[256,3072]{1,0:T(8,128)(2,1)}, bf16[256,3072]{1,0:T(8,128)(2,1)}) custom-call(s32[9]{0:T(128)} %stack.58.info, bf16[2,256,1536]{2,1,0:T(8,128)(2,1)} %get-tuple-element.61.own_ref, bf16[2,256,1536]{2,1,0:T(8,128)(2,1)} %collective-permute-done.16.rest_0_.rin_ref, bf16[2,256,1536]{2,1,0:T(8,128)(2,1)} %collective-permute-done.17.rest_1_.rout_ref, ...), custom_call_target="tpu_custom_call" | custom-call | flops 1572864 | bytes 6291456 | tf_op jit(solution)/shard_map/combine/pallas_call | solution.py:190
  241.0 4.9 %combine.3 = (bf16[256,3072]{1,0:T(8,128)(2,1)}, bf16[256,3072]{1,0:T(8,128)(2,1)}) custom-call(s32[9]{0:T(128)} %stack.58.info, bf16[2,256,1536]{2,1,0:T(8,128)(2,1)} %get-tuple-element.60.own_ref, bf16[2,256,1536]{2,1,0:T(8,128)(2,1)} %copy-done.3, ...), custom_call_target="tpu_custom_call", output_to_operand_aliasing={{0}: (4, {}), {1}: (5, {})} | custom-call | flops 1572864 | bytes 6291456 | tf_op jit(solution)/shard_map/combine/pallas_call | solution.py:190
  245.9 6.8 %collective-permute-done.25.refs_2_ = bf16[64,3072]{1,0:T(8,128)(2,1)S(1)} collective-permute-done((bf16[64,3072]{1,0:T(8,128)(2,1)}, bf16[64,3072]{1,0:T(8,128)(2,1)S(1)}, u32[]{:S(2)}, u32[]{:S(2)}) %collective-permute-start.25) | collective-permute-done | bytes 393248 | tf_op jit(solution)/shard_map/ppermute | solution.py:384
  258.2 3.2 %collective-permute-done.27.theirs_ref = bf16[256,3072]{1,0:T(8,128)(2,1)S(1)} collective-permute-done((bf16[256,3072]{1,0:T(8,128)(2,1)}, bf16[256,3072]{1,0:T(8,128)(2,1)S(1)}, u32[]{:S(2)}, u32[]{:S(2)}) %collective-permute-start.27) | collective-permute-done | bytes 1572896 | tf_op jit(solution)/shard_map/ppermute | solution.py:384
  262.6 6.6 %finish.1 = (bf16[256,3072]{1,0:T(8,128)(2,1)}, bf16[256,3072]{1,0:T(8,128)(2,1)}) custom-call(s32[9]{0:T(128)} %stack.58.info, bf16[256,3072]{1,0:T(8,128)(2,1)} %join.3.mine_ref, bf16[256,3072]{1,0:T(8,128)(2,1)} %copy-done.8, bf16[256,3072]{1,0:T(8,128)(2,1)} %get-tuple-element.64.refs_4_.gk_ref, ...), custom_call_target="tpu_custom_call", output_to_operand_aliasing={{0}: (3, {}), {1}: (4, {})} | custom-call | flops 1572864 | bytes 9437184 | tf_op jit(solution)/shard_map/finish/pallas_call | solution.py:234
  (125 shorter events, 68.8 us)
Async XLA Ops:
  7.2 80.5 %all-gather.3.cloned.1.call-start = ((), (), s32[]{:S(2)}) async-start(), calls=%async_computation.1 | async-start | bytes 5898240 | tf_op jit(solution)/shard_map/all_gather | solution.py:431
  10.0 138.1 %all-gather.5.cloned.1.call-start = ((), (), s32[]{:S(2)}) async-start(), calls=%async_computation.2 | async-start | bytes 5898240 | tf_op jit(solution)/shard_map/all_gather | solution.py:443
  14.2 14.3 %collective-permute-start = (bf16[2,256,3072]{2,1,0:T(8,128)(2,1)}, bf16[2,256,3072]{2,1,0:T(8,128)(2,1)}, u32[]{:S(2)}, u32[]{:S(2)}) collective-permute-start(bf16[2,256,3072]{2,1,0:T(8,128)(2,1)} %constant_dynamic-update-slice_fusion), channel_id=1, source_target_pairs={{0,1},{1,0},{2,3},{3,2},{4,5},{5,4},{6,7},{7,6},{8,9},{9,8},{10,11... | collective-permute-start | bytes 9437192 | tf_op jit(solution)/shard_map/ppermute | solution.py:384
  15.6 47.6 %collective-permute-start.1 = (bf16[2,256,3072]{2,1,0:T(8,128)(2,1)}, bf16[2,256,3072]{2,1,0:T(8,128)(2,1)}, u32[]{:S(2)}, u32[]{:S(2)}) collective-permute-start(bf16[2,256,3072]{2,1,0:T(8,128)(2,1)} %constant_dynamic-update-slice_fusion), channel_id=1, source_target_pairs={{1,2},{3,4},{5,6},{7,8},{9,10},{11,12},{13,14},{2,1},{4,3},{6,5},{... | collective-permute-start | bytes 9437192 | tf_op jit(solution)/shard_map/ppermute | solution.py:393
  21.5 60.8 %collective-permute-start.11 = (bf16[384,1536]{1,0:T(8,128)(2,1)S(1)}, bf16[384,1536]{1,0:T(8,128)(2,1)S(1)}, u32[]{:S(2)}, u32[]{:S(2)}) collective-permute-start(bf16[384,1536]{1,0:T(8,128)(2,1)S(1)} %copy-done.4), channel_id=1, source_target_pairs={{0,64},{64,0},{1,65},{65,1},{2,66},{66,2},{3,67},{67,3},{4,68},{68... | collective-permute-start | bytes 3538952 | tf_op jit(solution)/shard_map/ppermute | solution.py:384
  33.9 32.0 %collective-permute-start.3 = (bf16[64,3072]{1,0:T(8,128)(2,1)}, bf16[64,3072]{1,0:T(8,128)(2,1)S(1)}, u32[]{:S(2)}, u32[]{:S(2)}) collective-permute-start(bf16[64,3072]{1,0:T(8,128)(2,1)} %get-tuple-element.37), channel_id=1, source_target_pairs={{0,2},{2,4},{4,6},{6,0},{1,3},{3,5},{5,7},{7,1},{8,10},{10,12},{12... | collective-permute-start | bytes 1179656 | tf_op jit(solution)/shard_map/ppermute | solution.py:384
  35.2 37.8 %collective-permute-start.4 = (bf16[64,3072]{1,0:T(8,128)(2,1)}, bf16[64,3072]{1,0:T(8,128)(2,1)S(1)}, u32[]{:S(2)}, u32[]{:S(2)}) collective-permute-start(bf16[64,3072]{1,0:T(8,128)(2,1)} %get-tuple-element.38), channel_id=1, source_target_pairs={{0,4},{2,6},{4,0},{6,2},{1,5},{3,7},{5,1},{7,3},{8,12},{10,14},{12... | collective-permute-start | bytes 1179656 | tf_op jit(solution)/shard_map/ppermute | solution.py:384
  38.1 41.3 %collective-permute-start.5 = (bf16[64,3072]{1,0:T(8,128)(2,1)}, bf16[64,3072]{1,0:T(8,128)(2,1)S(1)}, u32[]{:S(2)}, u32[]{:S(2)}) collective-permute-start(bf16[64,3072]{1,0:T(8,128)(2,1)} %get-tuple-element.39), channel_id=1, source_target_pairs={{0,6},{2,0},{4,2},{6,4},{1,7},{3,1},{5,3},{7,5},{8,14},{10,8},{12,... | collective-permute-start | bytes 1179656 | tf_op jit(solution)/shard_map/ppermute | solution.py:384
  83.4 126.5 %reduce-scatter.2.cloned.1.call-start = ((), (), s32[]{:S(2)}) async-start(), calls=%async_computation.3 | async-start | bytes 983040 | tf_op jit(solution)/shard_map/reduce_scatter | solution.py:457
  83.5 10.9 %collective-permute-start.6 = (bf16[64,3072]{1,0:T(8,128)(2,1)S(1)}, bf16[64,3072]{1,0:T(8,128)(2,1)S(1)}, u32[]{:S(2)}, u32[]{:S(2)}) collective-permute-start(bf16[64,3072]{1,0:T(8,128)(2,1)S(1)} %copy-done.6), channel_id=1, source_target_pairs={{0,8},{8,0},{1,9},{9,1},{2,10},{10,2},{3,11},{11,3},{4,12},{12,4},... | collective-permute-start | bytes 1179656 | tf_op jit(solution)/shard_map/ppermute | solution.py:384
  97.1 10.8 %collective-permute-start.9 = (bf16[64,3072]{1,0:T(8,128)(2,1)}, bf16[64,3072]{1,0:T(8,128)(2,1)S(1)}, u32[]{:S(2)}, u32[]{:S(2)}) collective-permute-start(bf16[64,3072]{1,0:T(8,128)(2,1)} %pick.3.refs_0_), channel_id=1, source_target_pairs={{0,2},{2,4},{4,6},{6,0},{1,3},{3,5},{5,7},{7,1},{8,10},{10,12},{12... | collective-permute-start | bytes 1179656 | tf_op jit(solution)/shard_map/ppermute | solution.py:384
  97.1 21.7 %collective-permute-start.8 = (bf16[64,3072]{1,0:T(8,128)(2,1)}, bf16[64,3072]{1,0:T(8,128)(2,1)S(1)}, u32[]{:S(2)}, u32[]{:S(2)}) collective-permute-start(bf16[64,3072]{1,0:T(8,128)(2,1)} %pick.3.refs_0_), channel_id=1, source_target_pairs={{0,4},{2,6},{4,0},{6,2},{1,5},{3,7},{5,1},{7,3},{8,12},{10,14},{12... | collective-permute-start | bytes 1179656 | tf_op jit(solution)/shard_map/ppermute | solution.py:384
  102.4 16.7 %collective-permute-start.7 = (bf16[64,3072]{1,0:T(8,128)(2,1)}, bf16[64,3072]{1,0:T(8,128)(2,1)S(1)}, u32[]{:S(2)}, u32[]{:S(2)}) collective-permute-start(bf16[64,3072]{1,0:T(8,128)(2,1)} %pick.3.refs_0_), channel_id=1, source_target_pairs={{0,6},{2,0},{4,2},{6,4},{1,7},{3,1},{5,3},{7,5},{8,14},{10,8},{12,... | collective-permute-start | bytes 1179656 | tf_op jit(solution)/shard_map/ppermute | solution.py:384
  155.1 27.2 %collective-permute-start.16 = (bf16[2,256,1536]{2,1,0:T(8,128)(2,1)}, bf16[2,256,1536]{2,1,0:T(8,128)(2,1)}, u32[]{:S(2)}, u32[]{:S(2)}) collective-permute-start(bf16[2,256,1536]{2,1,0:T(8,128)(2,1)} %get-tuple-element.52), channel_id=1, source_target_pairs={{0,1},{1,0},{2,3},{3,2},{4,5},{5,4},{6,7},{7,6},{8,9},{9,8},{10,11... | collective-permute-start | bytes 4718600 | tf_op jit(solution)/shard_map/ppermute | solution.py:384
  155.4 28.4 %collective-permute-start.17 = (bf16[2,256,1536]{2,1,0:T(8,128)(2,1)}, bf16[2,256,1536]{2,1,0:T(8,128)(2,1)}, u32[]{:S(2)}, u32[]{:S(2)}) collective-permute-start(bf16[2,256,1536]{2,1,0:T(8,128)(2,1)} %get-tuple-element.53), channel_id=1, source_target_pairs={{1,2},{3,4},{5,6},{7,8},{9,10},{11,12},{13,14},{2,1},{4,3},{6,5},{... | collective-permute-start | bytes 4718600 | tf_op jit(solution)/shard_map/ppermute | solution.py:393
  178.4 35.1 %collective-permute-start.21 = (bf16[2,256,1536]{2,1,0:T(8,128)(2,1)}, bf16[2,256,1536]{2,1,0:T(8,128)(2,1)S(1)}, u32[]{:S(2)}, u32[]{:S(2)}) collective-permute-start(bf16[2,256,1536]{2,1,0:T(8,128)(2,1)} %get-tuple-element.58), channel_id=1, source_target_pairs={{0,1},{1,0},{2,3},{3,2},{4,5},{5,4},{6,7},{7,6},{8,9},{9,8},{10,11... | collective-permute-start | bytes 4718600 | tf_op jit(solution)/shard_map/ppermute | solution.py:384
  178.5 35.0 %collective-permute-start.22 = (bf16[2,256,1536]{2,1,0:T(8,128)(2,1)}, bf16[2,256,1536]{2,1,0:T(8,128)(2,1)}, u32[]{:S(2)}, u32[]{:S(2)}) collective-permute-start(bf16[2,256,1536]{2,1,0:T(8,128)(2,1)} %get-tuple-element.59), channel_id=1, source_target_pairs={{1,2},{3,4},{5,6},{7,8},{9,10},{11,12},{13,14},{2,1},{4,3},{6,5},{... | collective-permute-start | bytes 4718600 | tf_op jit(solution)/shard_map/ppermute | solution.py:393
  187.8 22.1 %collective-permute-start.18 = (bf16[64,1536]{1,0:T(8,128)(2,1)}, bf16[64,1536]{1,0:T(8,128)(2,1)S(1)}, u32[]{:S(2)}, u32[]{:S(2)}) collective-permute-start(bf16[64,1536]{1,0:T(8,128)(2,1)} %get-tuple-element.55), channel_id=1, source_target_pairs={{0,2},{2,4},{4,6},{6,0},{1,3},{3,5},{5,7},{7,1},{8,10},{10,12},{12... | collective-permute-start | bytes 589832 | tf_op jit(solution)/shard_map/ppermute | solution.py:384
  188.4 24.8 %collective-permute-start.19 = (bf16[64,1536]{1,0:T(8,128)(2,1)}, bf16[64,1536]{1,0:T(8,128)(2,1)S(1)}, u32[]{:S(2)}, u32[]{:S(2)}) collective-permute-start(bf16[64,1536]{1,0:T(8,128)(2,1)} %get-tuple-element.56), channel_id=1, source_target_pairs={{0,4},{2,6},{4,0},{6,2},{1,5},{3,7},{5,1},{7,3},{8,12},{10,14},{12... | collective-permute-start | bytes 589832 | tf_op jit(solution)/shard_map/ppermute | solution.py:384
  193.7 19.9 %collective-permute-start.20 = (bf16[64,1536]{1,0:T(8,128)(2,1)}, bf16[64,1536]{1,0:T(8,128)(2,1)S(1)}, u32[]{:S(2)}, u32[]{:S(2)}) collective-permute-start(bf16[64,1536]{1,0:T(8,128)(2,1)} %get-tuple-element.57), channel_id=1, source_target_pairs={{0,6},{2,0},{4,2},{6,4},{1,7},{3,1},{5,3},{7,5},{8,14},{10,8},{12,... | collective-permute-start | bytes 589832 | tf_op jit(solution)/shard_map/ppermute | solution.py:384
  216.9 12.0 %collective-permute-start.23 = (bf16[64,3072]{1,0:T(8,128)(2,1)}, bf16[64,3072]{1,0:T(8,128)(2,1)S(1)}, u32[]{:S(2)}, u32[]{:S(2)}) collective-permute-start(bf16[64,3072]{1,0:T(8,128)(2,1)} %gather.1.a_ref.rest_0_), channel_id=1, source_target_pairs={{0,8},{8,0},{1,9},{9,1},{2,10},{10,2},{3,11},{11,3},{4,12},{12,4},... | collective-permute-start | bytes 1179656 | tf_op jit(solution)/shard_map/ppermute | solution.py:384
  231.7 14.3 %collective-permute-start.26 = (bf16[64,3072]{1,0:T(8,128)(2,1)}, bf16[64,3072]{1,0:T(8,128)(2,1)S(1)}, u32[]{:S(2)}, u32[]{:S(2)}) collective-permute-start(bf16[64,3072]{1,0:T(8,128)(2,1)} %add.50.rest_2_.refs_0_), channel_id=1, source_target_pairs={{0,2},{2,4},{4,6},{6,0},{1,3},{3,5},{5,7},{7,1},{8,10},{10,12},{12... | collective-permute-start | bytes 1179656 | tf_op jit(solution)/shard_map/ppermute | solution.py:384
  231.7 21.0 %collective-permute-start.25 = (bf16[64,3072]{1,0:T(8,128)(2,1)}, bf16[64,3072]{1,0:T(8,128)(2,1)S(1)}, u32[]{:S(2)}, u32[]{:S(2)}) collective-permute-start(bf16[64,3072]{1,0:T(8,128)(2,1)} %add.50.rest_2_.refs_0_), channel_id=1, source_target_pairs={{0,4},{2,6},{4,0},{6,2},{1,5},{3,7},{5,1},{7,3},{8,12},{10,14},{12... | collective-permute-start | bytes 1179656 | tf_op jit(solution)/shard_map/ppermute | solution.py:384
  236.1 16.7 %collective-permute-start.24 = (bf16[64,3072]{1,0:T(8,128)(2,1)}, bf16[64,3072]{1,0:T(8,128)(2,1)S(1)}, u32[]{:S(2)}, u32[]{:S(2)}) collective-permute-start(bf16[64,3072]{1,0:T(8,128)(2,1)} %add.50.rest_2_.refs_0_), channel_id=1, source_target_pairs={{0,6},{2,0},{4,2},{6,4},{1,7},{3,1},{5,3},{7,5},{8,14},{10,8},{12,... | collective-permute-start | bytes 1179656 | tf_op jit(solution)/shard_map/ppermute | solution.py:384
  (37 other events, 146.5 us)
Sparse Core Ops, SparseCore 0:
  10.3 56.0 all-gather.2
  83.5 57.2 all-gather.4
  160.8 48.9 reduce-scatter.1

commit v4 on v3

--- a/solution.py
+++ b/solution.py
@@ -205,7 +205,8 @@
     )(info, own, rin, rout, *prior, *after)
 
 
-def finish_kernel(info, mine_ref, theirs_ref, gk_ref, gv_ref, ok_ref, ov_ref):
+def finish_kernel(info, *refs):
+    gk_ref, gv_ref, ok_ref, ov_ref = refs[8:]
     core, hit, y = info[3], info[4], info[5]
     ok_ref[...] = gk_ref[...]
     ov_ref[...] = gv_ref[...]
@@ -214,8 +215,7 @@
     def _():
         for r in range(4):
             rows = pl.ds(pl.multiple_of(lax.rem(y + r, 4) * PART, PART), PART)
-            mine = mine_ref[r * PART : (r + 1) * PART].astype(F32)
-            theirs = theirs_ref[r * PART : (r + 1) * PART].astype(F32)
+            mine, theirs = refs[r][...].astype(F32), refs[4 + r][...].astype(F32)
             k_sum, v_sum = jnp.where(core == 0, mine, theirs), jnp.where(core == 0, theirs, mine)
             ok_ref[rows] = (gk_ref[rows].astype(F32) + k_sum).astype(BF16)
             ov_ref[rows] = (gv_ref[rows].astype(F32) + v_sum).astype(BF16)
@@ -229,19 +229,19 @@
         return (0, lax.rem(info[6] * steps + t, 2 * steps))
 
     here = pl.BlockSpec((BLK, wide), head)
-    sums = pl.BlockSpec((BLK, wide), lambda t, *_: (0, t))
+    sums = pl.BlockSpec((PART, wide), lambda t, *_: (0, t))
     full = jax.ShapeDtypeStruct((BLK, D), BF16)
     return pl.pallas_call(
         finish_kernel,
         grid_spec=pltpu.PrefetchScalarGridSpec(
-            num_scalar_prefetch=1, grid=(2 * steps,), in_specs=[sums, sums, here, here], out_specs=[here, here]
+            num_scalar_prefetch=1, grid=(2 * steps,), in_specs=[sums] * 8 + [here, here], out_specs=[here, here]
         ),
         out_shape=[full, full],
-        input_output_aliases={3: 0, 4: 1},
+        input_output_aliases={9: 0, 10: 1},
         compiler_params=pltpu.CompilerParams(vmem_limit_bytes=VMEM),
         cost_estimate=pl.CostEstimate(flops=BLK * D * 2, bytes_accessed=BLK * D * 12, transcendentals=0),
         name="finish",
-    )(info, mine, theirs, gk, gv)
+    )(info, *mine, *theirs, gk, gv)
 
 
 def add_kernel(a_ref, b_ref, *rest):
@@ -444,9 +444,9 @@
     ga_own, ga_core = project(go_mine[None], go_core[None], (0, 0), near, (arrived[1],))
     other = move(mine, "x_hi", 1, 2)
     quarter = pick((root_x - x) % 2, (mine, other), (ga_own,))
-    held = join([quarter] + [move(quarter, "y", -r, 4) for r in range(1, 4)], ())
+    ga_near = (ga_own, swap_core(ga_core))
+    held = join([quarter] + [move(quarter, "y", -r, 4) for r in range(1, 4)], ga_near)
     rows = (q, k, v, inner, outer, held, swap_core(held))
-    ga_near = (ga_own, swap_core(ga_core))
 
     out = attention(0, 0, CHUNK, info, rows, ga_near, (), ())
     att, gq, own0, tin0, tout0, keep, send = out
@@ -464,8 +464,9 @@
     halves = add(quarters, move(quarters, "x_hi", 1, 2))
     grads = combine(0, info, own0, rin0, rout0, (), (quarters,))
     grads = combine(1, info, own1, rin1, rout1, grads, (halves,))
-    sums = join([halves] + [move(halves, "y", -r, 4) for r in range(1, 4)], grads)
-    gk, gv = finish(info, sums, swap_core(sums), *grads)
+    sums = [halves] + [move(halves, "y", -r, 4) for r in range(1, 4)]
+    sums[2] = hold(sums[2], grads)
+    gk, gv = finish(info, sums, [swap_core(s) for s in sums], *grads)
     return tuple(a[None] for a in (att, gq, gk, gv))
 
 

time: 277 us -> 272 us (0.982)
  waiting for transfers between devices: 104 us -> 100 us
    ppermute x25 -> x28, waiting for transfers between devices: 61.1 us -> 56.9 us  [move(): return lax.ppermute(x, axis, [(i, (i + step) % size) for i in range(size)])]
    ppermute x25 -> x28, starting transfers between devices: 35.6 us -> 36.9 us  [move(): return lax.ppermute(x, axis, [(i, (i + step) % size) for i in range(size)])]
    unnamed x61 -> x65, local copies, waits for them, and re-layouts: 16.9 us -> 16.3 us
  transfers between devices with their start and end apart: 31 -> 34, of which waited for: 18 -> 16; matrix products, arithmetic and copies ran while one was open for 3% -> 3% of each run, Pallas kernels for 26% -> 27%
where the time goes in v4:
time: 272 us; the launch traced here: 271 us
  waiting for transfers between devices  100 us (37%)
  Pallas kernels  83.6 us (31%)
  starting transfers between devices  46 us (17%)
  local copies, waits for them, and re-layouts  22.6 us (8%)
  between operations  18.4 us (7%)
    ppermute x28, waiting for transfers between devices, move(): return lax.ppermute(x, axis, [(i, (i + step) % size) for i in range(size)])  56.9 us
    ppermute x28, starting transfers between devices, move(): return lax.ppermute(x, axis, [(i, (i + step) % size) for i in range(size)])  36.9 us
    pallas_call x2, Pallas kernels, attention(): pl.pallas_call(functools.partial(attention_kernel, len(ga), part == 0), g...  33.8 us
    ppermute x3, waiting for transfers between devices, swap_outer(): return lax.ppermute(x, SKY, route)  26.6 us
    reduce_scatter x1, waiting for transfers between devices, local(): quarter0 = lax.psum_scatter(both0, 'y', scatter_dimension=0, tiled=True)  16.6 us
    unnamed x65, local copies, waits for them, and re-layouts  16.3 us
    pallas_call x2, Pallas kernels, project(): pl.pallas_call(project_kernel, grid=(width // ROWS,), in_specs=[first, se...  13.6 us
    pallas_call x2, Pallas kernels, combine(): pl.pallas_call(combine_kernel, grid_spec=pltpu.PrefetchScalarGridSpec(num...  9.92 us
  transfers between devices with their start and end apart: 34, of which 16 were waited for; matrix products, arithmetic and copies ran while one was open for 3% of the time, Pallas kernels for 27%

profile of v4, /device:TPU:1, one launch (start us, length us, event | category | flops | bytes accessed | tf_op | source)
XLA Modules:
  0.0 270.7 jit_solution(7902340536538993529)
XLA Ops:
  15.6 3.2 %collective-permute-start.1 = (bf16[2,256,3072]{2,1,0:T(8,128)(2,1)}, bf16[2,256,3072]{2,1,0:T(8,128)(2,1)}, u32[]{:S(2)}, u32[]{:S(2)}) collective-permute-start(bf16[2,256,3072]{2,1,0:T(8,128)(2,1)} %constant_dynamic-update-slice_fusion), channel_id=1, source_target_pairs={{1,2},{3,4},{5,6},{7,8},{9,10},{11,12},{13,14},{2,1},{4,3},{6,5},{... | collective-permute-start | bytes 9437192 | tf_op jit(solution)/shard_map/ppermute | solution.py:393
  29.1 4.5 %pack.1 = (bf16[64,3072]{1,0:T(8,128)(2,1)}, bf16[64,3072]{1,0:T(8,128)(2,1)}, bf16[64,3072]{1,0:T(8,128)(2,1)}, bf16[64,3072]{1,0:T(8,128)(2,1)}) custom-call(s32[9]{0:T(128)} %stack.58.info, bf16[256,3072]{1,0:T(8,128)(2,1)} %bitcast.32, bf16[256,3072]{1,0:T(8,128)(2,1)} %bitcast.35, bf16[2,256,3072]{2,1,0:T(8,128)(2,1)} %collective-permute-done.inner_ref, ...), custom_call_target="tpu_custom_call" | custom-call | bytes 7864320 | tf_op jit(solution)/shard_map/pack/pallas_call | solution.py:343
  34.9 2.9 %collective-permute-start.4 = (bf16[64,3072]{1,0:T(8,128)(2,1)}, bf16[64,3072]{1,0:T(8,128)(2,1)S(1)}, u32[]{:S(2)}, u32[]{:S(2)}) collective-permute-start(bf16[64,3072]{1,0:T(8,128)(2,1)} %get-tuple-element.38), channel_id=1, source_target_pairs={{0,4},{2,6},{4,0},{6,2},{1,5},{3,7},{5,1},{7,3},{8,12},{10,14},{12... | collective-permute-start | bytes 1179656 | tf_op jit(solution)/shard_map/ppermute | solution.py:384
  38.3 24.8 %collective-permute-done.1.refs_4_.outer_ref = bf16[2,256,3072]{2,1,0:T(8,128)(2,1)} collective-permute-done((bf16[2,256,3072]{2,1,0:T(8,128)(2,1)}, bf16[2,256,3072]{2,1,0:T(8,128)(2,1)}, u32[]{:S(2)}, u32[]{:S(2)}) %collective-permute-start.1) | collective-permute-done | bytes 3145760 | tf_op jit(solution)/shard_map/ppermute | solution.py:393
  65.9 7.2 %collective-permute-done.4.refs_2_ = bf16[64,3072]{1,0:T(8,128)(2,1)S(1)} collective-permute-done((bf16[64,3072]{1,0:T(8,128)(2,1)}, bf16[64,3072]{1,0:T(8,128)(2,1)S(1)}, u32[]{:S(2)}, u32[]{:S(2)}) %collective-permute-start.4) | collective-permute-done | bytes 393248 | tf_op jit(solution)/shard_map/ppermute | solution.py:384
  73.1 6.2 %collective-permute-done.5.refs_3_ = bf16[64,3072]{1,0:T(8,128)(2,1)S(1)} collective-permute-done((bf16[64,3072]{1,0:T(8,128)(2,1)}, bf16[64,3072]{1,0:T(8,128)(2,1)S(1)}, u32[]{:S(2)}, u32[]{:S(2)}) %collective-permute-start.5) | collective-permute-done | bytes 393248 | tf_op jit(solution)/shard_map/ppermute | solution.py:384
  83.4 4.2 %collective-permute-start.6 = (bf16[64,3072]{1,0:T(8,128)(2,1)S(1)}, bf16[64,3072]{1,0:T(8,128)(2,1)S(1)}, u32[]{:S(2)}, u32[]{:S(2)}) collective-permute-start(bf16[64,3072]{1,0:T(8,128)(2,1)S(1)} %copy-done.7), channel_id=1, source_target_pairs={{0,8},{8,0},{1,9},{9,1},{2,10},{10,2},{3,11},{11,3},{4,12},{12,4},... | collective-permute-start | bytes 1179656 | tf_op jit(solution)/shard_map/ppermute | solution.py:384
  87.5 6.8 %project.2 = (f32[256,1536]{1,0:T(8,128)}, bf16[256,1536]{1,0:T(8,128)(2,1)}) custom-call(bf16[1,256,1536]{2,1,0:T(8,128)(2,1)} %get-tuple-element.68.mine_ref, bf16[1,256,1536]{2,1,0:T(8,128)(2,1)} %bitcast.44, bf16[1536,1536]{1,0:T(8,128)(2,1)} %all-gather.3.cloned.1.call-done.piece_ref, bf16[64,3072]{1,0:T(8,128)(2,1)} %copy-done.22), custom_call_target="tpu_custom_call" | custom-call | flops 2415919104 | bytes 7077888 | tf_op jit(solution)/shard_map/project/pallas_call | solution.py:45
  94.3 4.3 %collective-permute-start.10 = (bf16[256,1536]{1,0:T(8,128)(2,1)}, bf16[256,1536]{1,0:T(8,128)(2,1)S(1)}, u32[]{:S(2)}, u32[]{:S(2)}) collective-permute-start(bf16[256,1536]{1,0:T(8,128)(2,1)} %get-tuple-element.41), channel_id=1, source_target_pairs={{0,1},{1,0},{2,3},{3,2},{4,5},{5,4},{6,7},{7,6},{8,9},{9,8},{10,11... | collective-permute-start | bytes 2359304 | tf_op jit(solution)/shard_map/ppermute | solution.py:384
  104.0 18.1 %collective-permute-done.9.refs_3_ = bf16[64,3072]{1,0:T(8,128)(2,1)S(1)} collective-permute-done((bf16[64,3072]{1,0:T(8,128)(2,1)}, bf16[64,3072]{1,0:T(8,128)(2,1)S(1)}, u32[]{:S(2)}, u32[]{:S(2)}) %collective-permute-start.9) | collective-permute-done | bytes 393248 | tf_op jit(solution)/shard_map/ppermute | solution.py:384
  127.4 3.2 %collective-permute-done.11.theirs_ref = bf16[256,3072]{1,0:T(8,128)(2,1)S(1)} collective-permute-done((bf16[256,3072]{1,0:T(8,128)(2,1)}, bf16[256,3072]{1,0:T(8,128)(2,1)S(1)}, u32[]{:S(2)}, u32[]{:S(2)}) %collective-permute-start.11) | collective-permute-done | bytes 1572896 | tf_op jit(solution)/shard_map/ppermute | solution.py:384
  131.8 16.9 %attention.2 = (bf16[256,3072]{1,0:T(8,128)(2,1)}, bf16[256,3072]{1,0:T(8,128)(2,1)}, bf16[2,256,1536]{2,1,0:T(8,128)(2,1)}, bf16[2,256,1536]{2,1,0:T(8,128)(2,1...) custom-call(s32[9]{0:T(128)} %stack.58.info, bf16[256,3072]{1,0:T(8,128)(2,1)} %bitcast.40, ...), custom_call_target="tpu_custom_call" | custom-call | flops 4831838208 | bytes 16515072 | tf_op jit(solution)/shard_map/attention/pallas_call | solution.py:161
  149.2 6.8 %project.3 = (f32[256,1536]{1,0:T(8,128)}, bf16[256,1536]{1,0:T(8,128)(2,1)}) custom-call(bf16[1,256,1536]{2,1,0:T(8,128)(2,1)} %get-tuple-element.68.mine_ref, bf16[1,256,1536]{2,1,0:T(8,128)(2,1)} %bitcast.45, bf16[1536,1536]{1,0:T(8,128)(2,1)} %all-gather.5.cloned.1.call-done.piece_ref, bf16[256,3072]{1,0:T(8,128)(2,1)} %join.1.rest_0_.held_ref), custom_call_target="tpu_custom_call" | custom-call | flops 2415919104 | bytes 7077888 | tf_op jit(solution)/shard_map/project/pallas_call | solution.py:45
  162.7 16.9 %attention.3 = (bf16[256,3072]{1,0:T(8,128)(2,1)}, bf16[256,3072]{1,0:T(8,128)(2,1)}, bf16[2,256,1536]{2,1,0:T(8,128)(2,1)}, bf16[2,256,1536]{2,1,0:T(8,128)(2,1...) custom-call(s32[9]{0:T(128)} %stack.58.info, ...), custom_call_target="tpu_custom_call", output_to_operand_aliasing={{0}: (10, {}), {1}: (11, {})} | custom-call | flops 4831838208 | bytes 16515072 | tf_op jit(solution)/shard_map/attention/pallas_call | solution.py:161
  179.7 3.6 %collective-permute-start.22 = (bf16[2,256,1536]{2,1,0:T(8,128)(2,1)}, bf16[2,256,1536]{2,1,0:T(8,128)(2,1)}, u32[]{:S(2)}, u32[]{:S(2)}) collective-permute-start(bf16[2,256,1536]{2,1,0:T(8,128)(2,1)} %get-tuple-element.59), channel_id=1, source_target_pairs={{1,2},{3,4},{5,6},{7,8},{9,10},{11,12},{13,14},{2,1},{4,3},{6,5},{... | collective-permute-start | bytes 4718600 | tf_op jit(solution)/shard_map/ppermute | solution.py:393
  190.5 5.3 %collective-permute-start.19 = (bf16[64,1536]{1,0:T(8,128)(2,1)}, bf16[64,1536]{1,0:T(8,128)(2,1)S(1)}, u32[]{:S(2)}, u32[]{:S(2)}) collective-permute-start(bf16[64,1536]{1,0:T(8,128)(2,1)} %get-tuple-element.56), channel_id=1, source_target_pairs={{0,4},{2,6},{4,0},{6,2},{1,5},{3,7},{5,1},{7,3},{8,12},{10,14},{12... | collective-permute-start | bytes 589832 | tf_op jit(solution)/shard_map/ppermute | solution.py:384
  195.8 16.6 %reduce-scatter.2.cloned.1.call-done.first_ref = bf16[64,1536]{1,0:T(8,128)(2,1)} async-done(((bf16[256,1536]{1,0:T(8,128)(2,1)}), bf16[64,1536]{1,0:T(8,128)(2,1)}) %reduce-scatter.2.cloned.1.call-update) | async-done | bytes 196624 | tf_op jit(solution)/shard_map/reduce_scatter | solution.py:457
  218.1 3.8 %collective-permute-start.23 = (bf16[64,3072]{1,0:T(8,128)(2,1)}, bf16[64,3072]{1,0:T(8,128)(2,1)S(1)}, u32[]{:S(2)}, u32[]{:S(2)}) collective-permute-start(bf16[64,3072]{1,0:T(8,128)(2,1)} %gather.1.a_ref.rest_0_), channel_id=1, source_target_pairs={{0,8},{8,0},{1,9},{9,1},{2,10},{10,2},{3,11},{11,3},{4,12},{12,4},... | collective-permute-start | bytes 1179656 | tf_op jit(solution)/shard_map/ppermute | solution.py:384
  221.8 9.3 %collective-permute-done.23.b_ref = bf16[64,3072]{1,0:T(8,128)(2,1)S(1)} collective-permute-done((bf16[64,3072]{1,0:T(8,128)(2,1)}, bf16[64,3072]{1,0:T(8,128)(2,1)S(1)}, u32[]{:S(2)}, u32[]{:S(2)}) %collective-permute-start.23) | collective-permute-done | bytes 393248 | tf_op jit(solution)/shard_map/ppermute | solution.py:384
  233.8 2.8 %collective-permute-start.26 = (bf16[64,3072]{1,0:T(8,128)(2,1)}, bf16[64,3072]{1,0:T(8,128)(2,1)S(1)}, u32[]{:S(2)}, u32[]{:S(2)}) collective-permute-start(bf16[64,3072]{1,0:T(8,128)(2,1)} %add.50.rest_2_.refs_0_), channel_id=1, source_target_pairs={{0,2},{2,4},{4,6},{6,0},{1,3},{3,5},{5,7},{7,1},{8,10},{10,12},{12... | collective-permute-start | bytes 1179656 | tf_op jit(solution)/shard_map/ppermute | solution.py:384
  236.6 5.0 %combine.2 = (bf16[256,3072]{1,0:T(8,128)(2,1)}, bf16[256,3072]{1,0:T(8,128)(2,1)}) custom-call(s32[9]{0:T(128)} %stack.58.info, bf16[2,256,1536]{2,1,0:T(8,128)(2,1)} %get-tuple-element.61.own_ref, bf16[2,256,1536]{2,1,0:T(8,128)(2,1)} %collective-permute-done.16.rest_0_.rin_ref, bf16[2,256,1536]{2,1,0:T(8,128)(2,1)} %collective-permute-done.17.rest_1_.rout_ref, ...), custom_call_target="tpu_custom_call" | custom-call | flops 1572864 | bytes 6291456 | tf_op jit(solution)/shard_map/combine/pallas_call | solution.py:190
  243.5 4.9 %combine.3 = (bf16[256,3072]{1,0:T(8,128)(2,1)}, bf16[256,3072]{1,0:T(8,128)(2,1)}) custom-call(s32[9]{0:T(128)} %stack.58.info, bf16[2,256,1536]{2,1,0:T(8,128)(2,1)} %get-tuple-element.60.own_ref, bf16[2,256,1536]{2,1,0:T(8,128)(2,1)} %copy-done.3, ...), custom_call_target="tpu_custom_call", output_to_operand_aliasing={{0}: (4, {}), {1}: (5, {})} | custom-call | flops 1572864 | bytes 6291456 | tf_op jit(solution)/shard_map/combine/pallas_call | solution.py:190
  249.3 5.1 %collective-permute-done.26.refs_3_ = bf16[64,3072]{1,0:T(8,128)(2,1)S(1)} collective-permute-done((bf16[64,3072]{1,0:T(8,128)(2,1)}, bf16[64,3072]{1,0:T(8,128)(2,1)S(1)}, u32[]{:S(2)}, u32[]{:S(2)}) %collective-permute-start.26) | collective-permute-done | bytes 393248 | tf_op jit(solution)/shard_map/ppermute | solution.py:384
  257.4 6.7 %finish.1 = (bf16[256,3072]{1,0:T(8,128)(2,1)}, bf16[256,3072]{1,0:T(8,128)(2,1)}) custom-call(s32[9]{0:T(128)} %stack.58.info, bf16[64,3072]{1,0:T(8,128)(2,1)} %add.50.rest_2_.refs_0_, bf16[64,3072]{1,0:T(8,128)(2,1)} %copy-done.16, bf16[64,3072]{1,0:T(8,128)(2,1)} %hold.3.refs_2_, ...), custom_call_target="tpu_custom_call", output_to_operand_aliasing={{0}: (9, {}), {1}: (10, {})} | custom-call | flops 1572864 | bytes 9437184 | tf_op jit(solution)/shard_map/finish/pallas_call | solution.py:234
  (135 shorter events, 63.3 us)
Async XLA Ops:
  7.2 80.4 %all-gather.3.cloned.1.call-start = ((), (), s32[]{:S(2)}) async-start(), calls=%async_computation.1 | async-start | bytes 5898240 | tf_op jit(solution)/shard_map/all_gather | solution.py:431
  10.0 139.3 %all-gather.5.cloned.1.call-start = ((), (), s32[]{:S(2)}) async-start(), calls=%async_computation.2 | async-start | bytes 5898240 | tf_op jit(solution)/shard_map/all_gather | solution.py:443
  14.1 14.1 %collective-permute-start = (bf16[2,256,3072]{2,1,0:T(8,128)(2,1)}, bf16[2,256,3072]{2,1,0:T(8,128)(2,1)}, u32[]{:S(2)}, u32[]{:S(2)}) collective-permute-start(bf16[2,256,3072]{2,1,0:T(8,128)(2,1)} %constant_dynamic-update-slice_fusion), channel_id=1, source_target_pairs={{0,1},{1,0},{2,3},{3,2},{4,5},{5,4},{6,7},{7,6},{8,9},{9,8},{10,11... | collective-permute-start | bytes 9437192 | tf_op jit(solution)/shard_map/ppermute | solution.py:384
  15.6 47.6 %collective-permute-start.1 = (bf16[2,256,3072]{2,1,0:T(8,128)(2,1)}, bf16[2,256,3072]{2,1,0:T(8,128)(2,1)}, u32[]{:S(2)}, u32[]{:S(2)}) collective-permute-start(bf16[2,256,3072]{2,1,0:T(8,128)(2,1)} %constant_dynamic-update-slice_fusion), channel_id=1, source_target_pairs={{1,2},{3,4},{5,6},{7,8},{9,10},{11,12},{13,14},{2,1},{4,3},{6,5},{... | collective-permute-start | bytes 9437192 | tf_op jit(solution)/shard_map/ppermute | solution.py:393
  21.5 60.7 %collective-permute-start.12 = (bf16[384,1536]{1,0:T(8,128)(2,1)S(1)}, bf16[384,1536]{1,0:T(8,128)(2,1)S(1)}, u32[]{:S(2)}, u32[]{:S(2)}) collective-permute-start(bf16[384,1536]{1,0:T(8,128)(2,1)S(1)} %copy-done.4), channel_id=1, source_target_pairs={{0,64},{64,0},{1,65},{65,1},{2,66},{66,2},{3,67},{67,3},{4,68},{68... | collective-permute-start | bytes 3538952 | tf_op jit(solution)/shard_map/ppermute | solution.py:384
  33.6 32.2 %collective-permute-start.3 = (bf16[64,3072]{1,0:T(8,128)(2,1)}, bf16[64,3072]{1,0:T(8,128)(2,1)S(1)}, u32[]{:S(2)}, u32[]{:S(2)}) collective-permute-start(bf16[64,3072]{1,0:T(8,128)(2,1)} %get-tuple-element.37), channel_id=1, source_target_pairs={{0,2},{2,4},{4,6},{6,0},{1,3},{3,5},{5,7},{7,1},{8,10},{10,12},{12... | collective-permute-start | bytes 1179656 | tf_op jit(solution)/shard_map/ppermute | solution.py:384
  34.9 38.1 %collective-permute-start.4 = (bf16[64,3072]{1,0:T(8,128)(2,1)}, bf16[64,3072]{1,0:T(8,128)(2,1)S(1)}, u32[]{:S(2)}, u32[]{:S(2)}) collective-permute-start(bf16[64,3072]{1,0:T(8,128)(2,1)} %get-tuple-element.38), channel_id=1, source_target_pairs={{0,4},{2,6},{4,0},{6,2},{1,5},{3,7},{5,1},{7,3},{8,12},{10,14},{12... | collective-permute-start | bytes 1179656 | tf_op jit(solution)/shard_map/ppermute | solution.py:384
  37.8 41.5 %collective-permute-start.5 = (bf16[64,3072]{1,0:T(8,128)(2,1)}, bf16[64,3072]{1,0:T(8,128)(2,1)S(1)}, u32[]{:S(2)}, u32[]{:S(2)}) collective-permute-start(bf16[64,3072]{1,0:T(8,128)(2,1)} %get-tuple-element.39), channel_id=1, source_target_pairs={{0,6},{2,0},{4,2},{6,4},{1,7},{3,1},{5,3},{7,5},{8,14},{10,8},{12,... | collective-permute-start | bytes 1179656 | tf_op jit(solution)/shard_map/ppermute | solution.py:384
  83.2 129.2 %reduce-scatter.2.cloned.1.call-start = ((), (), s32[]{:S(2)}) async-start(), calls=%async_computation.3 | async-start | bytes 983040 | tf_op jit(solution)/shard_map/reduce_scatter | solution.py:457
  83.4 15.2 %collective-permute-start.6 = (bf16[64,3072]{1,0:T(8,128)(2,1)S(1)}, bf16[64,3072]{1,0:T(8,128)(2,1)S(1)}, u32[]{:S(2)}, u32[]{:S(2)}) collective-permute-start(bf16[64,3072]{1,0:T(8,128)(2,1)S(1)} %copy-done.7), channel_id=1, source_target_pairs={{0,8},{8,0},{1,9},{9,1},{2,10},{10,2},{3,11},{11,3},{4,12},{12,4},... | collective-permute-start | bytes 1179656 | tf_op jit(solution)/shard_map/ppermute | solution.py:384
  94.3 28.1 %collective-permute-start.10 = (bf16[256,1536]{1,0:T(8,128)(2,1)}, bf16[256,1536]{1,0:T(8,128)(2,1)S(1)}, u32[]{:S(2)}, u32[]{:S(2)}) collective-permute-start(bf16[256,1536]{1,0:T(8,128)(2,1)} %get-tuple-element.41), channel_id=1, source_target_pairs={{0,1},{1,0},{2,3},{3,2},{4,5},{5,4},{6,7},{7,6},{8,9},{9,8},{10,11... | collective-permute-start | bytes 2359304 | tf_op jit(solution)/shard_map/ppermute | solution.py:384
  101.3 20.8 %collective-permute-start.9 = (bf16[64,3072]{1,0:T(8,128)(2,1)}, bf16[64,3072]{1,0:T(8,128)(2,1)S(1)}, u32[]{:S(2)}, u32[]{:S(2)}) collective-permute-start(bf16[64,3072]{1,0:T(8,128)(2,1)} %pick.3.refs_0_), channel_id=1, source_target_pairs={{0,2},{2,4},{4,6},{6,0},{1,3},{3,5},{5,7},{7,1},{8,10},{10,12},{12... | collective-permute-start | bytes 1179656 | tf_op jit(solution)/shard_map/ppermute | solution.py:384
  101.3 20.8 %collective-permute-start.8 = (bf16[64,3072]{1,0:T(8,128)(2,1)}, bf16[64,3072]{1,0:T(8,128)(2,1)S(1)}, u32[]{:S(2)}, u32[]{:S(2)}) collective-permute-start(bf16[64,3072]{1,0:T(8,128)(2,1)} %pick.3.refs_0_), channel_id=1, source_target_pairs={{0,4},{2,6},{4,0},{6,2},{1,5},{3,7},{5,1},{7,3},{8,12},{10,14},{12... | collective-permute-start | bytes 1179656 | tf_op jit(solution)/shard_map/ppermute | solution.py:384
  102.3 20.1 %collective-permute-start.7 = (bf16[64,3072]{1,0:T(8,128)(2,1)}, bf16[64,3072]{1,0:T(8,128)(2,1)S(1)}, u32[]{:S(2)}, u32[]{:S(2)}) collective-permute-start(bf16[64,3072]{1,0:T(8,128)(2,1)} %pick.3.refs_0_), channel_id=1, source_target_pairs={{0,6},{2,0},{4,2},{6,4},{1,7},{3,1},{5,3},{7,5},{8,14},{10,8},{12,... | collective-permute-start | bytes 1179656 | tf_op jit(solution)/shard_map/ppermute | solution.py:384
  156.2 27.3 %collective-permute-start.16 = (bf16[2,256,1536]{2,1,0:T(8,128)(2,1)}, bf16[2,256,1536]{2,1,0:T(8,128)(2,1)}, u32[]{:S(2)}, u32[]{:S(2)}) collective-permute-start(bf16[2,256,1536]{2,1,0:T(8,128)(2,1)} %get-tuple-element.52), channel_id=1, source_target_pairs={{0,1},{1,0},{2,3},{3,2},{4,5},{5,4},{6,7},{7,6},{8,9},{9,8},{10,11... | collective-permute-start | bytes 4718600 | tf_op jit(solution)/shard_map/ppermute | solution.py:384
  156.6 28.6 %collective-permute-start.17 = (bf16[2,256,1536]{2,1,0:T(8,128)(2,1)}, bf16[2,256,1536]{2,1,0:T(8,128)(2,1)}, u32[]{:S(2)}, u32[]{:S(2)}) collective-permute-start(bf16[2,256,1536]{2,1,0:T(8,128)(2,1)} %get-tuple-element.53), channel_id=1, source_target_pairs={{1,2},{3,4},{5,6},{7,8},{9,10},{11,12},{13,14},{2,1},{4,3},{6,5},{... | collective-permute-start | bytes 4718600 | tf_op jit(solution)/shard_map/ppermute | solution.py:393
  179.6 35.1 %collective-permute-start.21 = (bf16[2,256,1536]{2,1,0:T(8,128)(2,1)}, bf16[2,256,1536]{2,1,0:T(8,128)(2,1)S(1)}, u32[]{:S(2)}, u32[]{:S(2)}) collective-permute-start(bf16[2,256,1536]{2,1,0:T(8,128)(2,1)} %get-tuple-element.58), channel_id=1, source_target_pairs={{0,1},{1,0},{2,3},{3,2},{4,5},{5,4},{6,7},{7,6},{8,9},{9,8},{10,11... | collective-permute-start | bytes 4718600 | tf_op jit(solution)/shard_map/ppermute | solution.py:384
  179.7 35.0 %collective-permute-start.22 = (bf16[2,256,1536]{2,1,0:T(8,128)(2,1)}, bf16[2,256,1536]{2,1,0:T(8,128)(2,1)}, u32[]{:S(2)}, u32[]{:S(2)}) collective-permute-start(bf16[2,256,1536]{2,1,0:T(8,128)(2,1)} %get-tuple-element.59), channel_id=1, source_target_pairs={{1,2},{3,4},{5,6},{7,8},{9,10},{11,12},{13,14},{2,1},{4,3},{6,5},{... | collective-permute-start | bytes 4718600 | tf_op jit(solution)/shard_map/ppermute | solution.py:393
  189.0 23.5 %collective-permute-start.18 = (bf16[64,1536]{1,0:T(8,128)(2,1)}, bf16[64,1536]{1,0:T(8,128)(2,1)S(1)}, u32[]{:S(2)}, u32[]{:S(2)}) collective-permute-start(bf16[64,1536]{1,0:T(8,128)(2,1)} %get-tuple-element.55), channel_id=1, source_target_pairs={{0,2},{2,4},{4,6},{6,0},{1,3},{3,5},{5,7},{7,1},{8,10},{10,12},{12... | collective-permute-start | bytes 589832 | tf_op jit(solution)/shard_map/ppermute | solution.py:384
  190.5 23.3 %collective-permute-start.19 = (bf16[64,1536]{1,0:T(8,128)(2,1)}, bf16[64,1536]{1,0:T(8,128)(2,1)S(1)}, u32[]{:S(2)}, u32[]{:S(2)}) collective-permute-start(bf16[64,1536]{1,0:T(8,128)(2,1)} %get-tuple-element.56), channel_id=1, source_target_pairs={{0,4},{2,6},{4,0},{6,2},{1,5},{3,7},{5,1},{7,3},{8,12},{10,14},{12... | collective-permute-start | bytes 589832 | tf_op jit(solution)/shard_map/ppermute | solution.py:384
  195.8 18.9 %collective-permute-start.20 = (bf16[64,1536]{1,0:T(8,128)(2,1)}, bf16[64,1536]{1,0:T(8,128)(2,1)S(1)}, u32[]{:S(2)}, u32[]{:S(2)}) collective-permute-start(bf16[64,1536]{1,0:T(8,128)(2,1)} %get-tuple-element.57), channel_id=1, source_target_pairs={{0,6},{2,0},{4,2},{6,4},{1,7},{3,1},{5,3},{7,5},{8,14},{10,8},{12,... | collective-permute-start | bytes 589832 | tf_op jit(solution)/shard_map/ppermute | solution.py:384
  233.8 14.6 %collective-permute-start.25 = (bf16[64,3072]{1,0:T(8,128)(2,1)}, bf16[64,3072]{1,0:T(8,128)(2,1)S(1)}, u32[]{:S(2)}, u32[]{:S(2)}) collective-permute-start(bf16[64,3072]{1,0:T(8,128)(2,1)} %add.50.rest_2_.refs_0_), channel_id=1, source_target_pairs={{0,4},{2,6},{4,0},{6,2},{1,5},{3,7},{5,1},{7,3},{8,12},{10,14},{12... | collective-permute-start | bytes 1179656 | tf_op jit(solution)/shard_map/ppermute | solution.py:384
  233.8 20.5 %collective-permute-start.26 = (bf16[64,3072]{1,0:T(8,128)(2,1)}, bf16[64,3072]{1,0:T(8,128)(2,1)S(1)}, u32[]{:S(2)}, u32[]{:S(2)}) collective-permute-start(bf16[64,3072]{1,0:T(8,128)(2,1)} %add.50.rest_2_.refs_0_), channel_id=1, source_target_pairs={{0,2},{2,4},{4,6},{6,0},{1,3},{3,5},{5,7},{7,1},{8,10},{10,12},{12... | collective-permute-start | bytes 1179656 | tf_op jit(solution)/shard_map/ppermute | solution.py:384
  236.6 18.5 %collective-permute-start.24 = (bf16[64,3072]{1,0:T(8,128)(2,1)}, bf16[64,3072]{1,0:T(8,128)(2,1)S(1)}, u32[]{:S(2)}, u32[]{:S(2)}) collective-permute-start(bf16[64,3072]{1,0:T(8,128)(2,1)} %add.50.rest_2_.refs_0_), channel_id=1, source_target_pairs={{0,6},{2,0},{4,2},{6,4},{1,7},{3,1},{5,3},{7,5},{8,14},{10,8},{12,... | collective-permute-start | bytes 1179656 | tf_op jit(solution)/shard_map/ppermute | solution.py:384
  (42 other events, 137.0 us)
Sparse Core Ops, SparseCore 0:
  10.3 56.0 all-gather.2
  83.3 57.3 all-gather.4
  161.9 50.4 reduce-scatter.1

commit v5 on v4

--- a/solution.py
+++ b/solution.py
@@ -93,16 +93,17 @@
 
 
 def attention_kernel(
-    terms, rolled, info, q_ref, ko_ref, vo_ref, inner_ref, outer_ref, held_ref, theirs_ref, *rest
+    terms, rolled, info, q_ref, ko_ref, vo_ref, inner_ref, outer_ref, *rest
 ):
-    ga_refs = rest[:terms]
+    parts, ga_refs = rest[:8], rest[8 : 8 + terms]
     att_ref, gq_ref, own_ref, tin_ref, tout_ref, keep_ref, send_ref = rest[-7:]
     core, y = info[3], info[5]
     heads = []
     for a in range(PAIR):
         c = slice(a * HD, (a + 1) * HD)
         ga = functools.reduce(jnp.add, [ref[:, c].astype(F32) for ref in ga_refs]).astype(BF16)
-        held, theirs = held_ref[:, c], theirs_ref[:, c]
+        held = jnp.concatenate([ref[:, c] for ref in parts[:4]], axis=0)
+        theirs = jnp.concatenate([ref[:, c] for ref in parts[4:]], axis=0)
         keys = [ko_ref[:, c], inner_ref[0, :, c], outer_ref[0, :, c], jnp.where(core == 0, held, theirs)]
         values = [vo_ref[:, c], inner_ref[1, :, c], outer_ref[1, :, c], jnp.where(core == 0, theirs, held)]
         heads.append(one_head(info, q_ref[:, c], keys, values, ga))
@@ -148,7 +149,7 @@
     in_specs = (
         [pl.BlockSpec(one, head)] * 3
         + [pl.BlockSpec(two, heads)] * 2
-        + [pl.BlockSpec(one, head)] * 2
+        + [pl.BlockSpec((PART, wide), head)] * 8
         + [pl.BlockSpec(one, col)] * len(ga)
         + [ANY] * (len(prior) + len(after))
     )
@@ -164,7 +165,7 @@
             num_scalar_prefetch=1, grid=(steps,), in_specs=in_specs, out_specs=out_specs
         ),
         out_shape=[full, full, stacked, stacked, stacked, single, single],
-        input_output_aliases={8 + len(ga) + i: i for i in range(len(prior))},
+        input_output_aliases={14 + len(ga) + i: i for i in range(len(prior))},
         compiler_params=pltpu.CompilerParams(vmem_limit_bytes=VMEM),
         cost_estimate=pl.CostEstimate(
             flops=count * 12 * BLK * 4 * BLK * HD,
@@ -391,25 +392,6 @@
 def swap_outer(x):
     route = [(i, i + 1) for i in range(1, 15, 2)] + [(i + 1, i) for i in range(1, 15, 2)]
     return lax.ppermute(x, SKY, route)
-
-
-def join_kernel(*refs):
-    for r in range(4):
-        refs[-1][r * PART : (r + 1) * PART] = refs[r][...]
-
-
-def join(parts, after):
-    wide = D // 2
-    return pl.pallas_call(
-        join_kernel,
-        grid=(2,),
-        in_specs=[pl.BlockSpec((PART, wide), lambda t: (0, t))] * 4 + [ANY] * len(after),
-        out_specs=pl.BlockSpec((BLK, wide), lambda t: (0, t)),
-        out_shape=jax.ShapeDtypeStruct((BLK, D), BF16),
-        compiler_params=pltpu.CompilerParams(vmem_limit_bytes=VMEM),
-        cost_estimate=pl.CostEstimate(flops=0, bytes_accessed=BLK * D * 4, transcendentals=0),
-        name="join",
-    )(*parts, *after)
 
 
 def local(queries, key_states, value_states, key_blocks, global_block, w_out, grad_out):
@@ -445,12 +427,13 @@
     other = move(mine, "x_hi", 1, 2)
     quarter = pick((root_x - x) % 2, (mine, other), (ga_own,))
     ga_near = (ga_own, swap_core(ga_core))
-    held = join([quarter] + [move(quarter, "y", -r, 4) for r in range(1, 4)], ga_near)
-    rows = (q, k, v, inner, outer, held, swap_core(held))
+    held = [quarter] + [move(quarter, "y", -r, 4) for r in range(1, 4)]
+    held[2] = hold(held[2], ga_near)
+    rows = (q, k, v, inner, outer, *held, *[swap_core(h) for h in held])
 
     out = attention(0, 0, CHUNK, info, rows, ga_near, (), ())
     att, gq, own0, tin0, tout0, keep, send = out
-    ga_own, ga_core = project(go_mine[None], go_core[None], (0, 0), far, (held,))
+    ga_own, ga_core = project(go_mine[None], go_core[None], (0, 0), far, tuple(held))
     ga_far = (ga_own, swap_core(ga_core))
     rin0, rout0 = swap_core(tin0), swap_outer(tout0)
     both0 = add(keep, swap_core(send))

time: 272 us -> 268 us (0.985)
    ppermute x28 -> x31, waiting for transfers between devices: 56.9 us -> 56 us  [move(): return lax.ppermute(x, axis, [(i, (i + step) % size) for i in range(size)])]
    ppermute x28 -> x31, starting transfers between devices: 36.9 us -> 37.5 us  [move(): return lax.ppermute(x, axis, [(i, (i + step) % size) for i in range(size)])]
    unnamed x65 -> x71, local copies, waits for them, and re-layouts: 16.3 us -> 16 us
  transfers between devices with their start and end apart: 34 -> 37, of which waited for: 16 -> 15; matrix products, arithmetic and copies ran while one was open for 3% -> 3% of each run, Pallas kernels for 27% -> 27%
where the time goes in v5:
time: 268 us
  waiting for transfers between devices  97.4 us (36%)
  Pallas kernels  82.5 us (31%)
  starting transfers between devices  46.5 us (17%)
  local copies, waits for them, and re-layouts  22.4 us (8%)
  between operations  18.7 us (7%)
    ppermute x31, waiting for transfers between devices, move(): return lax.ppermute(x, axis, [(i, (i + step) % size) for i in range(size)])  56 us
    ppermute x31, starting transfers between devices, move(): return lax.ppermute(x, axis, [(i, (i + step) % size) for i in range(size)])  37.5 us
    pallas_call x2, Pallas kernels, attention(): pl.pallas_call(functools.partial(attention_kernel, len(ga), part == 0), g...  35.1 us
    ppermute x3, waiting for transfers between devices, swap_outer(): return lax.ppermute(x, SKY, route)  25.4 us
    unnamed x71, local copies, waits for them, and re-layouts  16 us
    reduce_scatter x1, waiting for transfers between devices, local(): quarter0 = lax.psum_scatter(both0, 'y', scatter_dimension=0, tiled=True)  16 us
    pallas_call x2, Pallas kernels, project(): pl.pallas_call(project_kernel, grid=(width // ROWS,), in_specs=[first, se...  13.6 us
    pallas_call x2, Pallas kernels, combine(): pl.pallas_call(combine_kernel, grid_spec=pltpu.PrefetchScalarGridSpec(num...  9.92 us
  transfers between devices with their start and end apart: 37, of which 15 were waited for; matrix products, arithmetic and copies ran while one was open for 3% of the time, Pallas kernels for 27%

profile of v5, /device:TPU:1, one launch (start us, length us, event | category | flops | bytes accessed | tf_op | source)
XLA Modules:
  0.0 267.5 jit_solution(3147260831604623132)
XLA Ops:
  10.0 2.8 %constant_dynamic-update-slice_fusion.1 = bf16[2,256,3072]{2,1,0:T(8,128)(2,1)} fusion(bf16[1,256,3072]{2,1,0:T(8,128)(2,1)} %param.8), kind=kLoop, calls=%fused_computation.2 | loop fusion | bytes 3145728
  15.5 3.2 %collective-permute-start.1 = (bf16[2,256,3072]{2,1,0:T(8,128)(2,1)}, bf16[2,256,3072]{2,1,0:T(8,128)(2,1)}, u32[]{:S(2)}, u32[]{:S(2)}) collective-permute-start(bf16[2,256,3072]{2,1,0:T(8,128)(2,1)} %constant_dynamic-update-slice_fusion), channel_id=1, source_target_pairs={{1,2},{3,4},{5,6},{7,8},{9,10},{11,12},{13,14},{2,1},{4,3},{6,5},{... | collective-permute-start | bytes 9437192 | tf_op jit(solution)/shard_map/ppermute | solution.py:394
  29.5 4.5 %pack.1 = (bf16[64,3072]{1,0:T(8,128)(2,1)}, bf16[64,3072]{1,0:T(8,128)(2,1)}, bf16[64,3072]{1,0:T(8,128)(2,1)}, bf16[64,3072]{1,0:T(8,128)(2,1)}) custom-call(s32[9]{0:T(128)} %stack.58.info, bf16[256,3072]{1,0:T(8,128)(2,1)} %bitcast.32, bf16[256,3072]{1,0:T(8,128)(2,1)} %bitcast.35, bf16[2,256,3072]{2,1,0:T(8,128)(2,1)} %collective-permute-done.inner_ref, ...), custom_call_target="tpu_custom_call" | custom-call | bytes 7864320 | tf_op jit(solution)/shard_map/pack/pallas_call | solution.py:344
  35.3 2.9 %collective-permute-start.4 = (bf16[64,3072]{1,0:T(8,128)(2,1)}, bf16[64,3072]{1,0:T(8,128)(2,1)S(1)}, u32[]{:S(2)}, u32[]{:S(2)}) collective-permute-start(bf16[64,3072]{1,0:T(8,128)(2,1)} %get-tuple-element.38), channel_id=1, source_target_pairs={{0,4},{2,6},{4,0},{6,2},{1,5},{3,7},{5,1},{7,3},{8,12},{10,14},{12... | collective-permute-start | bytes 1179656 | tf_op jit(solution)/shard_map/ppermute | solution.py:385
  38.7 24.4 %collective-permute-done.1.refs_4_.outer_ref = bf16[2,256,3072]{2,1,0:T(8,128)(2,1)} collective-permute-done((bf16[2,256,3072]{2,1,0:T(8,128)(2,1)}, bf16[2,256,3072]{2,1,0:T(8,128)(2,1)}, u32[]{:S(2)}, u32[]{:S(2)}) %collective-permute-start.1) | collective-permute-done | bytes 3145760 | tf_op jit(solution)/shard_map/ppermute | solution.py:394
  65.8 7.2 %collective-permute-done.4.refs_2_ = bf16[64,3072]{1,0:T(8,128)(2,1)S(1)} collective-permute-done((bf16[64,3072]{1,0:T(8,128)(2,1)}, bf16[64,3072]{1,0:T(8,128)(2,1)S(1)}, u32[]{:S(2)}, u32[]{:S(2)}) %collective-permute-start.4) | collective-permute-done | bytes 393248 | tf_op jit(solution)/shard_map/ppermute | solution.py:385
  73.0 6.4 %collective-permute-done.5.refs_3_ = bf16[64,3072]{1,0:T(8,128)(2,1)S(1)} collective-permute-done((bf16[64,3072]{1,0:T(8,128)(2,1)}, bf16[64,3072]{1,0:T(8,128)(2,1)S(1)}, u32[]{:S(2)}, u32[]{:S(2)}) %collective-permute-start.5) | collective-permute-done | bytes 393248 | tf_op jit(solution)/shard_map/ppermute | solution.py:385
  83.6 4.1 %collective-permute-start.6 = (bf16[64,3072]{1,0:T(8,128)(2,1)S(1)}, bf16[64,3072]{1,0:T(8,128)(2,1)S(1)}, u32[]{:S(2)}, u32[]{:S(2)}) collective-permute-start(bf16[64,3072]{1,0:T(8,128)(2,1)S(1)} %copy-done.7), channel_id=1, source_target_pairs={{0,8},{8,0},{1,9},{9,1},{2,10},{10,2},{3,11},{11,3},{4,12},{12,4},... | collective-permute-start | bytes 1179656 | tf_op jit(solution)/shard_map/ppermute | solution.py:385
  87.7 6.8 %project.2 = (f32[256,1536]{1,0:T(8,128)}, bf16[256,1536]{1,0:T(8,128)(2,1)}) custom-call(bf16[1,256,1536]{2,1,0:T(8,128)(2,1)} %get-tuple-element.68.mine_ref, bf16[1,256,1536]{2,1,0:T(8,128)(2,1)} %bitcast.44, bf16[1536,1536]{1,0:T(8,128)(2,1)} %all-gather.3.cloned.1.call-done.piece_ref, bf16[64,3072]{1,0:T(8,128)(2,1)} %copy-done.22), custom_call_target="tpu_custom_call" | custom-call | flops 2415919104 | bytes 7077888 | tf_op jit(solution)/shard_map/project/pallas_call | solution.py:45
  94.5 4.0 %collective-permute-start.9 = (bf16[256,1536]{1,0:T(8,128)(2,1)}, bf16[256,1536]{1,0:T(8,128)(2,1)S(1)}, u32[]{:S(2)}, u32[]{:S(2)}) collective-permute-start(bf16[256,1536]{1,0:T(8,128)(2,1)} %get-tuple-element.41), channel_id=1, source_target_pairs={{0,1},{1,0},{2,3},{3,2},{4,5},{5,4},{6,7},{7,6},{8,9},{9,8},{10,11... | collective-permute-start | bytes 2359304 | tf_op jit(solution)/shard_map/ppermute | solution.py:385
  104.4 17.6 %collective-permute-done.10.rest_3_ = bf16[64,3072]{1,0:T(8,128)(2,1)S(1)} collective-permute-done((bf16[64,3072]{1,0:T(8,128)(2,1)}, bf16[64,3072]{1,0:T(8,128)(2,1)S(1)}, u32[]{:S(2)}, u32[]{:S(2)}) %collective-permute-start.10) | collective-permute-done | bytes 393248 | tf_op jit(solution)/shard_map/ppermute | solution.py:385
  127.2 17.6 %attention.2 = (bf16[256,3072]{1,0:T(8,128)(2,1)}, bf16[256,3072]{1,0:T(8,128)(2,1)}, bf16[2,256,1536]{2,1,0:T(8,128)(2,1)}, bf16[2,256,1536]{2,1,0:T(8,128)(2,1...) custom-call(s32[9]{0:T(128)} %stack.58.info, bf16[256,3072]{1,0:T(8,128)(2,1)} %bitcast.40, ...), custom_call_target="tpu_custom_call" | custom-call | flops 4831838208 | bytes 16515072 | tf_op jit(solution)/shard_map/attention/pallas_call | solution.py:162
  145.2 6.8 %project.3 = (f32[256,1536]{1,0:T(8,128)}, bf16[256,1536]{1,0:T(8,128)(2,1)}) custom-call(bf16[1,256,1536]{2,1,0:T(8,128)(2,1)} %get-tuple-element.68.mine_ref, bf16[1,256,1536]{2,1,0:T(8,128)(2,1)} %bitcast.45, bf16[1536,1536]{1,0:T(8,128)(2,1)} %all-gather.5.cloned.1.call-done.piece_ref, bf16[64,3072]{1,0:T(8,128)(2,1)} %pick.3.rest_0_, ...), custom_call_target="tpu_custom_call" | custom-call | flops 2415919104 | bytes 7077888 | tf_op jit(solution)/shard_map/project/pallas_call | solution.py:45
  158.8 17.5 %attention.3 = (bf16[256,3072]{1,0:T(8,128)(2,1)}, bf16[256,3072]{1,0:T(8,128)(2,1)}, bf16[2,256,1536]{2,1,0:T(8,128)(2,1)}, bf16[2,256,1536]{2,1,0:T(8,128)(2,1...) custom-call(s32[9]{0:T(128)} %stack.58.info, ...), custom_call_target="tpu_custom_call", output_to_operand_aliasing={{0}: (16, {}), {1}: (17, {})} | custom-call | flops 4831838208 | bytes 16515072 | tf_op jit(solution)/shard_map/attention/pallas_call | solution.py:162
  176.3 3.5 %collective-permute-start.25 = (bf16[2,256,1536]{2,1,0:T(8,128)(2,1)}, bf16[2,256,1536]{2,1,0:T(8,128)(2,1)}, u32[]{:S(2)}, u32[]{:S(2)}) collective-permute-start(bf16[2,256,1536]{2,1,0:T(8,128)(2,1)} %get-tuple-element.59), channel_id=1, source_target_pairs={{1,2},{3,4},{5,6},{7,8},{9,10},{11,12},{13,14},{2,1},{4,3},{6,5},{... | collective-permute-start | bytes 4718600 | tf_op jit(solution)/shard_map/ppermute | solution.py:394
  187.6 5.0 %collective-permute-start.22 = (bf16[64,1536]{1,0:T(8,128)(2,1)}, bf16[64,1536]{1,0:T(8,128)(2,1)S(1)}, u32[]{:S(2)}, u32[]{:S(2)}) collective-permute-start(bf16[64,1536]{1,0:T(8,128)(2,1)} %get-tuple-element.56), channel_id=1, source_target_pairs={{0,4},{2,6},{4,0},{6,2},{1,5},{3,7},{5,1},{7,3},{8,12},{10,14},{12... | collective-permute-start | bytes 589832 | tf_op jit(solution)/shard_map/ppermute | solution.py:385
  192.6 16.0 %reduce-scatter.2.cloned.1.call-done.first_ref = bf16[64,1536]{1,0:T(8,128)(2,1)} async-done(((bf16[256,1536]{1,0:T(8,128)(2,1)}), bf16[64,1536]{1,0:T(8,128)(2,1)}) %reduce-scatter.2.cloned.1.call-update) | async-done | bytes 196624 | tf_op jit(solution)/shard_map/reduce_scatter | solution.py:440
  214.9 3.7 %collective-permute-start.26 = (bf16[64,3072]{1,0:T(8,128)(2,1)}, bf16[64,3072]{1,0:T(8,128)(2,1)S(1)}, u32[]{:S(2)}, u32[]{:S(2)}) collective-permute-start(bf16[64,3072]{1,0:T(8,128)(2,1)} %gather.1.a_ref.rest_0_), channel_id=1, source_target_pairs={{0,8},{8,0},{1,9},{9,1},{2,10},{10,2},{3,11},{11,3},{4,12},{12,4},... | collective-permute-start | bytes 1179656 | tf_op jit(solution)/shard_map/ppermute | solution.py:385
  218.6 9.3 %collective-permute-done.26.b_ref = bf16[64,3072]{1,0:T(8,128)(2,1)S(1)} collective-permute-done((bf16[64,3072]{1,0:T(8,128)(2,1)}, bf16[64,3072]{1,0:T(8,128)(2,1)S(1)}, u32[]{:S(2)}, u32[]{:S(2)}) %collective-permute-start.26) | collective-permute-done | bytes 393248 | tf_op jit(solution)/shard_map/ppermute | solution.py:385
  230.6 2.9 %collective-permute-start.29 = (bf16[64,3072]{1,0:T(8,128)(2,1)}, bf16[64,3072]{1,0:T(8,128)(2,1)S(1)}, u32[]{:S(2)}, u32[]{:S(2)}) collective-permute-start(bf16[64,3072]{1,0:T(8,128)(2,1)} %add.50.rest_2_.refs_0_), channel_id=1, source_target_pairs={{0,2},{2,4},{4,6},{6,0},{1,3},{3,5},{5,7},{7,1},{8,10},{10,12},{12... | collective-permute-start | bytes 1179656 | tf_op jit(solution)/shard_map/ppermute | solution.py:385
  233.5 5.0 %combine.2 = (bf16[256,3072]{1,0:T(8,128)(2,1)}, bf16[256,3072]{1,0:T(8,128)(2,1)}) custom-call(s32[9]{0:T(128)} %stack.58.info, bf16[2,256,1536]{2,1,0:T(8,128)(2,1)} %get-tuple-element.61.own_ref, bf16[2,256,1536]{2,1,0:T(8,128)(2,1)} %collective-permute-done.19.rest_0_.rin_ref, bf16[2,256,1536]{2,1,0:T(8,128)(2,1)} %collective-permute-done.20.rest_1_.rout_ref, ...), custom_call_target="tpu_custom_call" | custom-call | flops 1572864 | bytes 6291456 | tf_op jit(solution)/shard_map/combine/pallas_call | solution.py:191
  240.3 4.9 %combine.3 = (bf16[256,3072]{1,0:T(8,128)(2,1)}, bf16[256,3072]{1,0:T(8,128)(2,1)}) custom-call(s32[9]{0:T(128)} %stack.58.info, bf16[2,256,1536]{2,1,0:T(8,128)(2,1)} %get-tuple-element.60.own_ref, bf16[2,256,1536]{2,1,0:T(8,128)(2,1)} %copy-done.3, ...), custom_call_target="tpu_custom_call", output_to_operand_aliasing={{0}: (4, {}), {1}: (5, {})} | custom-call | flops 1572864 | bytes 6291456 | tf_op jit(solution)/shard_map/combine/pallas_call | solution.py:191
  246.1 5.0 %collective-permute-done.29.refs_3_ = bf16[64,3072]{1,0:T(8,128)(2,1)S(1)} collective-permute-done((bf16[64,3072]{1,0:T(8,128)(2,1)}, bf16[64,3072]{1,0:T(8,128)(2,1)S(1)}, u32[]{:S(2)}, u32[]{:S(2)}) %collective-permute-start.29) | collective-permute-done | bytes 393248 | tf_op jit(solution)/shard_map/ppermute | solution.py:385
  254.2 6.7 %finish.1 = (bf16[256,3072]{1,0:T(8,128)(2,1)}, bf16[256,3072]{1,0:T(8,128)(2,1)}) custom-call(s32[9]{0:T(128)} %stack.58.info, bf16[64,3072]{1,0:T(8,128)(2,1)} %add.50.rest_2_.refs_0_, bf16[64,3072]{1,0:T(8,128)(2,1)} %copy-done.16, bf16[64,3072]{1,0:T(8,128)(2,1)} %hold.5.refs_2_, ...), custom_call_target="tpu_custom_call", output_to_operand_aliasing={{0}: (9, {}), {1}: (10, {})} | custom-call | flops 1572864 | bytes 9437184 | tf_op jit(solution)/shard_map/finish/pallas_call | solution.py:235
  (147 shorter events, 60.9 us)
Async XLA Ops:
  7.2 80.5 %all-gather.3.cloned.1.call-start = ((), (), s32[]{:S(2)}) async-start(), calls=%async_computation.1 | async-start | bytes 5898240 | tf_op jit(solution)/shard_map/all_gather | solution.py:413
  10.0 135.2 %all-gather.5.cloned.1.call-start = ((), (), s32[]{:S(2)}) async-start(), calls=%async_computation.2 | async-start | bytes 5898240 | tf_op jit(solution)/shard_map/all_gather | solution.py:425
  15.5 47.6 %collective-permute-start.1 = (bf16[2,256,3072]{2,1,0:T(8,128)(2,1)}, bf16[2,256,3072]{2,1,0:T(8,128)(2,1)}, u32[]{:S(2)}, u32[]{:S(2)}) collective-permute-start(bf16[2,256,3072]{2,1,0:T(8,128)(2,1)} %constant_dynamic-update-slice_fusion), channel_id=1, source_target_pairs={{1,2},{3,4},{5,6},{7,8},{9,10},{11,12},{13,14},{2,1},{4,3},{6,5},{... | collective-permute-start | bytes 9437192 | tf_op jit(solution)/shard_map/ppermute | solution.py:394
  21.4 61.0 %collective-permute-start.15 = (bf16[384,1536]{1,0:T(8,128)(2,1)S(1)}, bf16[384,1536]{1,0:T(8,128)(2,1)S(1)}, u32[]{:S(2)}, u32[]{:S(2)}) collective-permute-start(bf16[384,1536]{1,0:T(8,128)(2,1)S(1)} %copy-done.4), channel_id=1, source_target_pairs={{0,64},{64,0},{1,65},{65,1},{2,66},{66,2},{3,67},{67,3},{4,68},{68... | collective-permute-start | bytes 3538952 | tf_op jit(solution)/shard_map/ppermute | solution.py:385
  34.0 31.8 %collective-permute-start.3 = (bf16[64,3072]{1,0:T(8,128)(2,1)}, bf16[64,3072]{1,0:T(8,128)(2,1)S(1)}, u32[]{:S(2)}, u32[]{:S(2)}) collective-permute-start(bf16[64,3072]{1,0:T(8,128)(2,1)} %get-tuple-element.37), channel_id=1, source_target_pairs={{0,2},{2,4},{4,6},{6,0},{1,3},{3,5},{5,7},{7,1},{8,10},{10,12},{12... | collective-permute-start | bytes 1179656 | tf_op jit(solution)/shard_map/ppermute | solution.py:385
  35.3 37.6 %collective-permute-start.4 = (bf16[64,3072]{1,0:T(8,128)(2,1)}, bf16[64,3072]{1,0:T(8,128)(2,1)S(1)}, u32[]{:S(2)}, u32[]{:S(2)}) collective-permute-start(bf16[64,3072]{1,0:T(8,128)(2,1)} %get-tuple-element.38), channel_id=1, source_target_pairs={{0,4},{2,6},{4,0},{6,2},{1,5},{3,7},{5,1},{7,3},{8,12},{10,14},{12... | collective-permute-start | bytes 1179656 | tf_op jit(solution)/shard_map/ppermute | solution.py:385
  38.2 41.2 %collective-permute-start.5 = (bf16[64,3072]{1,0:T(8,128)(2,1)}, bf16[64,3072]{1,0:T(8,128)(2,1)S(1)}, u32[]{:S(2)}, u32[]{:S(2)}) collective-permute-start(bf16[64,3072]{1,0:T(8,128)(2,1)} %get-tuple-element.39), channel_id=1, source_target_pairs={{0,6},{2,0},{4,2},{6,4},{1,7},{3,1},{5,3},{7,5},{8,14},{10,8},{12,... | collective-permute-start | bytes 1179656 | tf_op jit(solution)/shard_map/ppermute | solution.py:385
  83.4 125.2 %reduce-scatter.2.cloned.1.call-start = ((), (), s32[]{:S(2)}) async-start(), calls=%async_computation.3 | async-start | bytes 983040 | tf_op jit(solution)/shard_map/reduce_scatter | solution.py:440
  83.6 14.9 %collective-permute-start.6 = (bf16[64,3072]{1,0:T(8,128)(2,1)S(1)}, bf16[64,3072]{1,0:T(8,128)(2,1)S(1)}, u32[]{:S(2)}, u32[]{:S(2)}) collective-permute-start(bf16[64,3072]{1,0:T(8,128)(2,1)S(1)} %copy-done.7), channel_id=1, source_target_pairs={{0,8},{8,0},{1,9},{9,1},{2,10},{10,2},{3,11},{11,3},{4,12},{12,4},... | collective-permute-start | bytes 1179656 | tf_op jit(solution)/shard_map/ppermute | solution.py:385
  94.5 28.2 %collective-permute-start.9 = (bf16[256,1536]{1,0:T(8,128)(2,1)}, bf16[256,1536]{1,0:T(8,128)(2,1)S(1)}, u32[]{:S(2)}, u32[]{:S(2)}) collective-permute-start(bf16[256,1536]{1,0:T(8,128)(2,1)} %get-tuple-element.41), channel_id=1, source_target_pairs={{0,1},{1,0},{2,3},{3,2},{4,5},{5,4},{6,7},{7,6},{8,9},{9,8},{10,11... | collective-permute-start | bytes 2359304 | tf_op jit(solution)/shard_map/ppermute | solution.py:385
  101.3 20.8 %collective-permute-start.10 = (bf16[64,3072]{1,0:T(8,128)(2,1)}, bf16[64,3072]{1,0:T(8,128)(2,1)S(1)}, u32[]{:S(2)}, u32[]{:S(2)}) collective-permute-start(bf16[64,3072]{1,0:T(8,128)(2,1)} %pick.3.rest_0_), channel_id=1, source_target_pairs={{0,2},{2,4},{4,6},{6,0},{1,3},{3,5},{5,7},{7,1},{8,10},{10,12},{12... | collective-permute-start | bytes 1179656 | tf_op jit(solution)/shard_map/ppermute | solution.py:385
  101.3 21.4 %collective-permute-start.7 = (bf16[64,3072]{1,0:T(8,128)(2,1)}, bf16[64,3072]{1,0:T(8,128)(2,1)S(1)}, u32[]{:S(2)}, u32[]{:S(2)}) collective-permute-start(bf16[64,3072]{1,0:T(8,128)(2,1)} %pick.3.rest_0_), channel_id=1, source_target_pairs={{0,6},{2,0},{4,2},{6,4},{1,7},{3,1},{5,3},{7,5},{8,14},{10,8},{12,... | collective-permute-start | bytes 1179656 | tf_op jit(solution)/shard_map/ppermute | solution.py:385
  103.9 18.8 %collective-permute-start.8 = (bf16[64,3072]{1,0:T(8,128)(2,1)}, bf16[64,3072]{1,0:T(8,128)(2,1)S(1)}, u32[]{:S(2)}, u32[]{:S(2)}) collective-permute-start(bf16[64,3072]{1,0:T(8,128)(2,1)} %pick.3.rest_0_), channel_id=1, source_target_pairs={{0,4},{2,6},{4,0},{6,2},{1,5},{3,7},{5,1},{7,3},{8,12},{10,14},{12... | collective-permute-start | bytes 1179656 | tf_op jit(solution)/shard_map/ppermute | solution.py:385
  103.9 20.9 %collective-permute-start.11 = (bf16[64,3072]{1,0:T(8,128)(2,1)}, bf16[64,3072]{1,0:T(8,128)(2,1)S(1)}, u32[]{:S(2)}, u32[]{:S(2)}) collective-permute-start(bf16[64,3072]{1,0:T(8,128)(2,1)} %pick.3.rest_0_), channel_id=1, source_target_pairs={{0,1},{1,0},{2,3},{3,2},{4,5},{5,4},{6,7},{7,6},{8,9},{9,8},{10,11... | collective-permute-start | bytes 1179656 | tf_op jit(solution)/shard_map/ppermute | solution.py:385
  152.2 27.8 %collective-permute-start.19 = (bf16[2,256,1536]{2,1,0:T(8,128)(2,1)}, bf16[2,256,1536]{2,1,0:T(8,128)(2,1)}, u32[]{:S(2)}, u32[]{:S(2)}) collective-permute-start(bf16[2,256,1536]{2,1,0:T(8,128)(2,1)} %get-tuple-element.52), channel_id=1, source_target_pairs={{0,1},{1,0},{2,3},{3,2},{4,5},{5,4},{6,7},{7,6},{8,9},{9,8},{10,11... | collective-permute-start | bytes 4718600 | tf_op jit(solution)/shard_map/ppermute | solution.py:385
  152.5 28.5 %collective-permute-start.20 = (bf16[2,256,1536]{2,1,0:T(8,128)(2,1)}, bf16[2,256,1536]{2,1,0:T(8,128)(2,1)}, u32[]{:S(2)}, u32[]{:S(2)}) collective-permute-start(bf16[2,256,1536]{2,1,0:T(8,128)(2,1)} %get-tuple-element.53), channel_id=1, source_target_pairs={{1,2},{3,4},{5,6},{7,8},{9,10},{11,12},{13,14},{2,1},{4,3},{6,5},{... | collective-permute-start | bytes 4718600 | tf_op jit(solution)/shard_map/ppermute | solution.py:394
  176.3 35.3 %collective-permute-start.24 = (bf16[2,256,1536]{2,1,0:T(8,128)(2,1)}, bf16[2,256,1536]{2,1,0:T(8,128)(2,1)S(1)}, u32[]{:S(2)}, u32[]{:S(2)}) collective-permute-start(bf16[2,256,1536]{2,1,0:T(8,128)(2,1)} %get-tuple-element.58), channel_id=1, source_target_pairs={{0,1},{1,0},{2,3},{3,2},{4,5},{5,4},{6,7},{7,6},{8,9},{9,8},{10,11... | collective-permute-start | bytes 4718600 | tf_op jit(solution)/shard_map/ppermute | solution.py:385
  176.3 35.2 %collective-permute-start.25 = (bf16[2,256,1536]{2,1,0:T(8,128)(2,1)}, bf16[2,256,1536]{2,1,0:T(8,128)(2,1)}, u32[]{:S(2)}, u32[]{:S(2)}) collective-permute-start(bf16[2,256,1536]{2,1,0:T(8,128)(2,1)} %get-tuple-element.59), channel_id=1, source_target_pairs={{1,2},{3,4},{5,6},{7,8},{9,10},{11,12},{13,14},{2,1},{4,3},{6,5},{... | collective-permute-start | bytes 4718600 | tf_op jit(solution)/shard_map/ppermute | solution.py:394
  185.5 23.1 %collective-permute-start.21 = (bf16[64,1536]{1,0:T(8,128)(2,1)}, bf16[64,1536]{1,0:T(8,128)(2,1)S(1)}, u32[]{:S(2)}, u32[]{:S(2)}) collective-permute-start(bf16[64,1536]{1,0:T(8,128)(2,1)} %get-tuple-element.55), channel_id=1, source_target_pairs={{0,2},{2,4},{4,6},{6,0},{1,3},{3,5},{5,7},{7,1},{8,10},{10,12},{12... | collective-permute-start | bytes 589832 | tf_op jit(solution)/shard_map/ppermute | solution.py:385
  187.6 23.0 %collective-permute-start.22 = (bf16[64,1536]{1,0:T(8,128)(2,1)}, bf16[64,1536]{1,0:T(8,128)(2,1)S(1)}, u32[]{:S(2)}, u32[]{:S(2)}) collective-permute-start(bf16[64,1536]{1,0:T(8,128)(2,1)} %get-tuple-element.56), channel_id=1, source_target_pairs={{0,4},{2,6},{4,0},{6,2},{1,5},{3,7},{5,1},{7,3},{8,12},{10,14},{12... | collective-permute-start | bytes 589832 | tf_op jit(solution)/shard_map/ppermute | solution.py:385
  192.6 19.0 %collective-permute-start.23 = (bf16[64,1536]{1,0:T(8,128)(2,1)}, bf16[64,1536]{1,0:T(8,128)(2,1)S(1)}, u32[]{:S(2)}, u32[]{:S(2)}) collective-permute-start(bf16[64,1536]{1,0:T(8,128)(2,1)} %get-tuple-element.57), channel_id=1, source_target_pairs={{0,6},{2,0},{4,2},{6,4},{1,7},{3,1},{5,3},{7,5},{8,14},{10,8},{12,... | collective-permute-start | bytes 589832 | tf_op jit(solution)/shard_map/ppermute | solution.py:385
  230.6 14.6 %collective-permute-start.28 = (bf16[64,3072]{1,0:T(8,128)(2,1)}, bf16[64,3072]{1,0:T(8,128)(2,1)S(1)}, u32[]{:S(2)}, u32[]{:S(2)}) collective-permute-start(bf16[64,3072]{1,0:T(8,128)(2,1)} %add.50.rest_2_.refs_0_), channel_id=1, source_target_pairs={{0,4},{2,6},{4,0},{6,2},{1,5},{3,7},{5,1},{7,3},{8,12},{10,14},{12... | collective-permute-start | bytes 1179656 | tf_op jit(solution)/shard_map/ppermute | solution.py:385
  230.6 20.5 %collective-permute-start.29 = (bf16[64,3072]{1,0:T(8,128)(2,1)}, bf16[64,3072]{1,0:T(8,128)(2,1)S(1)}, u32[]{:S(2)}, u32[]{:S(2)}) collective-permute-start(bf16[64,3072]{1,0:T(8,128)(2,1)} %add.50.rest_2_.refs_0_), channel_id=1, source_target_pairs={{0,2},{2,4},{4,6},{6,0},{1,3},{3,5},{5,7},{7,1},{8,10},{10,12},{12... | collective-permute-start | bytes 1179656 | tf_op jit(solution)/shard_map/ppermute | solution.py:385
  233.5 18.5 %collective-permute-start.27 = (bf16[64,3072]{1,0:T(8,128)(2,1)}, bf16[64,3072]{1,0:T(8,128)(2,1)S(1)}, u32[]{:S(2)}, u32[]{:S(2)}) collective-permute-start(bf16[64,3072]{1,0:T(8,128)(2,1)} %add.50.rest_2_.refs_0_), channel_id=1, source_target_pairs={{0,6},{2,0},{4,2},{6,4},{1,7},{3,1},{5,3},{7,5},{8,14},{10,8},{12,... | collective-permute-start | bytes 1179656 | tf_op jit(solution)/shard_map/ppermute | solution.py:385
  (48 other events, 167.1 us)
Sparse Core Ops, SparseCore 0:
  10.3 56.0 all-gather.2
  83.5 57.0 all-gather.4
  157.9 50.6 reduce-scatter.1

commit v6 on v5

--- a/solution.py
+++ b/solution.py
@@ -160,7 +160,7 @@
     stacked = jax.ShapeDtypeStruct((2, BLK, CHUNK * HD), BF16)
     single = jax.ShapeDtypeStruct((BLK, CHUNK * HD), BF16)
     return pl.pallas_call(
-        functools.partial(attention_kernel, len(ga), part == 0),
+        functools.partial(attention_kernel, len(ga), False),
         grid_spec=pltpu.PrefetchScalarGridSpec(
             num_scalar_prefetch=1, grid=(steps,), in_specs=in_specs, out_specs=out_specs
         ),
@@ -285,27 +285,28 @@
     )(a, b, *after)
 
 
-def gather_kernel(first_ref, *refs):
-    total = functools.reduce(jnp.add, [ref[...].astype(F32) for ref in refs[:4]])
-    width = first_ref.shape[1]
-    refs[-1][:, :width] = first_ref[...]
-    refs[-1][:, width:] = total.astype(BF16)
-
-
-def gather(first, pieces, after):
-    pieces = [pieces[0]] + [move(pieces[r], "y", r, 4) for r in range(1, 4)]
+def gather_kernel(*refs):
+    half = refs[-1].shape[1] // 2
+    for part in range(2):
+        total = functools.reduce(jnp.add, [ref[...].astype(F32) for ref in refs[4 * part : 4 * part + 4]])
+        refs[-1][:, part * half : (part + 1) * half] = total.astype(BF16)
+
+
+def arrive(pieces):
+    return [pieces[0]] + [move(pieces[r], "y", r, 4) for r in range(1, 4)]
+
+
+def gather(first, second, after):
     whole = pl.BlockSpec(memory_space=pltpu.VMEM)
     return pl.pallas_call(
         gather_kernel,
-        in_specs=[whole] * 5 + [ANY] * len(after),
+        in_specs=[whole] * 8 + [ANY] * len(after),
         out_specs=whole,
         out_shape=jax.ShapeDtypeStruct((PART, D), BF16),
         compiler_params=pltpu.CompilerParams(vmem_limit_bytes=VMEM),
-        cost_estimate=pl.CostEstimate(
-            flops=pieces[0].size * 4, bytes_accessed=pieces[0].size * 14, transcendentals=0
-        ),
+        cost_estimate=pl.CostEstimate(flops=PART * D * 4, bytes_accessed=PART * D * 10, transcendentals=0),
         name="gather",
-    )(first, *pieces, *after)
+    )(*first, *second, *after)
 
 
 def hold_kernel(*refs):
@@ -436,14 +437,14 @@
     ga_own, ga_core = project(go_mine[None], go_core[None], (0, 0), far, tuple(held))
     ga_far = (ga_own, swap_core(ga_core))
     rin0, rout0 = swap_core(tin0), swap_outer(tout0)
-    both0 = add(keep, swap_core(send))
-    quarter0 = lax.psum_scatter(both0, "y", scatter_dimension=0, tiled=True)
-
-    out = attention(1, 0, CHUNK, info, rows, ga_far, (att, gq), (both0,))
+    both0 = split(keep, swap_core(send), ())
+    arrived0 = arrive(both0)
+
+    out = attention(1, 0, CHUNK, info, rows, ga_far, (att, gq), tuple(both0))
     att, gq, own1, tin1, tout1, keep, send = out
     rin1, rout1 = swap_core(tin1), swap_outer(tout1)
-    both1 = split(keep, swap_core(send), (rin0, rout0))
-    quarters = gather(quarter0, both1, (rin1, rout1))
+    both1 = split(keep, swap_core(send), (rin0, rout0, *arrived0[1:]))
+    quarters = gather(arrived0, arrive(both1), (rin1, rout1))
     halves = add(quarters, move(quarters, "x_hi", 1, 2))
     grads = combine(0, info, own0, rin0, rout0, (), (quarters,))
     grads = combine(1, info, own1, rin1, rout1, grads, (halves,))

time: 268 us -> 288 us (1.075)
  waiting for transfers between devices: 97.4 us -> 114 us
    ppermute x31 -> x34, waiting for transfers between devices: 56 us -> 89.7 us  [move(): return lax.ppermute(x, axis, [(i, (i + step) % size) for i in range(size)])]
    reduce_scatter x1 -> x0, waiting for transfers between devices: 16 us -> none  [local(): quarter0 = lax.psum_scatter(both0, 'y', scatter_dimension=0, tiled=True)]
    ppermute x31 -> x34, starting transfers between devices: 37.5 us -> 40 us  [move(): return lax.ppermute(x, axis, [(i, (i + step) % size) for i in range(size)])]
    unnamed x71 -> x81, local copies, waits for them, and re-layouts: 16 us -> 16.1 us
  transfers between devices with their start and end apart: 37 -> 39, of which waited for: 15 -> 15; matrix products, arithmetic and copies ran while one was open for 3% -> 3% of each run, Pallas kernels for 27% -> 25%
where the time goes in v6:
time: 288 us; the launch traced here: 287 us
  waiting for transfers between devices  114 us (40%)
  Pallas kernels  82.7 us (29%)
  starting transfers between devices  48.8 us (17%)
  local copies, waits for them, and re-layouts  22.5 us (8%)
  between operations  18.9 us (7%)
    ppermute x34, waiting for transfers between devices, move(): return lax.ppermute(x, axis, [(i, (i + step) % size) for i in range(size)])  89.7 us
    ppermute x34, starting transfers between devices, move(): return lax.ppermute(x, axis, [(i, (i + step) % size) for i in range(size)])  40 us
    pallas_call x2, Pallas kernels, attention(): pl.pallas_call(functools.partial(attention_kernel, len(ga), False), grid_...  35.1 us
    ppermute x3, waiting for transfers between devices, swap_outer(): return lax.ppermute(x, SKY, route)  24.5 us
    unnamed x81, local copies, waits for them, and re-layouts  16.1 us
    pallas_call x2, Pallas kernels, project(): pl.pallas_call(project_kernel, grid=(width // ROWS,), in_specs=[first, se...  13.6 us
    pallas_call x2, Pallas kernels, combine(): pl.pallas_call(combine_kernel, grid_spec=pltpu.PrefetchScalarGridSpec(num...  9.92 us
    ppermute x3, starting transfers between devices, swap_outer(): return lax.ppermute(x, SKY, route)  8.78 us
  transfers between devices with their start and end apart: 39, of which 15 were waited for; matrix products, arithmetic and copies ran while one was open for 3% of the time, Pallas kernels for 25%

profile of v6, /device:TPU:1, one launch (start us, length us, event | category | flops | bytes accessed | tf_op | source)
XLA Modules:
  0.0 287.2 jit_solution(15198720348835920631)
XLA Ops:
  15.5 3.2 %collective-permute-start.1 = (bf16[2,256,3072]{2,1,0:T(8,128)(2,1)}, bf16[2,256,3072]{2,1,0:T(8,128)(2,1)}, u32[]{:S(2)}, u32[]{:S(2)}) collective-permute-start(bf16[2,256,3072]{2,1,0:T(8,128)(2,1)} %constant_dynamic-update-slice_fusion), channel_id=1, source_target_pairs={{1,2},{3,4},{5,6},{7,8},{9,10},{11,12},{13,14},{2,1},{4,3},{6,5},{... | collective-permute-start | bytes 9437192 | tf_op jit(solution)/shard_map/ppermute | solution.py:395
  29.4 4.5 %pack.1 = (bf16[64,3072]{1,0:T(8,128)(2,1)}, bf16[64,3072]{1,0:T(8,128)(2,1)}, bf16[64,3072]{1,0:T(8,128)(2,1)}, bf16[64,3072]{1,0:T(8,128)(2,1)}) custom-call(s32[9]{0:T(128)} %stack.58.info, bf16[256,3072]{1,0:T(8,128)(2,1)} %bitcast.32, bf16[256,3072]{1,0:T(8,128)(2,1)} %bitcast.35, bf16[2,256,3072]{2,1,0:T(8,128)(2,1)} %collective-permute-done.inner_ref, ...), custom_call_target="tpu_custom_call" | custom-call | bytes 7864320 | tf_op jit(solution)/shard_map/pack/pallas_call | solution.py:345
  38.6 24.5 %collective-permute-done.1.refs_4_.outer_ref = bf16[2,256,3072]{2,1,0:T(8,128)(2,1)} collective-permute-done((bf16[2,256,3072]{2,1,0:T(8,128)(2,1)}, bf16[2,256,3072]{2,1,0:T(8,128)(2,1)}, u32[]{:S(2)}, u32[]{:S(2)}) %collective-permute-start.1) | collective-permute-done | bytes 3145760 | tf_op jit(solution)/shard_map/ppermute | solution.py:395
  65.9 7.2 %collective-permute-done.4.refs_2_ = bf16[64,3072]{1,0:T(8,128)(2,1)S(1)} collective-permute-done((bf16[64,3072]{1,0:T(8,128)(2,1)}, bf16[64,3072]{1,0:T(8,128)(2,1)S(1)}, u32[]{:S(2)}, u32[]{:S(2)}) %collective-permute-start.4) | collective-permute-done | bytes 393248 | tf_op jit(solution)/shard_map/ppermute | solution.py:386
  73.0 6.4 %collective-permute-done.5.refs_3_ = bf16[64,3072]{1,0:T(8,128)(2,1)S(1)} collective-permute-done((bf16[64,3072]{1,0:T(8,128)(2,1)}, bf16[64,3072]{1,0:T(8,128)(2,1)S(1)}, u32[]{:S(2)}, u32[]{:S(2)}) %collective-permute-start.5) | collective-permute-done | bytes 393248 | tf_op jit(solution)/shard_map/ppermute | solution.py:386
  83.5 4.1 %collective-permute-start.6 = (bf16[64,3072]{1,0:T(8,128)(2,1)S(1)}, bf16[64,3072]{1,0:T(8,128)(2,1)S(1)}, u32[]{:S(2)}, u32[]{:S(2)}) collective-permute-start(bf16[64,3072]{1,0:T(8,128)(2,1)S(1)} %copy-done.8), channel_id=1, source_target_pairs={{0,8},{8,0},{1,9},{9,1},{2,10},{10,2},{3,11},{11,3},{4,12},{12,4},... | collective-permute-start | bytes 1179656 | tf_op jit(solution)/shard_map/ppermute | solution.py:386
  87.7 6.8 %project.2 = (f32[256,1536]{1,0:T(8,128)}, bf16[256,1536]{1,0:T(8,128)(2,1)}) custom-call(bf16[1,256,1536]{2,1,0:T(8,128)(2,1)} %get-tuple-element.76.mine_ref, bf16[1,256,1536]{2,1,0:T(8,128)(2,1)} %bitcast.44, bf16[1536,1536]{1,0:T(8,128)(2,1)} %all-gather.3.cloned.1.call-done.piece_ref, bf16[64,3072]{1,0:T(8,128)(2,1)} %copy-done.25), custom_call_target="tpu_custom_call" | custom-call | flops 2415919104 | bytes 7077888 | tf_op jit(solution)/shard_map/project/pallas_call | solution.py:45
  94.5 4.1 %collective-permute-start.9 = (bf16[256,1536]{1,0:T(8,128)(2,1)}, bf16[256,1536]{1,0:T(8,128)(2,1)S(1)}, u32[]{:S(2)}, u32[]{:S(2)}) collective-permute-start(bf16[256,1536]{1,0:T(8,128)(2,1)} %get-tuple-element.45), channel_id=1, source_target_pairs={{0,1},{1,0},{2,3},{3,2},{4,5},{5,4},{6,7},{7,6},{8,9},{9,8},{10,11... | collective-permute-start | bytes 2359304 | tf_op jit(solution)/shard_map/ppermute | solution.py:386
  104.5 17.6 %collective-permute-done.10.rest_3_ = bf16[64,3072]{1,0:T(8,128)(2,1)S(1)} collective-permute-done((bf16[64,3072]{1,0:T(8,128)(2,1)}, bf16[64,3072]{1,0:T(8,128)(2,1)S(1)}, u32[]{:S(2)}, u32[]{:S(2)}) %collective-permute-start.10) | collective-permute-done | bytes 393248 | tf_op jit(solution)/shard_map/ppermute | solution.py:386
  127.2 17.5 %attention.2 = (bf16[256,3072]{1,0:T(8,128)(2,1)}, bf16[256,3072]{1,0:T(8,128)(2,1)}, bf16[2,256,1536]{2,1,0:T(8,128)(2,1)}, bf16[2,256,1536]{2,1,0:T(8,128)(2,1...) custom-call(s32[9]{0:T(128)} %stack.58.info, bf16[256,3072]{1,0:T(8,128)(2,1)} %bitcast.40, ...), custom_call_target="tpu_custom_call" | custom-call | flops 4831838208 | bytes 16515072 | tf_op jit(solution)/shard_map/attention/pallas_call | solution.py:162
  145.1 6.8 %project.3 = (f32[256,1536]{1,0:T(8,128)}, bf16[256,1536]{1,0:T(8,128)(2,1)}) custom-call(bf16[1,256,1536]{2,1,0:T(8,128)(2,1)} %get-tuple-element.76.mine_ref, bf16[1,256,1536]{2,1,0:T(8,128)(2,1)} %bitcast.45, bf16[1536,1536]{1,0:T(8,128)(2,1)} %all-gather.5.cloned.1.call-done.piece_ref, bf16[64,3072]{1,0:T(8,128)(2,1)} %pick.3.rest_0_, ...), custom_call_target="tpu_custom_call" | custom-call | flops 2415919104 | bytes 7077888 | tf_op jit(solution)/shard_map/project/pallas_call | solution.py:45
  158.6 17.6 %attention.3 = (bf16[256,3072]{1,0:T(8,128)(2,1)}, bf16[256,3072]{1,0:T(8,128)(2,1)}, bf16[2,256,1536]{2,1,0:T(8,128)(2,1)}, bf16[2,256,1536]{2,1,0:T(8,128)(2,1...) custom-call(s32[9]{0:T(128)} %stack.58.info, ...), custom_call_target="tpu_custom_call", output_to_operand_aliasing={{0}: (16, {}), {1}: (17, {})} | custom-call | flops 4831838208 | bytes 16515072 | tf_op jit(solution)/shard_map/attention/pallas_call | solution.py:162
  178.3 3.6 %collective-permute-start.28 = (bf16[2,256,1536]{2,1,0:T(8,128)(2,1)}, bf16[2,256,1536]{2,1,0:T(8,128)(2,1)S(1)}, u32[]{:S(2)}, u32[]{:S(2)}) collective-permute-start(bf16[2,256,1536]{2,1,0:T(8,128)(2,1)} %get-tuple-element.67), channel_id=1, source_target_pairs={{1,2},{3,4},{5,6},{7,8},{9,10},{11,12},{13,14},{2,1},{4,3},{6,5},{... | collective-permute-start | bytes 4718600 | tf_op jit(solution)/shard_map/ppermute | solution.py:395
  182.5 22.1 %collective-permute-done.19.rest_3_.refs_2_ = bf16[64,1536]{1,0:T(8,128)(2,1)S(1)} collective-permute-done((bf16[64,1536]{1,0:T(8,128)(2,1)S(1)}, bf16[64,1536]{1,0:T(8,128)(2,1)S(1)}, u32[]{:S(2)}, u32[]{:S(2)}) %collective-permute-start.19) | collective-permute-done | bytes 196640 | tf_op jit(solution)/shard_map/ppermute | solution.py:386
  204.6 6.3 %collective-permute-done.20.rest_4_.refs_3_ = bf16[64,1536]{1,0:T(8,128)(2,1)S(1)} collective-permute-done((bf16[64,1536]{1,0:T(8,128)(2,1)S(1)}, bf16[64,1536]{1,0:T(8,128)(2,1)S(1)}, u32[]{:S(2)}, u32[]{:S(2)}) %collective-permute-start.20) | collective-permute-done | bytes 196640 | tf_op jit(solution)/shard_map/ppermute | solution.py:386
  217.6 4.6 %collective-permute-start.25 = (bf16[64,1536]{1,0:T(8,128)(2,1)}, bf16[64,1536]{1,0:T(8,128)(2,1)S(1)}, u32[]{:S(2)}, u32[]{:S(2)}) collective-permute-start(bf16[64,1536]{1,0:T(8,128)(2,1)} %get-tuple-element.64), channel_id=1, source_target_pairs={{0,4},{2,6},{4,0},{6,2},{1,5},{3,7},{5,1},{7,3},{8,12},{10,14},{12... | collective-permute-start | bytes 589832 | tf_op jit(solution)/shard_map/ppermute | solution.py:386
  222.2 4.0 %collective-permute-done.24.refs_5_ = bf16[64,1536]{1,0:T(8,128)(2,1)S(1)} collective-permute-done((bf16[64,1536]{1,0:T(8,128)(2,1)}, bf16[64,1536]{1,0:T(8,128)(2,1)S(1)}, u32[]{:S(2)}, u32[]{:S(2)}) %collective-permute-start.24) | collective-permute-done | bytes 196640 | tf_op jit(solution)/shard_map/ppermute | solution.py:386
  226.2 5.1 %collective-permute-done.25.refs_6_ = bf16[64,1536]{1,0:T(8,128)(2,1)S(1)} collective-permute-done((bf16[64,1536]{1,0:T(8,128)(2,1)}, bf16[64,1536]{1,0:T(8,128)(2,1)S(1)}, u32[]{:S(2)}, u32[]{:S(2)}) %collective-permute-start.25) | collective-permute-done | bytes 196640 | tf_op jit(solution)/shard_map/ppermute | solution.py:386
  237.7 9.0 %collective-permute-done.29.b_ref = bf16[64,3072]{1,0:T(8,128)(2,1)S(1)} collective-permute-done((bf16[64,3072]{1,0:T(8,128)(2,1)}, bf16[64,3072]{1,0:T(8,128)(2,1)S(1)}, u32[]{:S(2)}, u32[]{:S(2)}) %collective-permute-start.29) | collective-permute-done | bytes 393248 | tf_op jit(solution)/shard_map/ppermute | solution.py:386
  249.3 3.9 %collective-permute-start.32 = (bf16[64,3072]{1,0:T(8,128)(2,1)}, bf16[64,3072]{1,0:T(8,128)(2,1)S(1)}, u32[]{:S(2)}, u32[]{:S(2)}) collective-permute-start(bf16[64,3072]{1,0:T(8,128)(2,1)} %add.45.rest_2_.refs_0_), channel_id=1, source_target_pairs={{0,2},{2,4},{4,6},{6,0},{1,3},{3,5},{5,7},{7,1},{8,10},{10,12},{12... | collective-permute-start | bytes 1179656 | tf_op jit(solution)/shard_map/ppermute | solution.py:386
  253.2 5.0 %combine.2 = (bf16[256,3072]{1,0:T(8,128)(2,1)}, bf16[256,3072]{1,0:T(8,128)(2,1)}) custom-call(s32[9]{0:T(128)} %stack.58.info, bf16[2,256,1536]{2,1,0:T(8,128)(2,1)} %get-tuple-element.69.own_ref, bf16[2,256,1536]{2,1,0:T(8,128)(2,1)} %collective-permute-done.22.rest_0_.rin_ref, bf16[2,256,1536]{2,1,0:T(8,128)(2,1)} %collective-permute-done.23.rest_1_.rout_ref, ...), custom_call_target="tpu_custom_call" | custom-call | flops 1572864 | bytes 6291456 | tf_op jit(solution)/shard_map/combine/pallas_call | solution.py:191
  260.2 4.9 %combine.3 = (bf16[256,3072]{1,0:T(8,128)(2,1)}, bf16[256,3072]{1,0:T(8,128)(2,1)}) custom-call(s32[9]{0:T(128)} %stack.58.info, bf16[2,256,1536]{2,1,0:T(8,128)(2,1)} %get-tuple-element.68.own_ref, bf16[2,256,1536]{2,1,0:T(8,128)(2,1)} %copy-done.3, bf16[2,256,1536]{2,1,0:T(8,128)(2,1)} %copy-done.4, ...), custom_call_target="tpu_custom_call", output_to_operand_aliasing={{0}: (4, {}), {1}: (5, {})} | custom-call | flops 1572864 | bytes 6291456 | tf_op jit(solution)/shard_map/combine/pallas_call | solution.py:191
  266.0 4.5 %collective-permute-done.32.refs_3_ = bf16[64,3072]{1,0:T(8,128)(2,1)S(1)} collective-permute-done((bf16[64,3072]{1,0:T(8,128)(2,1)}, bf16[64,3072]{1,0:T(8,128)(2,1)S(1)}, u32[]{:S(2)}, u32[]{:S(2)}) %collective-permute-start.32) | collective-permute-done | bytes 393248 | tf_op jit(solution)/shard_map/ppermute | solution.py:386
  273.6 6.7 %finish.1 = (bf16[256,3072]{1,0:T(8,128)(2,1)}, bf16[256,3072]{1,0:T(8,128)(2,1)}) custom-call(s32[9]{0:T(128)} %stack.58.info, bf16[64,3072]{1,0:T(8,128)(2,1)} %add.45.rest_2_.refs_0_, bf16[64,3072]{1,0:T(8,128)(2,1)} %copy-done.19, bf16[64,3072]{1,0:T(8,128)(2,1)} %hold.5.refs_2_, ...), custom_call_target="tpu_custom_call", output_to_operand_aliasing={{0}: (9, {}), {1}: (10, {})} | custom-call | flops 1572864 | bytes 9437184 | tf_op jit(solution)/shard_map/finish/pallas_call | solution.py:235
  (160 shorter events, 68.3 us)
Async XLA Ops:
  7.2 80.5 %all-gather.3.cloned.1.call-start = ((), (), s32[]{:S(2)}) async-start(), calls=%async_computation | async-start | bytes 5898240 | tf_op jit(solution)/shard_map/all_gather | solution.py:414
  10.0 135.2 %all-gather.5.cloned.1.call-start = ((), (), s32[]{:S(2)}) async-start(), calls=%async_computation.1 | async-start | bytes 5898240 | tf_op jit(solution)/shard_map/all_gather | solution.py:426
  14.1 14.4 %collective-permute-start = (bf16[2,256,3072]{2,1,0:T(8,128)(2,1)}, bf16[2,256,3072]{2,1,0:T(8,128)(2,1)}, u32[]{:S(2)}, u32[]{:S(2)}) collective-permute-start(bf16[2,256,3072]{2,1,0:T(8,128)(2,1)} %constant_dynamic-update-slice_fusion), channel_id=1, source_target_pairs={{0,1},{1,0},{2,3},{3,2},{4,5},{5,4},{6,7},{7,6},{8,9},{9,8},{10,11... | collective-permute-start | bytes 9437192 | tf_op jit(solution)/shard_map/ppermute | solution.py:386
  15.5 47.6 %collective-permute-start.1 = (bf16[2,256,3072]{2,1,0:T(8,128)(2,1)}, bf16[2,256,3072]{2,1,0:T(8,128)(2,1)}, u32[]{:S(2)}, u32[]{:S(2)}) collective-permute-start(bf16[2,256,3072]{2,1,0:T(8,128)(2,1)} %constant_dynamic-update-slice_fusion), channel_id=1, source_target_pairs={{1,2},{3,4},{5,6},{7,8},{9,10},{11,12},{13,14},{2,1},{4,3},{6,5},{... | collective-permute-start | bytes 9437192 | tf_op jit(solution)/shard_map/ppermute | solution.py:395
  21.5 60.9 %collective-permute-start.15 = (bf16[384,1536]{1,0:T(8,128)(2,1)S(1)}, bf16[384,1536]{1,0:T(8,128)(2,1)S(1)}, u32[]{:S(2)}, u32[]{:S(2)}) collective-permute-start(bf16[384,1536]{1,0:T(8,128)(2,1)S(1)} %copy-done.5), channel_id=1, source_target_pairs={{0,64},{64,0},{1,65},{65,1},{2,66},{66,2},{3,67},{67,3},{4,68},{68... | collective-permute-start | bytes 3538952 | tf_op jit(solution)/shard_map/ppermute | solution.py:386
  33.9 31.9 %collective-permute-start.3 = (bf16[64,3072]{1,0:T(8,128)(2,1)}, bf16[64,3072]{1,0:T(8,128)(2,1)S(1)}, u32[]{:S(2)}, u32[]{:S(2)}) collective-permute-start(bf16[64,3072]{1,0:T(8,128)(2,1)} %get-tuple-element.41), channel_id=1, source_target_pairs={{0,2},{2,4},{4,6},{6,0},{1,3},{3,5},{5,7},{7,1},{8,10},{10,12},{12... | collective-permute-start | bytes 1179656 | tf_op jit(solution)/shard_map/ppermute | solution.py:386
  35.3 37.8 %collective-permute-start.4 = (bf16[64,3072]{1,0:T(8,128)(2,1)}, bf16[64,3072]{1,0:T(8,128)(2,1)S(1)}, u32[]{:S(2)}, u32[]{:S(2)}) collective-permute-start(bf16[64,3072]{1,0:T(8,128)(2,1)} %get-tuple-element.42), channel_id=1, source_target_pairs={{0,4},{2,6},{4,0},{6,2},{1,5},{3,7},{5,1},{7,3},{8,12},{10,14},{12... | collective-permute-start | bytes 1179656 | tf_op jit(solution)/shard_map/ppermute | solution.py:386
  38.1 41.3 %collective-permute-start.5 = (bf16[64,3072]{1,0:T(8,128)(2,1)}, bf16[64,3072]{1,0:T(8,128)(2,1)S(1)}, u32[]{:S(2)}, u32[]{:S(2)}) collective-permute-start(bf16[64,3072]{1,0:T(8,128)(2,1)} %get-tuple-element.43), channel_id=1, source_target_pairs={{0,6},{2,0},{4,2},{6,4},{1,7},{3,1},{5,3},{7,5},{8,14},{10,8},{12,... | collective-permute-start | bytes 1179656 | tf_op jit(solution)/shard_map/ppermute | solution.py:386
  83.5 15.0 %collective-permute-start.6 = (bf16[64,3072]{1,0:T(8,128)(2,1)S(1)}, bf16[64,3072]{1,0:T(8,128)(2,1)S(1)}, u32[]{:S(2)}, u32[]{:S(2)}) collective-permute-start(bf16[64,3072]{1,0:T(8,128)(2,1)S(1)} %copy-done.8), channel_id=1, source_target_pairs={{0,8},{8,0},{1,9},{9,1},{2,10},{10,2},{3,11},{11,3},{4,12},{12,4},... | collective-permute-start | bytes 1179656 | tf_op jit(solution)/shard_map/ppermute | solution.py:386
  94.5 28.3 %collective-permute-start.9 = (bf16[256,1536]{1,0:T(8,128)(2,1)}, bf16[256,1536]{1,0:T(8,128)(2,1)S(1)}, u32[]{:S(2)}, u32[]{:S(2)}) collective-permute-start(bf16[256,1536]{1,0:T(8,128)(2,1)} %get-tuple-element.45), channel_id=1, source_target_pairs={{0,1},{1,0},{2,3},{3,2},{4,5},{5,4},{6,7},{7,6},{8,9},{9,8},{10,11... | collective-permute-start | bytes 2359304 | tf_op jit(solution)/shard_map/ppermute | solution.py:386
  101.3 20.8 %collective-permute-start.10 = (bf16[64,3072]{1,0:T(8,128)(2,1)}, bf16[64,3072]{1,0:T(8,128)(2,1)S(1)}, u32[]{:S(2)}, u32[]{:S(2)}) collective-permute-start(bf16[64,3072]{1,0:T(8,128)(2,1)} %pick.3.rest_0_), channel_id=1, source_target_pairs={{0,2},{2,4},{4,6},{6,0},{1,3},{3,5},{5,7},{7,1},{8,10},{10,12},{12... | collective-permute-start | bytes 1179656 | tf_op jit(solution)/shard_map/ppermute | solution.py:386
  101.3 21.4 %collective-permute-start.7 = (bf16[64,3072]{1,0:T(8,128)(2,1)}, bf16[64,3072]{1,0:T(8,128)(2,1)S(1)}, u32[]{:S(2)}, u32[]{:S(2)}) collective-permute-start(bf16[64,3072]{1,0:T(8,128)(2,1)} %pick.3.rest_0_), channel_id=1, source_target_pairs={{0,6},{2,0},{4,2},{6,4},{1,7},{3,1},{5,3},{7,5},{8,14},{10,8},{12,... | collective-permute-start | bytes 1179656 | tf_op jit(solution)/shard_map/ppermute | solution.py:386
  104.0 18.8 %collective-permute-start.8 = (bf16[64,3072]{1,0:T(8,128)(2,1)}, bf16[64,3072]{1,0:T(8,128)(2,1)S(1)}, u32[]{:S(2)}, u32[]{:S(2)}) collective-permute-start(bf16[64,3072]{1,0:T(8,128)(2,1)} %pick.3.rest_0_), channel_id=1, source_target_pairs={{0,4},{2,6},{4,0},{6,2},{1,5},{3,7},{5,1},{7,3},{8,12},{10,14},{12... | collective-permute-start | bytes 1179656 | tf_op jit(solution)/shard_map/ppermute | solution.py:386
  104.0 20.9 %collective-permute-start.11 = (bf16[64,3072]{1,0:T(8,128)(2,1)}, bf16[64,3072]{1,0:T(8,128)(2,1)S(1)}, u32[]{:S(2)}, u32[]{:S(2)}) collective-permute-start(bf16[64,3072]{1,0:T(8,128)(2,1)} %pick.3.rest_0_), channel_id=1, source_target_pairs={{0,1},{1,0},{2,3},{3,2},{4,5},{5,4},{6,7},{7,6},{8,9},{9,8},{10,11... | collective-permute-start | bytes 1179656 | tf_op jit(solution)/shard_map/ppermute | solution.py:386
  152.1 61.1 %collective-permute-start.22 = (bf16[2,256,1536]{2,1,0:T(8,128)(2,1)}, bf16[2,256,1536]{2,1,0:T(8,128)(2,1)}, u32[]{:S(2)}, u32[]{:S(2)}) collective-permute-start(bf16[2,256,1536]{2,1,0:T(8,128)(2,1)} %get-tuple-element.60), channel_id=1, source_target_pairs={{0,1},{1,0},{2,3},{3,2},{4,5},{5,4},{6,7},{7,6},{8,9},{9,8},{10,11... | collective-permute-start | bytes 4718600 | tf_op jit(solution)/shard_map/ppermute | solution.py:386
  152.5 60.8 %collective-permute-start.23 = (bf16[2,256,1536]{2,1,0:T(8,128)(2,1)}, bf16[2,256,1536]{2,1,0:T(8,128)(2,1)}, u32[]{:S(2)}, u32[]{:S(2)}) collective-permute-start(bf16[2,256,1536]{2,1,0:T(8,128)(2,1)} %get-tuple-element.61), channel_id=1, source_target_pairs={{1,2},{3,4},{5,6},{7,8},{9,10},{11,12},{13,14},{2,1},{4,3},{6,5},{... | collective-permute-start | bytes 4718600 | tf_op jit(solution)/shard_map/ppermute | solution.py:395
  157.5 24.4 %collective-permute-start.18 = (bf16[64,1536]{1,0:T(8,128)(2,1)}, bf16[64,1536]{1,0:T(8,128)(2,1)S(1)}, u32[]{:S(2)}, u32[]{:S(2)}) collective-permute-start(bf16[64,1536]{1,0:T(8,128)(2,1)} %get-tuple-element.53.rest_13_), channel_id=1, source_target_pairs={{0,2},{2,4},{4,6},{6,0},{1,3},{3,5},{5,7},{7,1},{8,10},{10,12},{12... | collective-permute-start | bytes 589832 | tf_op jit(solution)/shard_map/ppermute | solution.py:386
  176.2 55.1 %collective-permute-start.27 = (bf16[2,256,1536]{2,1,0:T(8,128)(2,1)}, bf16[2,256,1536]{2,1,0:T(8,128)(2,1)S(1)}, u32[]{:S(2)}, u32[]{:S(2)}) collective-permute-start(bf16[2,256,1536]{2,1,0:T(8,128)(2,1)} %get-tuple-element.66), channel_id=1, source_target_pairs={{0,1},{1,0},{2,3},{3,2},{4,5},{5,4},{6,7},{7,6},{8,9},{9,8},{10,11... | collective-permute-start | bytes 4718600 | tf_op jit(solution)/shard_map/ppermute | solution.py:386
  178.3 53.0 %collective-permute-start.28 = (bf16[2,256,1536]{2,1,0:T(8,128)(2,1)}, bf16[2,256,1536]{2,1,0:T(8,128)(2,1)S(1)}, u32[]{:S(2)}, u32[]{:S(2)}) collective-permute-start(bf16[2,256,1536]{2,1,0:T(8,128)(2,1)} %get-tuple-element.67), channel_id=1, source_target_pairs={{1,2},{3,4},{5,6},{7,8},{9,10},{11,12},{13,14},{2,1},{4,3},{6,5},{... | collective-permute-start | bytes 4718600 | tf_op jit(solution)/shard_map/ppermute | solution.py:395
  182.0 22.7 %collective-permute-start.19 = (bf16[64,1536]{1,0:T(8,128)(2,1)S(1)}, bf16[64,1536]{1,0:T(8,128)(2,1)S(1)}, u32[]{:S(2)}, u32[]{:S(2)}) collective-permute-start(bf16[64,1536]{1,0:T(8,128)(2,1)S(1)} %copy-done.35), channel_id=1, source_target_pairs={{0,4},{2,6},{4,0},{6,2},{1,5},{3,7},{5,1},{7,3},{8,12},{10,14},{12... | collective-permute-start | bytes 589832 | tf_op jit(solution)/shard_map/ppermute | solution.py:386
  249.3 15.7 %collective-permute-start.31 = (bf16[64,3072]{1,0:T(8,128)(2,1)}, bf16[64,3072]{1,0:T(8,128)(2,1)S(1)}, u32[]{:S(2)}, u32[]{:S(2)}) collective-permute-start(bf16[64,3072]{1,0:T(8,128)(2,1)} %add.45.rest_2_.refs_0_), channel_id=1, source_target_pairs={{0,4},{2,6},{4,0},{6,2},{1,5},{3,7},{5,1},{7,3},{8,12},{10,14},{12... | collective-permute-start | bytes 1179656 | tf_op jit(solution)/shard_map/ppermute | solution.py:386
  249.3 21.2 %collective-permute-start.32 = (bf16[64,3072]{1,0:T(8,128)(2,1)}, bf16[64,3072]{1,0:T(8,128)(2,1)S(1)}, u32[]{:S(2)}, u32[]{:S(2)}) collective-permute-start(bf16[64,3072]{1,0:T(8,128)(2,1)} %add.45.rest_2_.refs_0_), channel_id=1, source_target_pairs={{0,2},{2,4},{4,6},{6,0},{1,3},{3,5},{5,7},{7,1},{8,10},{10,12},{12... | collective-permute-start | bytes 1179656 | tf_op jit(solution)/shard_map/ppermute | solution.py:386
  253.2 17.8 %collective-permute-start.30 = (bf16[64,3072]{1,0:T(8,128)(2,1)}, bf16[64,3072]{1,0:T(8,128)(2,1)S(1)}, u32[]{:S(2)}, u32[]{:S(2)}) collective-permute-start(bf16[64,3072]{1,0:T(8,128)(2,1)} %add.45.rest_2_.refs_0_), channel_id=1, source_target_pairs={{0,6},{2,0},{4,2},{6,4},{1,7},{3,1},{5,3},{7,5},{8,14},{10,8},{12,... | collective-permute-start | bytes 1179656 | tf_op jit(solution)/shard_map/ppermute | solution.py:386
  258.3 13.7 %collective-permute-start.33 = (bf16[64,3072]{1,0:T(8,128)(2,1)S(1)}, bf16[64,3072]{1,0:T(8,128)(2,1)S(1)}, u32[]{:S(2)}, u32[]{:S(2)}) collective-permute-start(bf16[64,3072]{1,0:T(8,128)(2,1)S(1)} %copy-done.7), channel_id=1, source_target_pairs={{0,1},{1,0},{2,3},{3,2},{4,5},{5,4},{6,7},{7,6},{8,9},{9,8},{10,11... | collective-permute-start | bytes 1179656 | tf_op jit(solution)/shard_map/ppermute | solution.py:386
  (55 other events, 296.6 us)
Sparse Core Ops, SparseCore 0:
  10.3 56.0 all-gather.2
  83.5 57.1 all-gather.4
